TPU v7x, 32 devices: a whole 2x2x4 slice. The times are simulated.
32 devices in a mesh: az: 16 (over z, x, core), rad: 2 (over y).
Axes of the slice: x: 2, y: 2, z: 4, core: 2. Of those that a mesh axis runs over, the one named last changes fastest.
Arguments:
- density: float32 [1024, 64, 512], P('az', 'rad'), may hold values from -10 to 10
Outputs:
- potential: float32 [1024, 64, 512], P('az', 'rad')
All inputs are finite; a program needn't handle non-finite values.
Results may differ from a plain program's by a relative error of at most 0.000075.
Values sent between devices are 32-bit elements; how exact they have to be, the bound alone decides.
No kernel may reach another device: no remote copies, remote signals or barrier semaphores. Data moves between devices by JAX's collectives and lax.ppermute only.
A program may use at most 128 MiB of HBM per device.

v0:
```python
import math

import jax
import jax.numpy as jnp
from jax import lax
from jax.sharding import PartitionSpec as P

POST = 2
COARSE = 6


OMEGA = 0.8


def with_halo(cells, sides, width):
    for axis, dim in sides:
        count = lax.axis_size(axis)
        ends = count - 1
        head = lax.slice_in_dim(cells, 0, width, axis=dim)
        tail = lax.slice_in_dim(cells, cells.shape[dim] - width, cells.shape[dim], axis=dim)
        cells = jnp.concatenate(
            [
                lax.ppermute(tail, axis, [(i, (i + 1) % count) for i in range(ends)]),
                cells,
                lax.ppermute(head, axis, [((i + 1) % count, i) for i in range(ends)]),
            ],
            axis=dim,
        )
    return cells


def level_coefficients(first_row, row_count, spacing, mode_numbers):
    row_number = (jnp.arange(row_count, dtype=jnp.int32) + first_row).astype(jnp.float32)
    radius = spacing * (row_number + 0.5)
    outward = (row_number + 1.0) / (spacing * radius)
    inward = row_number / (spacing * radius)
    vertical = 1.0 / (spacing * spacing)
    diagonal = (outward + inward + 2.0 * vertical)[None, :] + (
        mode_numbers[:, None] / radius[None, :]
    ) ** 2
    return (diagonal[:, :, None], outward[None, :, None], inward[None, :, None], vertical)


def apply_op(iterate, padded, coefficients):
    diagonal, outward, inward, vertical = coefficients
    return (
        diagonal * iterate
        - outward * padded[:, 2:, 1:-1]
        - inward * padded[:, :-2, 1:-1]
        - vertical * (padded[:, 1:-1, 2:] + padded[:, 1:-1, :-2])
    )


def relax(iterate, source, coefficients, pad_both):
    return (
        iterate
        + OMEGA * (source - apply_op(iterate, pad_both(iterate), coefficients)) / coefficients[0]
    )


def restrict(residual):
    k_count, r_count, z_count = residual.shape
    parts = residual.reshape(k_count, r_count // 2, 2, z_count // 2, 2)
    return 0.25 * (
        parts[:, :, 0, :, 0] + parts[:, :, 1, :, 0] + parts[:, :, 0, :, 1] + parts[:, :, 1, :, 1]
    )


def prolong(correction):
    return jnp.repeat(jnp.repeat(correction, 2, axis=1), 2, axis=2)


def pad_fine(field):
    rows = with_halo(field, (("rad", 1),), 1)
    return jnp.pad(rows, ((0, 0), (0, 0), (1, 1)))


def pad_coarse(field):
    rows = with_halo(field, (("rad", 1),), 1)
    return jnp.pad(rows, ((0, 0), (0, 0), (1, 1)))


def mode_values(mode_index, azimuths):
    return jnp.where(mode_index <= azimuths // 2, mode_index, mode_index - azimuths // 2).astype(
        jnp.float32
    )


def fine_cycle(source, fine_coef, pad_sweep, coarse_solve):
    iterate = OMEGA * source / fine_coef[0]
    iterate = relax(iterate, source, fine_coef, pad_sweep)
    residual = source - apply_op(iterate, pad_sweep(iterate), fine_coef)
    iterate = iterate + prolong(coarse_solve(restrict(residual)))
    for sweep_index in range(POST):
        iterate = relax(iterate, source, fine_coef, pad_sweep)
    return iterate


def body(density):
    local_phi, local_rows, vertical_cells = density.shape
    az_count = lax.axis_size("az")
    azimuths = local_phi * az_count
    cell_count = local_rows * vertical_cells // az_count
    numbers = jnp.arange(azimuths, dtype=jnp.int32)
    all_modes = jnp.where(numbers <= azimuths // 2, numbers, numbers - azimuths // 2)
    phase = all_modes[:, None] * numbers[None, :] % azimuths
    phase_angle = phase.astype(jnp.float32) * (2.0 * math.pi / azimuths)
    analysis_table = jnp.where(
        (numbers <= azimuths // 2)[:, None], jnp.cos(phase_angle), jnp.sin(phase_angle)
    )
    synth_weight = jnp.where(
        (numbers == 0) | (numbers == azimuths // 2), 1.0 / azimuths, 2.0 / azimuths
    )
    synthesis_table = analysis_table.T * synth_weight[None, :]

    def transform_with(table, columns):
        width = columns.shape[2]
        matrix = columns.reshape(azimuths, width)
        result = jnp.dot(
            table, matrix, precision=lax.Precision.HIGHEST, preferred_element_type=jnp.float32
        )
        return result.reshape(azimuths, 1, width)

    lines = density.reshape(local_phi, az_count, cell_count)
    spectral = transform_with(
        analysis_table, lax.all_to_all(lines, "az", split_axis=1, concat_axis=0, tiled=True)
    )
    coefficients = lax.all_to_all(spectral, "az", split_axis=0, concat_axis=1, tiled=True)
    source = -coefficients.reshape(local_phi, local_rows, vertical_cells)
    rad_index = lax.axis_index("rad")
    half_rows = local_rows // 2
    mode_index = lax.axis_index("az") * local_phi + jnp.arange(local_phi, dtype=jnp.int32)
    mode_numbers = mode_values(mode_index, azimuths)
    fine_coef = level_coefficients(rad_index * local_rows, local_rows, 1.0, mode_numbers)
    coarse_coef = level_coefficients(rad_index * half_rows, half_rows, 2.0, mode_numbers)

    def coarse_halo(coarse_source):
        correction = OMEGA * coarse_source / coarse_coef[0]
        for sweep_index in range(COARSE - 1):
            correction = relax(correction, coarse_source, coarse_coef, pad_coarse)
        return correction

    iterate = fine_cycle(source, fine_coef, pad_fine, coarse_halo)
    mode_lines = iterate.reshape(local_phi, az_count, cell_count)
    physical = transform_with(
        synthesis_table, lax.all_to_all(mode_lines, "az", split_axis=1, concat_axis=0, tiled=True)
    )
    field = lax.all_to_all(physical, "az", split_axis=0, concat_axis=1, tiled=True)
    return field.reshape(local_phi, local_rows, vertical_cells)


def solution(mesh):
    placed = (P("az", "rad", None),)
    return jax.shard_map(
        body, mesh=mesh, in_specs=placed, out_specs=P("az", "rad", None), check_vma=False
    )
```

profile of v0, /device:TPU:11, one launch (start us, length us, event | category | flops | bytes accessed | tf_op | source)
XLA Modules:
  0.0 689.4 jit_solution(17518113914636866704)
XLA Ops:
  0.0 5.2 reshape.204
  5.2 6.7 copy.29
  11.9 6.6 all-to-all-start
  18.4 92.4 %all-to-all-done = f32[64,16,1024]{2,0,1:T(8,128)} async-done(((f32[64,16,1024]{2,0,1:T(8,128)}), f32[64,16,1024]{2,0,1:T(8,128)}, u32[]{:S(2)}, u32[]{:S(2)}) %all-to-all-start) | async-done | bytes 4194336 | tf_op jit(solution)/shard_map/all_to_all | solution.py:126
  110.9 33.6 %fusion.65 = f32[1024,1,1024]{2,0,1:T(8,128)S(1)} fusion(f32[1024,1024]{1,0:T(8,128)} %bitcast.2, s32[1024]{0:T(1024)S(1)} %add_select_fusion.2, pred[1024]{0:T(1024)(128)(4,1)S(1)} %iota_compare_fusion.6), kind=kOutput, calls=%fused_computation.99 | convolution fusion | flops 12900630528 | bytes 8393728 | tf_op jit(solution)/shard_map/dot_general | solution.py:119
  144.5 6.3 copy.30
  150.8 4.9 all-to-all-start.1
  155.8 92.4 %all-to-all-done.1 = f32[1024,1,1024]{2,1,0:T(1,128)} async-done(((f32[1024,1,1024]{2,1,0:T(1,128)}), f32[1024,1,1024]{2,1,0:T(1,128)}, u32[]{:S(2)}, u32[]{:S(2)}) %all-to-all-start.1) | async-done | bytes 4194336 | tf_op jit(solution)/shard_map/all_to_all | solution.py:128
  248.2 5.8 neg.12
  254.0 4.4 copy.50
  258.4 5.0 neg.15
  263.4 2.7 multiply_divide_fusion
  266.1 2.0 copy-done.3
  269.7 4.0 collective-permute-start.1
  276.0 5.5 select_maximum_fusion.6
  281.6 5.1 fusion.35
  288.2 4.1 collective-permute-start.3
  294.2 3.8 select_maximum_fusion.4
  298.1 5.4 fusion.26
  303.5 7.0 %copy.32 = f32[64,32,512]{0,2,1:T(8,128)} copy(f32[64,32,512]{2,1,0:T(8,128)} %fusion.26) | data formatting | bytes 8388608 | tf_op jit(solution)/shard_map/sub | solution.py:92
  310.5 9.4 %broadcast_multiply_fusion = (f32[64,16,1,256,1]{0,4,3,2,1:T(1,128)S(1)}, f32[64,16,1,256,1]{0,4,3,2,1:T(1,128)S(1)}) fusion(f32[64,16,2,256,2]{0,4,3,2,1:T(2,128)} %bitcast.52), kind=kLoop, calls=%fused_computation.181 | loop fusion | flops 1048576 | bytes 6291456 | tf_op jit(solution)/shard_map/mul | solution.py:64
  319.9 2.3 broadcast_multiply_fusion.1
  323.8 4.0 collective-permute-start.5
  329.9 1.7 fusion.113
  333.0 4.0 collective-permute-start.7
  342.2 4.0 collective-permute-start.9
  348.4 1.9 fusion.93
  351.7 4.0 collective-permute-start.11
  360.9 4.0 collective-permute-start.13
  370.1 2.4 broadcast_in_dim.26
  372.5 4.4 broadcast_in_dim.27
  376.9 7.7 %copy.40 = f32[64,32,512]{2,1,0:T(8,128)} copy(f32[64,32,512]{0,1,2:T(8,128)} %bitcast.53) | data formatting | bytes 8388608 | tf_op jit(solution)/shard_map/reshape | solution.py:70
  384.6 4.5 add.309
  390.7 4.0 collective-permute-start.15
  396.6 4.1 select_maximum_fusion.2
  400.7 5.1 fusion.20
  407.3 4.0 collective-permute-start.17
  413.2 3.7 select_maximum_fusion
  416.9 6.0 fusion.11
  422.9 5.3 reshape.210
  428.2 6.6 copy.41
  434.8 15.0 %all-to-all-start.2 = ((f32[64,16,1024]{2,0,1:T(8,128)}), f32[64,16,1024]{2,0,1:T(8,128)}, u32[]{:S(2)}, u32[]{:S(2)}) async-start(f32[64,16,1024]{2,0,1:T(8,128)} %copy.41), calls=%async_computation.2 | async-start | bytes 8388608 | tf_op jit(solution)/shard_map/all_to_all | solution.py:146
  449.8 92.5 %all-to-all-done.2 = f32[64,16,1024]{2,0,1:T(8,128)} async-done(((f32[64,16,1024]{2,0,1:T(8,128)}), f32[64,16,1024]{2,0,1:T(8,128)}, u32[]{:S(2)}, u32[]{:S(2)}) %all-to-all-start.2) | async-done | bytes 4194336 | tf_op jit(solution)/shard_map/all_to_all | solution.py:146
  542.2 34.1 %fusion.62 = f32[1024,1,1024]{2,0,1:T(8,128)} fusion(f32[1024,1024]{1,0:T(8,128)} %bitcast.18, f32[1024]{0:T(1024)S(1)} %fusion.134, s32[1024]{0:T(1024)S(1)} %add_select_fusion.2, pred[1024]{0:T(1024)(128)(4,1)S(1)} %iota_compare_fusion.6), kind=kOutput, calls=%fused_computation.98 | convolution fusion | flops 12901679104 | bytes 8397824 | tf_op jit(solution)/shard_map/dot_general | solution.py:119
  576.4 6.5 copy.42
  582.9 96.9 %all_to_all.54 = f32[1024,1,1024]{2,1,0:T(1,128)S(1)} all-to-all(f32[1024,1,1024]{2,1,0:T(1,128)S(1)} %copy.42), channel_id=1, replica_groups=mesh['az'=16,'rad'=2] {'az'}, dimensions={0} | all-to-all | bytes 8388608 | tf_op jit(solution)/shard_map/all_to_all | solution.py:148
  679.8 4.4 copy.43
  684.3 4.9 reshape.213
  (65 shorter events, 38.4 us)
Async XLA Ops:
  11.9 99.0 %all-to-all-start = ((f32[64,16,1024]{2,0,1:T(8,128)}), f32[64,16,1024]{2,0,1:T(8,128)}, u32[]{:S(2)}, u32[]{:S(2)}) async-start(f32[64,16,1024]{2,0,1:T(8,128)} %copy.29), calls=%async_computation | async-start | bytes 8388608 | tf_op jit(solution)/shard_map/all_to_all | solution.py:126
  150.8 97.4 %all-to-all-start.1 = ((f32[1024,1,1024]{2,1,0:T(1,128)}), f32[1024,1,1024]{2,1,0:T(1,128)}, u32[]{:S(2)}, u32[]{:S(2)}) async-start(f32[1024,1,1024]{2,1,0:T(1,128)} %copy.30), calls=%async_computation.1 | async-start | bytes 8388608 | tf_op jit(solution)/shard_map/all_to_all | solution.py:128
  266.1 2.0 copy-start.3
  268.4 6.8 collective-permute-start
  269.7 6.4 collective-permute-start.1
  276.0 5.5 copy-start
  276.0 5.5 copy-start.4
  286.6 11.5 %copy-start.2 = (f32[64,32,512]{2,1,0:T(8,128)}, f32[64,32,512]{2,1,0:T(8,128)S(1)}, u32[]{:S(2)}) copy-start(f32[64,32,512]{2,1,0:T(8,128)S(1)} %fusion.35) | copy-start | bytes 12582916
  286.9 5.8 collective-permute-start.2
  288.2 6.0 collective-permute-start.3
  322.5 5.7 collective-permute-start.4
  323.8 5.9 collective-permute-start.5
  331.7 5.7 collective-permute-start.6
  333.0 5.9 collective-permute-start.7
  340.9 5.7 collective-permute-start.8
  342.2 5.9 collective-permute-start.9
  350.4 5.7 collective-permute-start.10
  351.7 5.9 collective-permute-start.11
  359.6 5.7 collective-permute-start.12
  360.9 5.9 collective-permute-start.13
  389.4 5.7 collective-permute-start.14
  390.7 5.9 collective-permute-start.15
  396.6 4.1 copy-start.1
  406.0 5.7 collective-permute-start.16
  407.3 5.9 collective-permute-start.17
  434.8 107.4 %all-to-all-start.2 = ((f32[64,16,1024]{2,0,1:T(8,128)}), f32[64,16,1024]{2,0,1:T(8,128)}, u32[]{:S(2)}, u32[]{:S(2)}) async-start(f32[64,16,1024]{2,0,1:T(8,128)} %copy.41), calls=%async_computation.2 | async-start | bytes 8388608 | tf_op jit(solution)/shard_map/all_to_all | solution.py:146
where the time goes:
time: 695 us; the launch traced here: 689 us
  waiting for transfers between devices  295 us (42%)
  blocking collectives  96.9 us (14%)
  local copies, waits for them, and re-layouts  81.2 us (12%)
  starting transfers between devices  74.2 us (11%)
  other arithmetic  73.7 us (11%)
  matrix products  67.7 us (10%)
    all_to_all x1, blocking collectives, body(): lax.all_to_all(physical, 'az', split_axis=0, concat_axis=1, tiled=True)  96.9 us
    all_to_all x1, waiting for transfers between devices, body(): lax.all_to_all(mode_lines, 'az', split_axis=1, concat_axis=0, tiled=True)  92.5 us
    all_to_all x1, waiting for transfers between devices, body(): lax.all_to_all(lines, 'az', split_axis=1, concat_axis=0, tiled=True)  92.4 us
    all_to_all x1, waiting for transfers between devices, body(): lax.all_to_all(spectral, 'az', split_axis=0, concat_axis=1, tiled=True)  92.4 us
    dot_general x2, matrix products, transform_with(): jnp.dot(table, matrix, precision=lax.Precision.HIGHEST, preferred_element...  67.7 us
    ppermute x9, starting transfers between devices, with_halo(): lax.ppermute(tail, axis, [(i, (i + 1) % count) for i in range(ends)])  36.1 us
    add x8, other arithmetic, relax(): iterate + OMEGA * (source - apply_op(iterate, pad_both(iterate), coeffici...  24.9 us
    concatenate x9, other arithmetic, with_halo(): jnp.concatenate([lax.ppermute(tail, axis, [(i, (i + 1) % count) for i in...  18.3 us
  transfers between devices with their start and end apart: 21, of which 21 were waited for; matrix products, arithmetic and copies ran while one was open for 0% of the time, Pallas kernels for 0%

commit v1 on v0

--- a/solution.py
+++ b/solution.py
@@ -2,14 +2,25 @@
 
 import jax
 import jax.numpy as jnp
+import numpy as np
 from jax import lax
+from jax.experimental import pallas as pl
+from jax.experimental.pallas import tpu as pltpu
 from jax.sharding import PartitionSpec as P
 
+PRE = 2
 POST = 2
 COARSE = 6
 
 
 OMEGA = 0.8
+
+LANES = 128
+TILE = 8
+DEEP = 2 * COARSE + 2
+NEAR = 3
+FAR = COARSE
+VMEM_LIMIT = 56 * 1024 * 1024
 
 
 def with_halo(cells, sides, width):
@@ -70,12 +81,7 @@
     return jnp.repeat(jnp.repeat(correction, 2, axis=1), 2, axis=2)
 
 
-def pad_fine(field):
-    rows = with_halo(field, (("rad", 1),), 1)
-    return jnp.pad(rows, ((0, 0), (0, 0), (1, 1)))
-
-
-def pad_coarse(field):
+def pad_level(field):
     rows = with_halo(field, (("rad", 1),), 1)
     return jnp.pad(rows, ((0, 0), (0, 0), (1, 1)))
 
@@ -88,7 +94,8 @@
 
 def fine_cycle(source, fine_coef, pad_sweep, coarse_solve):
     iterate = OMEGA * source / fine_coef[0]
-    iterate = relax(iterate, source, fine_coef, pad_sweep)
+    for sweep_index in range(PRE - 1):
+        iterate = relax(iterate, source, fine_coef, pad_sweep)
     residual = source - apply_op(iterate, pad_sweep(iterate), fine_coef)
     iterate = iterate + prolong(coarse_solve(restrict(residual)))
     for sweep_index in range(POST):
@@ -96,7 +103,7 @@
     return iterate
 
 
-def body(density):
+def general_body(density):
     local_phi, local_rows, vertical_cells = density.shape
     az_count = lax.axis_size("az")
     azimuths = local_phi * az_count
@@ -137,16 +144,569 @@
     def coarse_halo(coarse_source):
         correction = OMEGA * coarse_source / coarse_coef[0]
         for sweep_index in range(COARSE - 1):
-            correction = relax(correction, coarse_source, coarse_coef, pad_coarse)
+            correction = relax(correction, coarse_source, coarse_coef, pad_level)
         return correction
 
-    iterate = fine_cycle(source, fine_coef, pad_fine, coarse_halo)
+    iterate = fine_cycle(source, fine_coef, pad_level, coarse_halo)
     mode_lines = iterate.reshape(local_phi, az_count, cell_count)
     physical = transform_with(
         synthesis_table, lax.all_to_all(mode_lines, "az", split_axis=1, concat_axis=0, tiled=True)
     )
     field = lax.all_to_all(physical, "az", split_axis=0, concat_axis=1, tiled=True)
     return field.reshape(local_phi, local_rows, vertical_cells)
+
+
+def mode_tables(azimuths):
+    half = azimuths // 2
+    even = np.concatenate([np.arange(0, half + 1, 2), np.arange(2, half, 2)])
+    odd = np.concatenate([np.arange(1, half, 2), np.arange(1, half, 2)])
+    even_cos = np.arange(half) <= half // 2
+    odd_cos = np.arange(half) < half // 2
+    modes = np.concatenate([even, odd])
+    is_cos = np.concatenate([even_cos, odd_cos])
+    angle = 2.0 * np.pi / azimuths * (np.arange(half)[:, None] * modes[None, :] % azimuths)
+    values = np.where(is_cos[None, :], np.cos(angle), np.sin(angle))
+    weight = np.where((modes == 0) | (modes == half), 1.0, 2.0) / azimuths
+    return modes.astype(np.float32), -values, values * weight[None, :]
+
+
+def high_low(values):
+    values = values.astype(np.float32)
+    high = values.astype(jnp.bfloat16)
+    low = (values - high.astype(np.float32)).astype(jnp.bfloat16)
+    return jnp.asarray(high), jnp.asarray(low)
+
+
+def split_value(value):
+    high = value.astype(jnp.bfloat16)
+    return high, (value - high.astype(jnp.float32)).astype(jnp.bfloat16)
+
+
+def swap_chunks(parts, chunk):
+    count = len(parts)
+    parts = list(parts)
+    lane = lax.broadcasted_iota(jnp.int32, parts[0].shape, parts[0].ndim - 1) // chunk
+    span = count // 2
+    while span:
+        keep = (lane & span) == 0
+        for i in range(count):
+            if i & span:
+                continue
+            a, b = parts[i], parts[i + span]
+            axis = a.ndim - 1
+            parts[i] = jnp.where(keep, a, pltpu.roll(b, span * chunk, axis))
+            parts[i + span] = jnp.where(keep, pltpu.roll(a, LANES - span * chunk, axis), b)
+        span //= 2
+    return parts
+
+
+def tile_row(pos_ref, row):
+    return jnp.where(pos_ref[0] == 0, TILE - 1 - row, row)
+
+
+def pack_kernel(block, pos_ref, x_ref, o_ref):
+    rows = LANES // block
+    local_phi = x_ref.shape[0]
+    flat = x_ref.reshape(local_phi * TILE, LANES)
+    for group in range(TILE // rows):
+        parts = [
+            flat[pl.ds(tile_row(pos_ref, group * rows + i), local_phi, stride=TILE), :]
+            for i in range(rows)
+        ]
+        for q, part in enumerate(swap_chunks(parts, block)):
+            o_ref[q, group] = part
+
+
+def unpack_kernel(block, pos_ref, x_ref, o_ref):
+    rows = LANES // block
+    local_phi = o_ref.shape[0]
+    flat = o_ref.reshape(local_phi * TILE, LANES)
+    for group in range(TILE // rows):
+        parts = [x_ref[q, group] for q in range(rows)]
+        for i, part in enumerate(swap_chunks(parts, block)):
+            flat[pl.ds(tile_row(pos_ref, group * rows + i), local_phi, stride=TILE), :] = part
+
+
+def analysis_kernel(x_ref, high_ref, low_ref, o_ref, edge_ref=None):
+    sources, groups, width, lanes = x_ref.shape
+    half = sources // 2 * width
+    rows, cells = o_ref.shape[0], o_ref.shape[1]
+    for parity in range(2):
+        turned = []
+        for group in range(groups):
+            near, far = x_ref[: sources // 2, group], x_ref[sources // 2 :, group]
+            folded = near + far if parity == 0 else near - far
+            turned.append(folded.reshape(half, lanes).T)
+        high, low = split_value(jnp.concatenate(turned, axis=0))
+        columns = slice(parity * half, (parity + 1) * half)
+        t_high, t_low = high_ref[:, columns], low_ref[:, columns]
+        result = (
+            jnp.dot(high, t_high, preferred_element_type=jnp.float32)
+            + jnp.dot(high, t_low, preferred_element_type=jnp.float32)
+            + jnp.dot(low, t_high, preferred_element_type=jnp.float32)
+        )
+        for part in range(half // LANES):
+            piece = result[:, part * LANES : (part + 1) * LANES]
+            o_ref[:, :, parity * (half // LANES) + part, :] = piece.reshape(rows, cells, LANES)
+    if edge_ref is not None:
+        for step in range(-(-DEEP // rows)):
+
+            @pl.when(pl.program_id(0) == step)
+            def _():
+                for row in range(rows):
+                    if step * rows + row < DEEP:
+                        edge_ref[DEEP - 1 - step * rows - row] = o_ref[row]
+
+
+def synthesis_kernel(u_ref, high_ref, low_ref, o_ref):
+    rows, cells = u_ref.shape[0], u_ref.shape[1]
+    half = high_ref.shape[0]
+    parts = half // LANES
+    sums = []
+    for parity in range(2):
+        field = jnp.concatenate(
+            [u_ref[:, :, parity * parts + i, :].reshape(rows * cells, LANES) for i in range(parts)],
+            axis=1,
+        )
+        high, low = split_value(field)
+        columns = slice(parity * half, (parity + 1) * half)
+        t_high, t_low = high_ref[:, columns], low_ref[:, columns]
+        contract = (((1,), (1,)), ((), ()))
+        sums.append(
+            lax.dot_general(t_high, high, contract, preferred_element_type=jnp.float32)
+            + lax.dot_general(t_high, low, contract, preferred_element_type=jnp.float32)
+            + lax.dot_general(t_low, high, contract, preferred_element_type=jnp.float32)
+        )
+    near, far = sums[0] + sums[1], sums[0] - sums[1]
+    targets, groups, width, lanes = o_ref.shape
+    for group in range(groups):
+        columns = slice(group * lanes, (group + 1) * lanes)
+        o_ref[: targets // 2, group] = near[:, columns].reshape(targets // 2, width, lanes)
+        o_ref[targets // 2 :, group] = far[:, columns].reshape(targets // 2, width, lanes)
+
+
+def row_weights(upper, boundary, first, count, squares_ref, c_ref, ahead_ref, behind_ref):
+    def one(index, carry):
+        row = jnp.where(upper, index + (boundary + first), (boundary - 1 - first) - index)
+        number = jnp.full(squares_ref.shape, row, jnp.int32).astype(jnp.float32)
+        radius = number + 0.5
+        outward = (number + 1.0) / radius
+        inward = number / radius
+        diagonal = outward + inward + 2.0 + squares_ref[...] / (radius * radius)
+        c_ref[index] = OMEGA / diagonal
+        ahead_ref[index] = jnp.where(upper, outward, inward)
+        behind_ref[index] = jnp.where(upper, inward, outward)
+        return carry
+
+    lax.fori_loop(0, count, one, 0)
+
+
+def cell_tiles(first, last, cells, size=16):
+    tiles = []
+    if first < 0:
+        tiles.append((first, -first, -1))
+    for start in range(max(first, 0), min(last, cells), size):
+        tiles.append((start, min(size, min(last, cells) - start), 0))
+    if last > cells:
+        tiles.append((cells, last - cells, 1))
+    return tiles
+
+
+def sweep(rows, cells, block, src, source, dst, weights, masks):
+    (src_ref, src_t, src_z), (g_ref, g_t, g_z), (dst_ref, dst_t, dst_z) = src, source, dst
+    c_ref, ahead_ref, behind_ref, w_t = weights
+    low = rows[0]
+
+    def one(step, carry):
+        at = step + (low - w_t)
+        c_row, ahead, behind = c_ref[at], ahead_ref[at], behind_ref[at]
+        for first, count, side in cell_tiles(cells[0], cells[1], block):
+            c = c_row if side == 0 else c_row * masks[0 if side < 0 else 1]
+            z = first - src_z
+            row = low - src_t
+            middle = src_ref[step + row, z - 1 : z + count + 1]
+            gathered = (
+                g_ref[step + (low - g_t), first - g_z : first - g_z + count]
+                + ahead * src_ref[step + (row + 1), z : z + count]
+                + behind * src_ref[step + (row - 1), z : z + count]
+                + (middle[:-2] + middle[2:])
+            )
+            dst_ref[step + (low - dst_t), first - dst_z : first - dst_z + count] = (
+                (1.0 - OMEGA) * middle[1:-1] + c * gathered
+            )
+        return carry
+
+    lax.fori_loop(0, rows[1] - low, one, 0)
+
+
+def first_sweep(rows, cells, block, source, dst, weights, masks):
+    (g_ref, g_t, g_z), (dst_ref, dst_t, dst_z) = source, dst
+    c_ref, w_t = weights[0], weights[3]
+    low = rows[0]
+
+    def one(step, carry):
+        c_row = c_ref[step + (low - w_t)]
+        for first, count, side in cell_tiles(cells[0], cells[1], block):
+            c = c_row if side == 0 else c_row * masks[0 if side < 0 else 1]
+            dst_ref[step + (low - dst_t), first - dst_z : first - dst_z + count] = (
+                c * g_ref[step + (low - g_t), first - g_z : first - g_z + count]
+            )
+        return carry
+
+    lax.fori_loop(0, rows[1] - low, one, 0)
+
+
+def side_masks(pos_ref, shape):
+    left = jnp.full(shape, pos_ref[1] > 0).astype(jnp.float32)
+    right = jnp.full(shape, pos_ref[1] < pos_ref[2] - 1).astype(jnp.float32)
+    return left, right
+
+
+def copies_in(pairs, sems):
+    started = []
+    for i, (src, dst) in enumerate(pairs):
+        copy = pltpu.make_async_copy(src, dst, sems.at[i])
+        copy.start()
+        started.append(copy)
+    return started
+
+
+def smooth_kernel(
+    local_rows, block, pos_ref, squares_ref, deep_ref, near_ref, far_ref, left_ref, right_ref,
+    s_ref, s_left_ref, s_right_ref, u_out, g_out,
+    g, u1, u2, c_ref, ahead_ref, behind_ref, sems, out_sems,
+):
+    upper = pos_ref[0] == 1
+    part = near_ref.shape[0]
+    loads = copies_in(
+        [
+            (deep_ref, g.at[0:DEEP, NEAR : NEAR + block]),
+            (near_ref, g.at[DEEP : DEEP + part, NEAR : NEAR + block]),
+            (far_ref, g.at[DEEP + part : DEEP + local_rows, NEAR : NEAR + block]),
+            (left_ref, g.at[:, 0:NEAR]),
+            (right_ref, g.at[:, NEAR + block : NEAR + block + NEAR]),
+        ],
+        sems,
+    )
+    row_weights(upper, local_rows, -DEEP, DEEP + local_rows, squares_ref, c_ref, ahead_ref, behind_ref)
+    masks = side_masks(pos_ref, squares_ref.shape)
+    weights = (c_ref, ahead_ref, behind_ref, -DEEP)
+    g_at = (g, -DEEP, -NEAR)
+    u1_at = (u1, -DEEP, -NEAR)
+    u2_at = (u2, 1 - DEEP, 1 - NEAR)
+    u1[DEEP + local_rows] = jnp.zeros(u1.shape[1:], jnp.float32)
+    u2[DEEP - 1 + local_rows] = jnp.zeros(u2.shape[1:], jnp.float32)
+    for load in loads:
+        load.wait()
+    g_copy = pltpu.make_async_copy(
+        g.at[DEEP - 1 : DEEP + local_rows, NEAR - 1 : NEAR + block + 1], g_out, out_sems.at[0]
+    )
+    g_copy.start()
+    first_sweep((-DEEP, local_rows), (-NEAR, block + NEAR), block, g_at, u1_at, weights, masks)
+    sweep(
+        (1 - DEEP, local_rows), (1 - NEAR, block + NEAR - 1), block, u1_at, g_at, u2_at, weights, masks
+    )
+    u_copy = pltpu.make_async_copy(
+        u2.at[DEEP - 3 : DEEP - 1 + local_rows, :], u_out, out_sems.at[1]
+    )
+    u_copy.start()
+
+    def residual_row(index, first, count):
+        z = first - u2_at[2]
+        middle = u2[index - 1, z - 1 : z + count + 1]
+        return (
+            g[index, first + NEAR : first + NEAR + count]
+            + ahead_ref[index] * u2[index, z : z + count]
+            + behind_ref[index] * u2[index - 2, z : z + count]
+            + (middle[:-2] + middle[2:])
+            - (OMEGA / c_ref[index]) * middle[1:-1]
+        )
+
+    def restrict_row(index, carry):
+        at = 2 * index + (DEEP - 2 * FAR)
+        for first, count, _ in cell_tiles(0, block, block):
+            both = residual_row(at, first, count) + residual_row(at + 1, first, count)
+            pairs = both.reshape(count // 2, 2, *both.shape[1:])
+            s_ref[index, first // 2 : (first + count) // 2] = pairs[:, 0] + pairs[:, 1]
+        s_left_ref[index] = s_ref[index, 0:FAR]
+        s_right_ref[index] = s_ref[index, block // 2 - FAR : block // 2]
+        return carry
+
+    lax.fori_loop(0, FAR + local_rows // 2, restrict_row, 0)
+    g_copy.wait()
+    u_copy.wait()
+
+
+def correct_kernel(
+    local_rows, block, pos_ref, squares_ref, s_own, s_left, s_right, u_in, g_in,
+    o_ref,
+    s, e0, e1, u, v, g, c_ref, ahead_ref, behind_ref, cc_ref, cahead_ref, cbehind_ref, sems,
+):
+    upper = pos_ref[0] == 1
+    half_rows, half = local_rows // 2, block // 2
+    loads = copies_in(
+        [
+            (s_own, s.at[:, FAR : FAR + half]),
+            (s_left, s.at[:, 0:FAR]),
+            (s_right, s.at[:, FAR + half : FAR + half + FAR]),
+            (u_in, u.at[0 : local_rows + 2]),
+            (g_in, g),
+        ],
+        sems,
+    )
+    masks = side_masks(pos_ref, squares_ref.shape)
+    row_weights(upper, half_rows, -FAR, FAR + half_rows, squares_ref, cc_ref, cahead_ref, cbehind_ref)
+    row_weights(upper, local_rows, -1, 1 + local_rows, squares_ref, c_ref, ahead_ref, behind_ref)
+    coarse = (cc_ref, cahead_ref, cbehind_ref, -FAR)
+    fine = (c_ref, ahead_ref, behind_ref, -1)
+    for buffer in (e0, e1):
+        buffer[FAR + half_rows] = jnp.zeros(buffer.shape[1:], jnp.float32)
+    u[2 + local_rows] = jnp.zeros(u.shape[1:], jnp.float32)
+    v[1 + local_rows] = jnp.zeros(v.shape[1:], jnp.float32)
+    for load in loads[:3]:
+        load.wait()
+    s_at = (s, -FAR, -FAR)
+    here, there = (e0, -FAR, -FAR), (e1, -FAR, -FAR)
+    first_sweep((-FAR, half_rows), (-FAR, half + FAR), half, s_at, here, coarse, masks)
+    for step in range(1, COARSE):
+        sweep(
+            (step - FAR, half_rows), (step - FAR, half + FAR - step), half, here, s_at, there, coarse, masks
+        )
+        here, there = there, here
+    e = here[0]
+    for load in loads[3:]:
+        load.wait()
+
+    def add_correction(index, carry):
+        for first, count in ((-1, (half + 2) // 2), (-1 + (half + 2) // 2, half + 2 - (half + 2) // 2)):
+            part = e[index + FAR - 1, first + FAR : first + FAR + count]
+            twice = jnp.broadcast_to(part[:, None], (count, 2) + part.shape[1:])
+            twice = twice.reshape(2 * count, *part.shape[1:])
+            cells = slice(2 * first + 2, 2 * first + 2 + 2 * count)
+            for offset in range(2):
+                u[2 * index + offset, cells] = u[2 * index + offset, cells] + twice
+        return carry
+
+    lax.fori_loop(0, half_rows + 1, add_correction, 0)
+    u_at, v_at, g_at = (u, -2, -2), (v, -1, -1), (g, -1, -1)
+    sweep((-1, local_rows), (-1, block + 1), block, u_at, g_at, v_at, fine, masks)
+    sweep((0, local_rows), (0, block), block, v_at, g_at, (o_ref, 0, 0), fine, masks)
+
+
+def params(*order):
+    return pltpu.CompilerParams(dimension_semantics=order or None, vmem_limit_bytes=VMEM_LIMIT)
+
+
+def cell_body(density):
+    local_phi, local_rows, vertical_cells = density.shape
+    az_count = lax.axis_size("az")
+    azimuths = local_phi * az_count
+    block = vertical_cells // az_count
+    rows = LANES // block
+    tiles = local_rows // TILE
+    groups = TILE // rows
+    chunks = 2
+    chunk_tiles = tiles // chunks
+    chunk_rows = local_rows // chunks
+    modes, analysis, synthesis = mode_tables(azimuths)
+    squares = jnp.asarray((modes * modes).reshape(-1, LANES))
+    lines = squares.shape[0]
+    point = (lines, LANES)
+    f32 = jnp.float32
+    a_high, a_low = high_low(analysis)
+    s_high, s_low = high_low(synthesis)
+    az_index = lax.axis_index("az")
+    position = jnp.stack([lax.axis_index("rad"), az_index, jnp.int32(az_count)]).astype(jnp.int32)
+    table = pl.BlockSpec((azimuths // 2, azimuths), lambda j, *_: (0, 0))
+    product = 2 * 3 * azimuths * azimuths // 2
+
+    def row_tile(tile, pos_ref):
+        return jnp.where(pos_ref[0] == 0, tiles - 1 - tile, tile)
+
+    def pack(first_tile):
+        return pl.pallas_call(
+            lambda *refs: pack_kernel(block, *refs),
+            grid_spec=pltpu.PrefetchScalarGridSpec(
+                num_scalar_prefetch=1,
+                grid=(chunk_tiles, vertical_cells // LANES),
+                in_specs=[
+                    pl.BlockSpec(
+                        (local_phi, TILE, LANES),
+                        lambda j, k, pos: (0, row_tile(first_tile + j, pos), k),
+                    )
+                ],
+                out_specs=pl.BlockSpec(
+                    (rows, groups, local_phi, LANES), lambda j, k, pos: (k, j, 0, 0)
+                ),
+            ),
+            out_shape=jax.ShapeDtypeStruct(
+                (az_count, chunk_tiles * groups, local_phi, LANES), f32
+            ),
+            compiler_params=params("arbitrary", "arbitrary"),
+            name="pack",
+        )(position, density)
+
+    def analyse(received, with_edge):
+        out_shape = [jax.ShapeDtypeStruct((chunk_rows, block) + point, f32)]
+        out_specs = [pl.BlockSpec((TILE, block) + point, lambda j: (j, 0, 0, 0))]
+        if with_edge:
+            out_shape.append(jax.ShapeDtypeStruct((DEEP, block) + point, f32))
+            out_specs.append(pl.BlockSpec((DEEP, block) + point, lambda j: (0, 0, 0, 0)))
+        return pl.pallas_call(
+            analysis_kernel,
+            grid=(chunk_tiles,),
+            in_specs=[
+                pl.BlockSpec((az_count, groups, local_phi, LANES), lambda j: (0, j, 0, 0)),
+                table,
+                table,
+            ],
+            out_specs=out_specs,
+            out_shape=out_shape,
+            compiler_params=params("arbitrary"),
+            cost_estimate=pl.CostEstimate(
+                flops=product * chunk_rows * block, bytes_accessed=3 * received.size * 4, transcendentals=0
+            ),
+            name="analysis",
+        )(received, a_high, a_low)
+
+    def exchange(value):
+        return lax.all_to_all(value, "az", split_axis=0, concat_axis=0, tiled=True)
+
+    first_received = exchange(pack(0))
+    second_received = exchange(pack(chunk_tiles))
+    near, edge = analyse(first_received, True)
+    deep = lax.ppermute(edge, "rad", [(0, 1), (1, 0)])
+    (far,) = analyse(second_received, False)
+
+    to_right = [(i, i + 1) for i in range(az_count - 1)]
+    to_left = [(i + 1, i) for i in range(az_count - 1)]
+
+    def side(start):
+        return jnp.concatenate([part[:, start : start + NEAR] for part in (deep, near, far)], axis=0)
+
+    left = lax.ppermute(side(block - NEAR), "az", to_right)
+    right = lax.ppermute(side(0), "az", to_left)
+
+    anywhere = pl.BlockSpec(memory_space=pl.ANY)
+    in_vmem = pl.BlockSpec(memory_space=pltpu.VMEM)
+    in_smem = pl.BlockSpec(memory_space=pltpu.SMEM)
+    half_rows, half = local_rows // 2, block // 2
+    all_rows = DEEP + local_rows
+    coarse_rows = FAR + half_rows
+
+    def field(row_count, cell_count):
+        return jax.ShapeDtypeStruct((row_count, cell_count) + point, f32)
+
+    def scratch(row_count, *cell_count):
+        return pltpu.VMEM((row_count,) + cell_count + point, f32)
+
+    s_own, s_head, s_tail, u_two, g_near = pl.pallas_call(
+        lambda *refs: smooth_kernel(local_rows, block, *refs),
+        in_specs=[in_smem, in_vmem] + [anywhere] * 5,
+        out_specs=[in_vmem] * 3 + [anywhere] * 2,
+        out_shape=[
+            field(coarse_rows, half),
+            field(coarse_rows, FAR),
+            field(coarse_rows, FAR),
+            field(local_rows + 2, block + 4),
+            field(local_rows + 1, block + 2),
+        ],
+        scratch_shapes=[
+            scratch(all_rows, block + 2 * NEAR),
+            scratch(all_rows + 1, block + 2 * NEAR),
+            scratch(all_rows, block + 2 * NEAR - 2),
+            scratch(all_rows),
+            scratch(all_rows),
+            scratch(all_rows),
+            pltpu.SemaphoreType.DMA((5,)),
+            pltpu.SemaphoreType.DMA((2,)),
+        ],
+        compiler_params=params(),
+        name="smooth",
+    )(position, squares, deep, near, far, left, right)
+
+    s_left = lax.ppermute(s_tail, "az", to_right)
+    s_right = lax.ppermute(s_head, "az", to_left)
+
+    solved = pl.pallas_call(
+        lambda *refs: correct_kernel(local_rows, block, *refs),
+        in_specs=[in_smem, in_vmem] + [anywhere] * 5,
+        out_specs=in_vmem,
+        out_shape=field(local_rows, block),
+        scratch_shapes=[
+            scratch(coarse_rows, half + 2 * FAR),
+            scratch(coarse_rows + 1, half + 2 * FAR),
+            scratch(coarse_rows + 1, half + 2 * FAR),
+            scratch(local_rows + 3, block + 4),
+            scratch(local_rows + 2, block + 2),
+            scratch(local_rows + 1, block + 2),
+            scratch(local_rows + 1),
+            scratch(local_rows + 1),
+            scratch(local_rows + 1),
+            scratch(coarse_rows),
+            scratch(coarse_rows),
+            scratch(coarse_rows),
+            pltpu.SemaphoreType.DMA((5,)),
+        ],
+        compiler_params=params(),
+        name="correct",
+    )(position, squares, s_own, s_left, s_right, u_two, g_near)
+
+    physical = pl.pallas_call(
+        synthesis_kernel,
+        grid=(tiles,),
+        in_specs=[
+            pl.BlockSpec((TILE, block) + point, lambda j: (j, 0, 0, 0)),
+            table,
+            table,
+        ],
+        out_specs=pl.BlockSpec((az_count, groups, local_phi, LANES), lambda j: (0, j, 0, 0)),
+        out_shape=jax.ShapeDtypeStruct((az_count, tiles * groups, local_phi, LANES), f32),
+        compiler_params=params("arbitrary"),
+        name="synthesis",
+    )(solved, s_high, s_low)
+
+    returned = exchange(physical)
+    return pl.pallas_call(
+        lambda *refs: unpack_kernel(block, *refs),
+        grid_spec=pltpu.PrefetchScalarGridSpec(
+            num_scalar_prefetch=1,
+            grid=(tiles, vertical_cells // LANES),
+            in_specs=[
+                pl.BlockSpec((rows, groups, local_phi, LANES), lambda j, k, pos: (k, j, 0, 0))
+            ],
+            out_specs=pl.BlockSpec(
+                (local_phi, TILE, LANES), lambda j, k, pos: (0, row_tile(j, pos), k)
+            ),
+        ),
+        out_shape=jax.ShapeDtypeStruct(density.shape, f32),
+        compiler_params=params("arbitrary", "arbitrary"),
+        name="unpack",
+    )(position, returned)
+
+
+def fits_cells(density):
+    local_phi, local_rows, vertical_cells = density.shape
+    az_count, rad_count = lax.axis_size("az"), lax.axis_size("rad")
+    block = vertical_cells // az_count
+    return (
+        rad_count == 2
+        and vertical_cells % (az_count * 2) == 0
+        and vertical_cells % LANES == 0
+        and LANES // TILE <= block <= LANES
+        and LANES % block == 0
+        and block // 2 >= FAR
+        and local_rows % (4 * TILE) == 0
+        and local_rows // 2 >= DEEP
+        and az_count % 2 == 0
+        and local_phi % TILE == 0
+        and (az_count * local_phi) % (2 * LANES) == 0
+        and az_count * local_phi == TILE * LANES
+    )
+
+
+def body(density):
+    return cell_body(density) if fits_cells(density) else general_body(density)
 
 
 def solution(mesh):

time: 695 us -> 305 us (0.44)
  waiting for transfers between devices: 295 us -> 98.7 us
  local copies, waits for them, and re-layouts: 81.2 us -> 7.39 us
  other arithmetic: 73.7 us -> 0.67 us
  Pallas kernels: 0 us -> 71 us
  matrix products: 67.7 us -> 0 us
  starting transfers between devices: 74.2 us -> 24.1 us
    all_to_all x3 -> x2, waiting for transfers between devices: 277 us -> 80 us  [exchange(): return lax.all_to_all(value, 'az', split_axis=0, concat_axis=0, tiled=True)]
    pallas_call x0 -> x8, Pallas kernels: none -> 71 us  [the longest x2 14.7 us: pack(): pl.pallas_call(lambda *refs: pack_kernel(block, *refs), grid_spec=pltpu.P...]
    dot_general x2 -> x0, matrix products: 67.7 us -> none  [transform_with(): jnp.dot(table, matrix, precision=lax.Precision.HIGHEST, preferred_element...]
    reshape x8 -> x0, local copies, waits for them, and re-layouts: 49.2 us -> none  [the longest x2 12.8 us: transform_with(): return result.reshape(azimuths, 1, width)]
    ppermute x18 -> x5, starting transfers between devices: 47.7 us -> 12.6 us  [the longest x1 4.37 us: cell_body(): s_right = lax.ppermute(s_head, 'az', to_left)]
    add x13 -> x0, other arithmetic: 29.6 us -> none  [the longest x8 24.9 us: relax(): iterate + OMEGA * (source - apply_op(iterate, pad_both(iterate), coeffici...]
    concatenate x9 -> x2, other arithmetic: 18.3 us -> 0.08 us  [side(): jnp.concatenate([part[:, start:start + NEAR] for part in (deep, near, far...]
    all_to_all x3 -> x2, starting transfers between devices: 26.4 us -> 11.5 us  [exchange(): return lax.all_to_all(value, 'az', split_axis=0, concat_axis=0, tiled=True)]
  transfers between devices with their start and end apart: 21 -> 7, of which waited for: 21 -> 6; matrix products, arithmetic and copies ran while one was open for 0% -> 1% of each run, Pallas kernels for 0% -> 7%
where the time goes in v1:
time: 305 us; the launch traced here: 303 us
  blocking collectives  101 us (33%)
  waiting for transfers between devices  98.7 us (32%)
  Pallas kernels  71 us (23%)
  starting transfers between devices  24.1 us (8%)
  local copies, waits for them, and re-layouts  7.39 us (2%)
    all_to_all x1, blocking collectives, exchange(): return lax.all_to_all(value, 'az', split_axis=0, concat_axis=0, tiled=True)  101 us
    all_to_all x2, waiting for transfers between devices, exchange(): return lax.all_to_all(value, 'az', split_axis=0, concat_axis=0, tiled=True)  80 us
    pallas_call x2, Pallas kernels, pack(): pl.pallas_call(lambda *refs: pack_kernel(block, *refs), grid_spec=pltpu.P...  14.7 us
    pallas_call x1, Pallas kernels, cell_body(): pl.pallas_call(lambda *refs: unpack_kernel(block, *refs), grid_spec=pltpu...  12.9 us
    pallas_call x2, Pallas kernels, analyse(): pl.pallas_call(analysis_kernel, grid=(chunk_tiles,), in_specs=[pl.BlockSp...  12.5 us
    pallas_call x1, Pallas kernels, cell_body(): pl.pallas_call(lambda *refs: correct_kernel(local_rows, block, *refs), in...  11.6 us
    all_to_all x2, starting transfers between devices, exchange(): return lax.all_to_all(value, 'az', split_axis=0, concat_axis=0, tiled=True)  11.5 us
    pallas_call x1, Pallas kernels, cell_body(): pl.pallas_call(lambda *refs: smooth_kernel(local_rows, block, *refs), in_...  10.6 us
  transfers between devices with their start and end apart: 7, of which 6 were waited for; matrix products, arithmetic and copies ran while one was open for 1% of the time, Pallas kernels for 7%

profile of v1, /device:TPU:11, one launch (start us, length us, event | category | flops | bytes accessed | tf_op | source)
XLA Modules:
  0.0 302.6 jit_solution(17592404379587173691)
XLA Ops:
  0.0 0.6 pad_add_fusion.refs_0_
  0.6 7.3 %pack.2 = f32[16,4,64,128]{3,2,1,0:T(8,128)} custom-call(s32[3]{0:T(128)} %pad_add_fusion.refs_0_, f32[64,32,512]{2,1,0:T(8,128)} %refs_1_.5), custom_call_target="tpu_custom_call" | custom-call | tf_op jit(solution)/shard_map/pack/pallas_call | solution.py:527
  7.9 6.6 %all-to-all-start = ((f32[16,4,64,128]{3,2,1,0:T(8,128)}), f32[16,4,64,128]{3,2,1,0:T(8,128)S(1)}, u32[]{:S(2)}, u32[]{:S(2)}) async-start(f32[16,4,64,128]{3,2,1,0:T(8,128)} %pack.2), calls=%async_computation | async-start | bytes 4194304 | tf_op jit(solution)/shard_map/all_to_all | solution.py:573
  14.5 7.3 %pack.3 = f32[16,4,64,128]{3,2,1,0:T(8,128)} custom-call(s32[3]{0:T(128)} %pad_add_fusion.refs_0_, f32[64,32,512]{2,1,0:T(8,128)} %refs_1_.5), custom_call_target="tpu_custom_call" | custom-call | tf_op jit(solution)/shard_map/pack/pallas_call | solution.py:527
  21.8 40.1 %all-to-all-done.x_ref = f32[16,4,64,128]{3,2,1,0:T(8,128)S(1)} async-done(((f32[16,4,64,128]{3,2,1,0:T(8,128)}), f32[16,4,64,128]{3,2,1,0:T(8,128)S(1)}, u32[]{:S(2)}, u32[]{:S(2)}) %all-to-all-start) | async-done | bytes 2097184 | tf_op jit(solution)/shard_map/all_to_all | solution.py:573
  61.9 0.0 copy-start.1
  61.9 1.3 copy-done.1
  63.2 4.9 %all-to-all-start.1 = ((f32[16,4,64,128]{3,2,1,0:T(8,128)}), f32[16,4,64,128]{3,2,1,0:T(8,128)S(1)}, u32[]{:S(2)}, u32[]{:S(2)}) async-start(f32[16,4,64,128]{3,2,1,0:T(8,128)} %pack.3), calls=%async_computation.1 | async-start | bytes 4194304 | tf_op jit(solution)/shard_map/all_to_all | solution.py:573
  68.1 6.6 %analysis.2 = (f32[16,32,8,128]{3,2,1,0:T(8,128)}, f32[14,32,8,128]{3,2,1,0:T(8,128)}) custom-call(f32[16,4,64,128]{3,2,1,0:T(8,128)} %copy-done.1, bf16[512,1024]{1,0:T(8,128)(2,1)} %constant.21.clone.high_ref, bf16[512,1024]{1,0:T(8,128)(2,1)} %constant.22.clone.low_ref), custom_call_target="tpu_custom_call" | custom-call | flops 1610612736 | bytes 6291456 | tf_op jit(solution)/shard_map/analysis/pallas_call | solution.py:555
  74.7 1.2 collective-permute-start
  76.0 40.0 %all-to-all-done.1.x_ref = f32[16,4,64,128]{3,2,1,0:T(8,128)S(1)} async-done(((f32[16,4,64,128]{3,2,1,0:T(8,128)}), f32[16,4,64,128]{3,2,1,0:T(8,128)S(1)}, u32[]{:S(2)}, u32[]{:S(2)}) %all-to-all-start.1) | async-done | bytes 2097184 | tf_op jit(solution)/shard_map/all_to_all | solution.py:573
  115.9 0.0 copy-start
  115.9 1.3 copy-done
  117.3 5.9 %analysis.3.refs_4_ = f32[16,32,8,128]{3,2,1,0:T(8,128)} custom-call(f32[16,4,64,128]{3,2,1,0:T(8,128)} %copy-done, bf16[512,1024]{1,0:T(8,128)(2,1)} %constant.21.clone.high_ref, bf16[512,1024]{1,0:T(8,128)(2,1)} %constant.22.clone.low_ref), custom_call_target="tpu_custom_call" | custom-call | flops 1610612736 | bytes 6291456 | tf_op jit(solution)/shard_map/analysis/pallas_call | solution.py:555
  123.2 1.1 fusion.1
  124.2 1.1 fusion
  125.3 0.0 collective-permute-done.refs_2_
  125.3 1.0 fusion.2
  126.4 3.2 %collective-permute-start.1 = (f32[46,3,8,128]{3,2,1,0:T(8,128)S(1)}, f32[46,3,8,128]{3,2,1,0:T(8,128)S(1)}, u32[]{:S(2)}, u32[]{:S(2)}) collective-permute-start(f32[46,3,8,128]{3,2,1,0:T(8,128)S(1)} %pad_maximum_fusion), channel_id=1, source_target_pairs={{0,2},{2,4},{4,6},{6,8},{8,10},{10,12},{12,14},{14,16},{16,18},{18... | collective-permute-start | bytes 1695752 | tf_op jit(solution)/shard_map/ppermute | solution.py:587
  129.6 1.9 collective-permute-start.2
  131.5 4.6 %collective-permute-done.1.refs_5_ = f32[46,3,8,128]{3,2,1,0:T(8,128)S(1)} collective-permute-done((f32[46,3,8,128]{3,2,1,0:T(8,128)S(1)}, f32[46,3,8,128]{3,2,1,0:T(8,128)S(1)}, u32[]{:S(2)}, u32[]{:S(2)}) %collective-permute-start.1) | collective-permute-done | bytes 565280 | tf_op jit(solution)/shard_map/ppermute | solution.py:587
  136.1 0.0 copy-start.2
  136.1 5.4 %collective-permute-done.2.refs_6_ = f32[46,3,8,128]{3,2,1,0:T(8,128)S(1)} collective-permute-done((f32[46,3,8,128]{3,2,1,0:T(8,128)S(1)}, f32[46,3,8,128]{3,2,1,0:T(8,128)S(1)}, u32[]{:S(2)}, u32[]{:S(2)}) %collective-permute-start.2) | collective-permute-done | bytes 565280 | tf_op jit(solution)/shard_map/ppermute | solution.py:588
  141.5 0.0 copy-done.2
  141.5 0.0 copy-start.3
  141.5 0.8 copy-done.3
  142.3 10.6 %smooth.1 = (f32[22,16,8,128]{3,2,1,0:T(8,128)}, f32[22,6,8,128]{3,2,1,0:T(8,128)}, f32[22,6,8,128]{3,2,1,0:T(8,128)}, f32[34,36,8,128]{3,2,1,0:T(8,128)}, f32[33,34,8,128]{3,2,1,0:T(8,128)}) custom-call(s32[3]{0:T(128)} %pad_add_fusion.refs_0_, f32[8,128]{1,0:T(8,128)} %constant.20.clone.refs_1_, f32[14,32,8,128]{3,2,1,0:T(8,128)} %collective-permute-done.refs_2_, ...), custom_call_target="tpu_custom_call" | custom-call | tf_op jit(solution)/shard_map/smooth/pallas_call | solution.py:603
  152.9 1.9 collective-permute-start.3
  154.8 4.4 %collective-permute-start.4 = (f32[22,6,8,128]{3,2,1,0:T(8,128)}, f32[22,6,8,128]{3,2,1,0:T(8,128)S(1)}, u32[]{:S(2)}, u32[]{:S(2)}) collective-permute-start(f32[22,6,8,128]{3,2,1,0:T(8,128)} %get-tuple-element.16), channel_id=1, source_target_pairs={{2,0},{4,2},{6,4},{8,6},{10,8},{12,10},{14,12},{16,14},{18,16},{20... | collective-permute-start | bytes 1622024 | tf_op jit(solution)/shard_map/ppermute | solution.py:629
  159.2 2.2 collective-permute-done.3.refs_3_
  161.4 0.0 copy-start.4
  161.4 6.5 %collective-permute-done.4.refs_4_ = f32[22,6,8,128]{3,2,1,0:T(8,128)S(1)} collective-permute-done((f32[22,6,8,128]{3,2,1,0:T(8,128)}, f32[22,6,8,128]{3,2,1,0:T(8,128)S(1)}, u32[]{:S(2)}, u32[]{:S(2)}) %collective-permute-start.4) | collective-permute-done | bytes 540704 | tf_op jit(solution)/shard_map/ppermute | solution.py:629
  167.9 0.0 copy-start.5
  167.9 0.0 copy-done.4
  167.9 0.8 copy-done.5
  168.7 11.6 %correct.1.u_ref = f32[32,32,8,128]{3,2,1,0:T(8,128)} custom-call(s32[3]{0:T(128)} %pad_add_fusion.refs_0_, f32[8,128]{1,0:T(8,128)} %constant.20.clone.refs_1_, f32[22,16,8,128]{3,2,1,0:T(8,128)} %get-tuple-element.14.refs_2_, f32[22,6,8,128]{3,2,1,0:T(8,128)} %copy-done.4, f32[22,6,8,128]{3,2,1,0:T(8,128)} %copy-done.5, ...), custom_call_target="tpu_custom_call" | custom-call | tf_op jit(solution)/shard_map/correct/pallas_call | solution.py:631
  180.3 8.8 %synthesis.1 = f32[16,8,64,128]{3,2,1,0:T(8,128)} custom-call(f32[32,32,8,128]{3,2,1,0:T(8,128)} %correct.1.u_ref, bf16[512,1024]{1,0:T(8,128)(2,1)} %constant.23.clone.high_ref, bf16[512,1024]{1,0:T(8,128)(2,1)} %constant.24.clone.low_ref), custom_call_target="tpu_custom_call" | custom-call | tf_op jit(solution)/shard_map/synthesis/pallas_call | solution.py:655
  189.1 100.6 %all_to_all.15.refs_1_ = f32[16,8,64,128]{3,2,1,0:T(8,128)} all-to-all(f32[16,8,64,128]{3,2,1,0:T(8,128)} %synthesis.1), channel_id=1, replica_groups=mesh['az'=16,'rad'=2] {'az'}, dimensions={0} | all-to-all | bytes 8388608 | tf_op jit(solution)/shard_map/all_to_all | solution.py:573
  289.7 12.9 %unpack.1 = f32[64,32,512]{2,1,0:T(8,128)} custom-call(s32[3]{0:T(128)} %pad_add_fusion.refs_0_, f32[16,8,64,128]{3,2,1,0:T(8,128)} %all_to_all.15.refs_1_), custom_call_target="tpu_custom_call" | custom-call | tf_op jit(solution)/shard_map/unpack/pallas_call | solution.py:670
  (2 shorter events, 0.1 us)
Async XLA Ops:
  7.9 54.0 %all-to-all-start = ((f32[16,4,64,128]{3,2,1,0:T(8,128)}), f32[16,4,64,128]{3,2,1,0:T(8,128)S(1)}, u32[]{:S(2)}, u32[]{:S(2)}) async-start(f32[16,4,64,128]{3,2,1,0:T(8,128)} %pack.2), calls=%async_computation | async-start | bytes 4194304 | tf_op jit(solution)/shard_map/all_to_all | solution.py:573
  61.9 1.3 copy-start.1
  63.2 52.7 %all-to-all-start.1 = ((f32[16,4,64,128]{3,2,1,0:T(8,128)}), f32[16,4,64,128]{3,2,1,0:T(8,128)S(1)}, u32[]{:S(2)}, u32[]{:S(2)}) async-start(f32[16,4,64,128]{3,2,1,0:T(8,128)} %pack.3), calls=%async_computation.1 | async-start | bytes 4194304 | tf_op jit(solution)/shard_map/all_to_all | solution.py:573
  74.7 50.5 %collective-permute-start = (f32[14,32,8,128]{3,2,1,0:T(8,128)}, f32[14,32,8,128]{3,2,1,0:T(8,128)}, u32[]{:S(2)}, u32[]{:S(2)}) collective-permute-start(f32[14,32,8,128]{3,2,1,0:T(8,128)} %get-tuple-element.12), channel_id=1, source_target_pairs={{0,1},{1,0},{2,3},{3,2},{4,5},{5,4},{6,7},{7,6},{8,9},{9,8},{10,11... | collective-permute-start | bytes 5505032 | tf_op jit(solution)/shard_map/ppermute | solution.py:578
  115.9 1.3 copy-start
  126.4 9.8 %collective-permute-start.1 = (f32[46,3,8,128]{3,2,1,0:T(8,128)S(1)}, f32[46,3,8,128]{3,2,1,0:T(8,128)S(1)}, u32[]{:S(2)}, u32[]{:S(2)}) collective-permute-start(f32[46,3,8,128]{3,2,1,0:T(8,128)S(1)} %pad_maximum_fusion), channel_id=1, source_target_pairs={{0,2},{2,4},{4,6},{6,8},{8,10},{10,12},{12,14},{14,16},{16,18},{18... | collective-permute-start | bytes 1695752 | tf_op jit(solution)/shard_map/ppermute | solution.py:587
  129.6 11.9 %collective-permute-start.2 = (f32[46,3,8,128]{3,2,1,0:T(8,128)S(1)}, f32[46,3,8,128]{3,2,1,0:T(8,128)S(1)}, u32[]{:S(2)}, u32[]{:S(2)}) collective-permute-start(f32[46,3,8,128]{3,2,1,0:T(8,128)S(1)} %pad_maximum_fusion.1), channel_id=1, source_target_pairs={{2,0},{4,2},{6,4},{8,6},{10,8},{12,10},{14,12},{16,14},{18,16},{20... | collective-permute-start | bytes 1695752 | tf_op jit(solution)/shard_map/ppermute | solution.py:588
  136.1 5.4 %copy-start.2 = (f32[46,3,8,128]{3,2,1,0:T(8,128)}, f32[46,3,8,128]{3,2,1,0:T(8,128)S(1)}, u32[]{:S(2)}) copy-start(f32[46,3,8,128]{3,2,1,0:T(8,128)S(1)} %collective-permute-done.1.refs_5_) | copy-start | bytes 1695748
  141.5 0.8 copy-start.3
  152.9 8.5 %collective-permute-start.3 = (f32[22,6,8,128]{3,2,1,0:T(8,128)}, f32[22,6,8,128]{3,2,1,0:T(8,128)S(1)}, u32[]{:S(2)}, u32[]{:S(2)}) collective-permute-start(f32[22,6,8,128]{3,2,1,0:T(8,128)} %get-tuple-element.15), channel_id=1, source_target_pairs={{0,2},{2,4},{4,6},{6,8},{8,10},{10,12},{12,14},{14,16},{16,18},{18... | collective-permute-start | bytes 1622024 | tf_op jit(solution)/shard_map/ppermute | solution.py:628
  154.8 13.1 %collective-permute-start.4 = (f32[22,6,8,128]{3,2,1,0:T(8,128)}, f32[22,6,8,128]{3,2,1,0:T(8,128)S(1)}, u32[]{:S(2)}, u32[]{:S(2)}) collective-permute-start(f32[22,6,8,128]{3,2,1,0:T(8,128)} %get-tuple-element.16), channel_id=1, source_target_pairs={{2,0},{4,2},{6,4},{8,6},{10,8},{12,10},{14,12},{16,14},{18,16},{20... | collective-permute-start | bytes 1622024 | tf_op jit(solution)/shard_map/ppermute | solution.py:629
  161.4 6.5 %copy-start.4 = (f32[22,6,8,128]{3,2,1,0:T(8,128)}, f32[22,6,8,128]{3,2,1,0:T(8,128)S(1)}, u32[]{:S(2)}) copy-start(f32[22,6,8,128]{3,2,1,0:T(8,128)S(1)} %collective-permute-done.3.refs_3_) | copy-start | bytes 1622020
  167.9 0.8 copy-start.5

commit v2 on v1

--- a/solution.py
+++ b/solution.py
@@ -20,7 +20,6 @@
 DEEP = 2 * COARSE + 2
 NEAR = 3
 FAR = COARSE
-VMEM_LIMIT = 56 * 1024 * 1024
 
 
 def with_halo(cells, sides, width):
@@ -180,6 +179,10 @@
 def split_value(value):
     high = value.astype(jnp.bfloat16)
     return high, (value - high.astype(jnp.float32)).astype(jnp.bfloat16)
+
+
+def row_tile(pos_ref, local_rows, tile):
+    return jnp.where(pos_ref[0] == 0, local_rows // TILE - 1 - tile, tile)
 
 
 def swap_chunks(parts, chunk):
@@ -204,30 +207,64 @@
     return jnp.where(pos_ref[0] == 0, TILE - 1 - row, row)
 
 
-def pack_kernel(block, pos_ref, x_ref, o_ref):
+def pack_kernel(block, order, first_tile, pos_ref, x_ref, o_ref, x, o, in_sems, out_sems):
     rows = LANES // block
-    local_phi = x_ref.shape[0]
-    flat = x_ref.reshape(local_phi * TILE, LANES)
-    for group in range(TILE // rows):
-        parts = [
-            flat[pl.ds(tile_row(pos_ref, group * rows + i), local_phi, stride=TILE), :]
-            for i in range(rows)
-        ]
-        for q, part in enumerate(swap_chunks(parts, block)):
-            o_ref[q, group] = part
-
-
-def unpack_kernel(block, pos_ref, x_ref, o_ref):
+    local_phi, local_rows, cells = x_ref.shape
+    tiles, lane_tiles, groups = x.shape[0], x.shape[1], TILE // rows
+    pieces = [(j, k) for j in range(tiles) for k in range(lane_tiles)]
+    loads, stores = [], []
+    for n, (j, k) in enumerate(pieces):
+        start = pl.multiple_of(row_tile(pos_ref, local_rows, first_tile + j) * TILE, TILE)
+        source = x_ref.at[:, pl.ds(start, TILE), k * LANES : (k + 1) * LANES]
+        loads.append(pltpu.make_async_copy(source, x.at[j, k], in_sems.at[n]))
+        loads[-1].start()
+    for n, (j, k) in enumerate(pieces):
+        loads[n].wait()
+        flat = x.at[j, k].reshape(local_phi * TILE, LANES)
+        for group in range(groups):
+            parts = [
+                flat[pl.ds(tile_row(pos_ref, group * rows + i), local_phi, stride=TILE), :]
+                for i in range(rows)
+            ]
+            for q, part in enumerate(swap_chunks(parts, block)):
+                o[order[k * rows + q], j * groups + group] = part
+        if k == lane_tiles - 1:
+            span = slice(j * groups, (j + 1) * groups)
+            stores.append(pltpu.make_async_copy(o.at[:, span], o_ref.at[:, span], out_sems.at[j]))
+            stores[-1].start()
+    for store in stores:
+        store.wait()
+
+
+def unpack_kernel(block, order, pos_ref, x_ref, o_ref, x, o, in_sems, out_sems):
     rows = LANES // block
-    local_phi = o_ref.shape[0]
-    flat = o_ref.reshape(local_phi * TILE, LANES)
-    for group in range(TILE // rows):
-        parts = [x_ref[q, group] for q in range(rows)]
-        for i, part in enumerate(swap_chunks(parts, block)):
-            flat[pl.ds(tile_row(pos_ref, group * rows + i), local_phi, stride=TILE), :] = part
-
-
-def analysis_kernel(x_ref, high_ref, low_ref, o_ref, edge_ref=None):
+    local_phi, local_rows, cells = o_ref.shape
+    tiles, lane_tiles, groups = o.shape[0], o.shape[1], TILE // rows
+    loads, stores = [], []
+    for j in range(tiles):
+        span = slice(j * groups, (j + 1) * groups)
+        loads.append(pltpu.make_async_copy(x_ref.at[:, span], x.at[:, span], in_sems.at[j]))
+        loads[-1].start()
+    for j in range(tiles):
+        loads[j].wait()
+        start = pl.multiple_of(row_tile(pos_ref, local_rows, j) * TILE, TILE)
+        for k in range(lane_tiles):
+            flat = o.at[j, k].reshape(local_phi * TILE, LANES)
+            for group in range(groups):
+                parts = [x[order[k * rows + q], j * groups + group] for q in range(rows)]
+                for i, part in enumerate(swap_chunks(parts, block)):
+                    at = tile_row(pos_ref, group * rows + i)
+                    flat[pl.ds(at, local_phi, stride=TILE), :] = part
+            target = o_ref.at[:, pl.ds(start, TILE), k * LANES : (k + 1) * LANES]
+            stores.append(
+                pltpu.make_async_copy(o.at[j, k], target, out_sems.at[j * lane_tiles + k])
+            )
+            stores[-1].start()
+    for store in stores:
+        store.wait()
+
+
+def analysis_kernel(x_ref, high_ref, low_ref, o_ref, head_ref, tail_ref, *edge_refs):
     sources, groups, width, lanes = x_ref.shape
     half = sources // 2 * width
     rows, cells = o_ref.shape[0], o_ref.shape[1]
@@ -248,14 +285,20 @@
         for part in range(half // LANES):
             piece = result[:, part * LANES : (part + 1) * LANES]
             o_ref[:, :, parity * (half // LANES) + part, :] = piece.reshape(rows, cells, LANES)
-    if edge_ref is not None:
+    head_ref[...] = o_ref[:, :NEAR]
+    tail_ref[...] = o_ref[:, cells - NEAR :]
+    if edge_refs:
+        edge_ref, edge_head_ref, edge_tail_ref = edge_refs
         for step in range(-(-DEEP // rows)):
 
             @pl.when(pl.program_id(0) == step)
             def _():
                 for row in range(rows):
-                    if step * rows + row < DEEP:
-                        edge_ref[DEEP - 1 - step * rows - row] = o_ref[row]
+                    at = DEEP - 1 - step * rows - row
+                    if at >= 0:
+                        edge_ref[at] = o_ref[row]
+                        edge_head_ref[at] = o_ref[row, :NEAR]
+                        edge_tail_ref[at] = o_ref[row, cells - NEAR :]
 
 
 def synthesis_kernel(u_ref, high_ref, low_ref, o_ref):
@@ -372,22 +415,21 @@
 
 
 def smooth_kernel(
-    local_rows, block, pos_ref, squares_ref, deep_ref, near_ref, far_ref, left_ref, right_ref,
+    local_rows, block, pos_ref, squares_ref, *refs
+):
+    field_refs, (
     s_ref, s_left_ref, s_right_ref, u_out, g_out,
     g, u1, u2, c_ref, ahead_ref, behind_ref, sems, out_sems,
-):
+    ) = refs[:9], refs[9:]
     upper = pos_ref[0] == 1
-    part = near_ref.shape[0]
-    loads = copies_in(
-        [
-            (deep_ref, g.at[0:DEEP, NEAR : NEAR + block]),
-            (near_ref, g.at[DEEP : DEEP + part, NEAR : NEAR + block]),
-            (far_ref, g.at[DEEP + part : DEEP + local_rows, NEAR : NEAR + block]),
-            (left_ref, g.at[:, 0:NEAR]),
-            (right_ref, g.at[:, NEAR + block : NEAR + block + NEAR]),
-        ],
-        sems,
-    )
+    columns = (slice(NEAR, NEAR + block), slice(0, NEAR), slice(NEAR + block, NEAR + block + NEAR))
+    pairs, start = [], 0
+    for n in range(3):
+        count = field_refs[3 * n].shape[0]
+        for ref, column in zip(field_refs[3 * n : 3 * n + 3], columns):
+            pairs.append((ref, g.at[start : start + count, column]))
+        start += count
+    loads = copies_in(pairs, sems)
     row_weights(upper, local_rows, -DEEP, DEEP + local_rows, squares_ref, c_ref, ahead_ref, behind_ref)
     masks = side_masks(pos_ref, squares_ref.shape)
     weights = (c_ref, ahead_ref, behind_ref, -DEEP)
@@ -493,8 +535,10 @@
     sweep((0, local_rows), (0, block), block, v_at, g_at, (o_ref, 0, 0), fine, masks)
 
 
-def params(*order):
-    return pltpu.CompilerParams(dimension_semantics=order or None, vmem_limit_bytes=VMEM_LIMIT)
+def params(mebibytes, *order):
+    return pltpu.CompilerParams(
+        dimension_semantics=order or None, vmem_limit_bytes=mebibytes * 1024 * 1024
+    )
 
 
 def cell_body(density):
@@ -515,43 +559,49 @@
     f32 = jnp.float32
     a_high, a_low = high_low(analysis)
     s_high, s_low = high_low(synthesis)
+    order = block_order(az_count)
     az_index = lax.axis_index("az")
-    position = jnp.stack([lax.axis_index("rad"), az_index, jnp.int32(az_count)]).astype(jnp.int32)
+    rad_index = lax.axis_index("rad")
+    block_index = jnp.where((az_index // 4) % 2 == 1, az_index ^ 2, az_index)
+    position = jnp.stack([rad_index, block_index, jnp.int32(az_count)]).astype(jnp.int32)
     table = pl.BlockSpec((azimuths // 2, azimuths), lambda j, *_: (0, 0))
     product = 2 * 3 * azimuths * azimuths // 2
-
-    def row_tile(tile, pos_ref):
-        return jnp.where(pos_ref[0] == 0, tiles - 1 - tile, tile)
+    lane_tiles = vertical_cells // LANES
+    anywhere = pl.BlockSpec(memory_space=pl.ANY)
+    in_vmem = pl.BlockSpec(memory_space=pltpu.VMEM)
+    in_smem = pl.BlockSpec(memory_space=pltpu.SMEM)
 
     def pack(first_tile):
         return pl.pallas_call(
-            lambda *refs: pack_kernel(block, *refs),
-            grid_spec=pltpu.PrefetchScalarGridSpec(
-                num_scalar_prefetch=1,
-                grid=(chunk_tiles, vertical_cells // LANES),
-                in_specs=[
-                    pl.BlockSpec(
-                        (local_phi, TILE, LANES),
-                        lambda j, k, pos: (0, row_tile(first_tile + j, pos), k),
-                    )
-                ],
-                out_specs=pl.BlockSpec(
-                    (rows, groups, local_phi, LANES), lambda j, k, pos: (k, j, 0, 0)
-                ),
-            ),
+            lambda *refs: pack_kernel(block, order, first_tile, *refs),
+            in_specs=[in_smem, anywhere],
+            out_specs=anywhere,
             out_shape=jax.ShapeDtypeStruct(
                 (az_count, chunk_tiles * groups, local_phi, LANES), f32
             ),
-            compiler_params=params("arbitrary", "arbitrary"),
+            scratch_shapes=[
+                pltpu.VMEM((chunk_tiles, lane_tiles, local_phi, TILE, LANES), f32),
+                pltpu.VMEM((az_count, chunk_tiles * groups, local_phi, LANES), f32),
+                pltpu.SemaphoreType.DMA((chunk_tiles * lane_tiles,)),
+                pltpu.SemaphoreType.DMA((chunk_tiles,)),
+            ],
+            compiler_params=params(8),
             name="pack",
         )(position, density)
 
     def analyse(received, with_edge):
-        out_shape = [jax.ShapeDtypeStruct((chunk_rows, block) + point, f32)]
-        out_specs = [pl.BlockSpec((TILE, block) + point, lambda j: (j, 0, 0, 0))]
+        def whole(count, cells):
+            return pl.BlockSpec((count, cells) + point, lambda j: (0, 0, 0, 0))
+
+        def moving(cells):
+            return pl.BlockSpec((TILE, cells) + point, lambda j: (j, 0, 0, 0))
+
+        widths = (block, NEAR, NEAR)
+        out_shape = [field(chunk_rows, width) for width in widths]
+        out_specs = [moving(width) for width in widths]
         if with_edge:
-            out_shape.append(jax.ShapeDtypeStruct((DEEP, block) + point, f32))
-            out_specs.append(pl.BlockSpec((DEEP, block) + point, lambda j: (0, 0, 0, 0)))
+            out_shape += [field(DEEP, width) for width in widths]
+            out_specs += [whole(DEEP, width) for width in widths]
         return pl.pallas_call(
             analysis_kernel,
             grid=(chunk_tiles,),
@@ -562,7 +612,7 @@
             ],
             out_specs=out_specs,
             out_shape=out_shape,
-            compiler_params=params("arbitrary"),
+            compiler_params=params(24, "arbitrary"),
             cost_estimate=pl.CostEstimate(
                 flops=product * chunk_rows * block, bytes_accessed=3 * received.size * 4, transcendentals=0
             ),
@@ -572,37 +622,38 @@
     def exchange(value):
         return lax.all_to_all(value, "az", split_axis=0, concat_axis=0, tiled=True)
 
+    to_right = [(order[i], order[i + 1]) for i in range(az_count - 1)]
+    to_left = [(b, a) for a, b in to_right]
+
+    def from_sides(head, tail):
+        return lax.ppermute(tail, "az", to_right), lax.ppermute(head, "az", to_left)
+
+    def across(pairs):
+        return [(2 * a + y, 2 * b + 1 - y) for a, b in pairs for y in range(2)]
+
+    def field(row_count, cell_count):
+        return jax.ShapeDtypeStruct((row_count, cell_count) + point, f32)
+
+    def scratch(row_count, *cell_count):
+        return pltpu.VMEM((row_count,) + cell_count + point, f32)
+
     first_received = exchange(pack(0))
     second_received = exchange(pack(chunk_tiles))
-    near, edge = analyse(first_received, True)
+    near, near_head, near_tail, edge, edge_head, edge_tail = analyse(first_received, True)
     deep = lax.ppermute(edge, "rad", [(0, 1), (1, 0)])
-    (far,) = analyse(second_received, False)
-
-    to_right = [(i, i + 1) for i in range(az_count - 1)]
-    to_left = [(i + 1, i) for i in range(az_count - 1)]
-
-    def side(start):
-        return jnp.concatenate([part[:, start : start + NEAR] for part in (deep, near, far)], axis=0)
-
-    left = lax.ppermute(side(block - NEAR), "az", to_right)
-    right = lax.ppermute(side(0), "az", to_left)
-
-    anywhere = pl.BlockSpec(memory_space=pl.ANY)
-    in_vmem = pl.BlockSpec(memory_space=pltpu.VMEM)
-    in_smem = pl.BlockSpec(memory_space=pltpu.SMEM)
+    near_left, near_right = from_sides(near_head, near_tail)
+    deep_left = lax.ppermute(edge_tail, ("az", "rad"), across(to_right))
+    deep_right = lax.ppermute(edge_head, ("az", "rad"), across(to_left))
+    far, far_head, far_tail = analyse(second_received, False)
+    far_left, far_right = from_sides(far_head, far_tail)
+
     half_rows, half = local_rows // 2, block // 2
     all_rows = DEEP + local_rows
     coarse_rows = FAR + half_rows
 
-    def field(row_count, cell_count):
-        return jax.ShapeDtypeStruct((row_count, cell_count) + point, f32)
-
-    def scratch(row_count, *cell_count):
-        return pltpu.VMEM((row_count,) + cell_count + point, f32)
-
     s_own, s_head, s_tail, u_two, g_near = pl.pallas_call(
         lambda *refs: smooth_kernel(local_rows, block, *refs),
-        in_specs=[in_smem, in_vmem] + [anywhere] * 5,
+        in_specs=[in_smem, in_vmem] + [anywhere] * 9,
         out_specs=[in_vmem] * 3 + [anywhere] * 2,
         out_shape=[
             field(coarse_rows, half),
@@ -618,15 +669,16 @@
             scratch(all_rows),
             scratch(all_rows),
             scratch(all_rows),
-            pltpu.SemaphoreType.DMA((5,)),
+            pltpu.SemaphoreType.DMA((9,)),
             pltpu.SemaphoreType.DMA((2,)),
         ],
-        compiler_params=params(),
+        compiler_params=params(32),
         name="smooth",
-    )(position, squares, deep, near, far, left, right)
-
-    s_left = lax.ppermute(s_tail, "az", to_right)
-    s_right = lax.ppermute(s_head, "az", to_left)
+    )(
+        position, squares, deep, deep_left, deep_right, near, near_left, near_right, far, far_left, far_right
+    )
+
+    s_left, s_right = from_sides(s_head, s_tail)
 
     solved = pl.pallas_call(
         lambda *refs: correct_kernel(local_rows, block, *refs),
@@ -648,7 +700,7 @@
             scratch(coarse_rows),
             pltpu.SemaphoreType.DMA((5,)),
         ],
-        compiler_params=params(),
+        compiler_params=params(36),
         name="correct",
     )(position, squares, s_own, s_left, s_right, u_two, g_near)
 
@@ -662,27 +714,30 @@
         ],
         out_specs=pl.BlockSpec((az_count, groups, local_phi, LANES), lambda j: (0, j, 0, 0)),
         out_shape=jax.ShapeDtypeStruct((az_count, tiles * groups, local_phi, LANES), f32),
-        compiler_params=params("arbitrary"),
+        compiler_params=params(24, "arbitrary"),
         name="synthesis",
     )(solved, s_high, s_low)
 
     returned = exchange(physical)
+    side = jnp.stack([rad_index, rad_index]).astype(jnp.int32)
     return pl.pallas_call(
-        lambda *refs: unpack_kernel(block, *refs),
-        grid_spec=pltpu.PrefetchScalarGridSpec(
-            num_scalar_prefetch=1,
-            grid=(tiles, vertical_cells // LANES),
-            in_specs=[
-                pl.BlockSpec((rows, groups, local_phi, LANES), lambda j, k, pos: (k, j, 0, 0))
-            ],
-            out_specs=pl.BlockSpec(
-                (local_phi, TILE, LANES), lambda j, k, pos: (0, row_tile(j, pos), k)
-            ),
-        ),
+        lambda *refs: unpack_kernel(block, order, *refs),
+        in_specs=[in_smem, anywhere],
+        out_specs=anywhere,
         out_shape=jax.ShapeDtypeStruct(density.shape, f32),
-        compiler_params=params("arbitrary", "arbitrary"),
+        scratch_shapes=[
+            pltpu.VMEM((az_count, tiles * groups, local_phi, LANES), f32),
+            pltpu.VMEM((tiles, lane_tiles, local_phi, TILE, LANES), f32),
+            pltpu.SemaphoreType.DMA((tiles,)),
+            pltpu.SemaphoreType.DMA((tiles * lane_tiles,)),
+        ],
+        compiler_params=params(12),
         name="unpack",
-    )(position, returned)
+    )(side, returned)
+
+
+def block_order(az_count):
+    return [i ^ 2 if (i // 4) % 2 else i for i in range(az_count)]
 
 
 def fits_cells(density):
@@ -698,7 +753,7 @@
         and block // 2 >= FAR
         and local_rows % (4 * TILE) == 0
         and local_rows // 2 >= DEEP
-        and az_count % 2 == 0
+        and az_count % 4 == 0
         and local_phi % TILE == 0
         and (az_count * local_phi) % (2 * LANES) == 0
         and az_count * local_phi == TILE * LANES

time: 305 us -> 280 us (0.918)
  blocking collectives: 101 us -> 0 us
  waiting for transfers between devices: 98.7 us -> 179 us
  Pallas kernels: 71 us -> 48.5 us
  starting transfers between devices: 24.1 us -> 36.7 us
  local copies, waits for them, and re-layouts: 7.39 us -> 14.2 us
    all_to_all x1 -> x0, blocking collectives: 101 us -> none  [exchange(): return lax.all_to_all(value, 'az', split_axis=0, concat_axis=0, tiled=True)]
    all_to_all x2 -> x3, waiting for transfers between devices: 80 us -> 166 us  [exchange(): return lax.all_to_all(value, 'az', split_axis=0, concat_axis=0, tiled=True)]
    pallas_call x3, Pallas kernels: 27.6 us -> 15.4 us  [the longest x2 8.57 us: pack(): pl.pallas_call(lambda *refs: pack_kernel(block, order, first_tile, *refs)...]
    unnamed x12 -> x24, local copies, waits for them, and re-layouts: 4.25 us -> 14.2 us
    ppermute x4 -> x8, starting transfers between devices: 11.4 us -> 19.3 us  [the longest x3 7 us: from_sides(): lax.ppermute(tail, 'az', to_right)]
    ppermute x4 -> x8, waiting for transfers between devices: 18.7 us -> 13.6 us  [the longest x3 9.1 us: from_sides(): lax.ppermute(head, 'az', to_left)]
    all_to_all x2 -> x3, starting transfers between devices: 11.5 us -> 16.2 us  [exchange(): return lax.all_to_all(value, 'az', split_axis=0, concat_axis=0, tiled=True)]
    pallas_call x2, Pallas kernels: 12.5 us -> 8.94 us  [analyse(): pl.pallas_call(analysis_kernel, grid=(chunk_tiles,), in_specs=[pl.BlockSp...]
  transfers between devices with their start and end apart: 7 -> 12, of which waited for: 6 -> 7; matrix products, arithmetic and copies ran while one was open for 1% -> 0% of each run, Pallas kernels for 7% -> 5%
where the time goes in v2:
time: 280 us; the launch traced here: 279 us
  waiting for transfers between devices  179 us (64%)
  Pallas kernels  48.5 us (17%)
  starting transfers between devices  36.7 us (13%)
  local copies, waits for them, and re-layouts  14.2 us (5%)
    all_to_all x3, waiting for transfers between devices, exchange(): return lax.all_to_all(value, 'az', split_axis=0, concat_axis=0, tiled=True)  166 us
    all_to_all x3, starting transfers between devices, exchange(): return lax.all_to_all(value, 'az', split_axis=0, concat_axis=0, tiled=True)  16.2 us
    unnamed x24, local copies, waits for them, and re-layouts  14.2 us
    pallas_call x1, Pallas kernels, cell_body(): pl.pallas_call(lambda *refs: correct_kernel(local_rows, block, *refs), in...  9.98 us
    ppermute x3, waiting for transfers between devices, from_sides(): lax.ppermute(head, 'az', to_left)  9.1 us
    pallas_call x2, Pallas kernels, analyse(): pl.pallas_call(analysis_kernel, grid=(chunk_tiles,), in_specs=[pl.BlockSp...  8.94 us
    pallas_call x2, Pallas kernels, pack(): pl.pallas_call(lambda *refs: pack_kernel(block, order, first_tile, *refs)...  8.57 us
    pallas_call x1, Pallas kernels, cell_body(): pl.pallas_call(lambda *refs: smooth_kernel(local_rows, block, *refs), in_...  8.21 us
  transfers between devices with their start and end apart: 12, of which 7 were waited for; matrix products, arithmetic and copies ran while one was open for 0% of the time, Pallas kernels for 5%

profile of v2, /device:TPU:11, one launch (start us, length us, event | category | flops | bytes accessed | tf_op | source)
XLA Modules:
  0.0 279.0 jit_solution(16188957508531620224)
XLA Ops:
  0.0 0.1 pad_add_fusion.1.refs_0_
  0.1 2.2 copy-done
  2.3 4.3 %pack.2 = f32[16,4,64,128]{3,2,1,0:T(8,128)} custom-call(s32[3]{0:T(128)S(1)} %pad_add_fusion.1.refs_0_, f32[64,32,512]{2,1,0:T(8,128)S(1)} %copy-done), custom_call_target="tpu_custom_call" | custom-call | tf_op jit(solution)/shard_map/pack/pallas_call | solution.py:575
  6.6 6.6 %all-to-all-start = ((f32[16,4,64,128]{3,2,1,0:T(8,128)}), f32[16,4,64,128]{3,2,1,0:T(8,128)S(1)}, u32[]{:S(2)}, u32[]{:S(2)}) async-start(f32[16,4,64,128]{3,2,1,0:T(8,128)} %pack.2), calls=%async_computation | async-start | bytes 4194304 | tf_op jit(solution)/shard_map/all_to_all | solution.py:623
  13.1 2.2 copy-done.1
  15.3 4.3 %pack.3 = f32[16,4,64,128]{3,2,1,0:T(8,128)} custom-call(s32[3]{0:T(128)S(1)} %pad_add_fusion.1.refs_0_, f32[64,32,512]{2,1,0:T(8,128)S(1)} %copy-done.1), custom_call_target="tpu_custom_call" | custom-call | tf_op jit(solution)/shard_map/pack/pallas_call | solution.py:575
  19.6 40.9 %all-to-all-done.x_ref = f32[16,4,64,128]{3,2,1,0:T(8,128)S(1)} async-done(((f32[16,4,64,128]{3,2,1,0:T(8,128)}), f32[16,4,64,128]{3,2,1,0:T(8,128)S(1)}, u32[]{:S(2)}, u32[]{:S(2)}) %all-to-all-start) | async-done | bytes 2097184 | tf_op jit(solution)/shard_map/all_to_all | solution.py:623
  60.5 1.3 copy-done.3
  61.9 4.9 %all-to-all-start.1 = ((f32[16,4,64,128]{3,2,1,0:T(8,128)}), f32[16,4,64,128]{3,2,1,0:T(8,128)}, u32[]{:S(2)}, u32[]{:S(2)}) async-start(f32[16,4,64,128]{3,2,1,0:T(8,128)} %pack.3), calls=%async_computation.1 | async-start | bytes 4194304 | tf_op jit(solution)/shard_map/all_to_all | solution.py:623
  66.8 1.6 copy-done.4
  68.4 1.2 copy-done.8
  69.6 1.2 copy-done.10
  70.8 4.6 %analysis.2 = (f32[16,32,8,128]{3,2,1,0:T(8,128)S(1)}, f32[16,3,8,128]{3,2,1,0:T(8,128)S(1)}, f32[16,3,8,128]{3,2,1,0:T(8,128)S(1)}, f32[14,32,8,128]{3,2,1,0:T(...) custom-call(f32[16,4,64,128]{3,2,1,0:T(8,128)S(1)} %copy-done.4, bf16[512,1024]{1,0:T(8,128)(2,1)S(1)} %copy-done.10, ...), custom_call_target="tpu_custom_call" | custom-call | flops 1610612736 | bytes 6291456 | tf_op jit(solution)/shard_map/analysis/pallas_call | solution.py:605
  75.4 1.2 collective-permute-start
  76.7 2.7 collective-permute-start.1
  79.3 0.0 copy-start.7
  79.4 2.9 %collective-permute-start.2 = (f32[14,3,8,128]{3,2,1,0:T(8,128)S(1)}, f32[14,3,8,128]{3,2,1,0:T(8,128)S(1)}, u32[]{:S(2)}, u32[]{:S(2)}) collective-permute-start(f32[14,3,8,128]{3,2,1,0:T(8,128)S(1)} %get-tuple-element.21), channel_id=1, source_target_pairs={{2,1},{3,0},{4,3},{5,2},{6,5},{7,4},{12,7},{13,6},{14,13},{15,12},... | collective-permute-start | bytes 516104 | tf_op jit(solution)/shard_map/ppermute | solution.py:646
  82.3 32.3 %all-to-all-done.1.x_ref = f32[16,4,64,128]{3,2,1,0:T(8,128)} async-done(((f32[16,4,64,128]{3,2,1,0:T(8,128)}), f32[16,4,64,128]{3,2,1,0:T(8,128)}, u32[]{:S(2)}, u32[]{:S(2)}) %all-to-all-start.1) | async-done | bytes 2097184 | tf_op jit(solution)/shard_map/all_to_all | solution.py:623
  114.6 1.2 copy-done.9
  115.8 1.2 copy-done.11
  117.0 4.3 %analysis.3 = (f32[16,32,8,128]{3,2,1,0:T(8,128)S(1)}, f32[16,3,8,128]{3,2,1,0:T(8,128)S(1)}, f32[16,3,8,128]{3,2,1,0:T(8,128)S(1)}) custom-call(f32[16,4,64,128]{3,2,1,0:T(8,128)} %all-to-all-done.1.x_ref, bf16[512,1024]{1,0:T(8,128)(2,1)S(1)} %copy-done.11, bf16[512,1024]{1,0:T(8,128)(2,1)S(1)} %copy-done.9), custom_call_target="tpu_custom_call" | custom-call | flops 1610612736 | bytes 6291456 | tf_op jit(solution)/shard_map/analysis/pallas_call | solution.py:605
  121.4 1.9 collective-permute-start.5
  123.3 2.4 collective-permute-start.6
  125.7 0.0 collective-permute-done.1.refs_3_
  125.7 3.2 %collective-permute-start.3 = (f32[16,3,8,128]{3,2,1,0:T(8,128)S(1)}, f32[16,3,8,128]{3,2,1,0:T(8,128)S(1)}, u32[]{:S(2)}, u32[]{:S(2)}) collective-permute-start(f32[16,3,8,128]{3,2,1,0:T(8,128)S(1)} %get-tuple-element.23), channel_id=1, source_target_pairs={{0,2},{2,4},{4,6},{6,12},{12,14},{14,8},{8,10},{10,16},{16,18},{18... | collective-permute-start | bytes 589832 | tf_op jit(solution)/shard_map/ppermute | solution.py:629
  128.9 0.0 collective-permute-done.2.refs_4_
  128.9 1.9 collective-permute-start.4
  130.8 0.0 collective-permute-done.5.refs_9_
  130.8 0.0 collective-permute-done.6.refs_10_
  130.9 0.6 collective-permute-done.3.refs_6_
  131.5 4.4 %collective-permute-done.4.refs_7_ = f32[16,3,8,128]{3,2,1,0:T(8,128)S(1)} collective-permute-done((f32[16,3,8,128]{3,2,1,0:T(8,128)S(1)}, f32[16,3,8,128]{3,2,1,0:T(8,128)S(1)}, u32[]{:S(2)}, u32[]{:S(2)}) %collective-permute-start.4) | collective-permute-done | bytes 196640 | tf_op jit(solution)/shard_map/ppermute | solution.py:629
  135.9 0.0 collective-permute-done.refs_2_
  135.9 0.0 copy-done.7
  135.9 8.2 %smooth.1 = (f32[22,16,8,128]{3,2,1,0:T(8,128)S(1)}, f32[22,6,8,128]{3,2,1,0:T(8,128)S(1)}, f32[22,6,8,128]{3,2,1,0:T(8,128)S(1)}, f32[34,36,8,128]{3,2,1,0:T(8,128)S(1)}, f32[33,34,8,128]{3,2,1,0:T(8,128)S(1)}) custom-call(s32[3]{0:T(128)S(1)} %pad_add_fusion.1.refs_0_, f32[8,128]{1,0:T(8,128)S(1)} %copy-done.7, ...), custom_call_target="tpu_custom_call" | custom-call | tf_op jit(solution)/shard_map/smooth/pallas_call | solution.py:654
  144.1 1.9 collective-permute-start.7
  146.1 2.4 collective-permute-start.8
  148.5 3.9 %collective-permute-done.7.refs_3_ = f32[22,6,8,128]{3,2,1,0:T(8,128)S(1)} collective-permute-done((f32[22,6,8,128]{3,2,1,0:T(8,128)S(1)}, f32[22,6,8,128]{3,2,1,0:T(8,128)S(1)}, u32[]{:S(2)}, u32[]{:S(2)}) %collective-permute-start.7) | collective-permute-done | bytes 540704 | tf_op jit(solution)/shard_map/ppermute | solution.py:629
  152.3 4.7 %collective-permute-done.8.refs_4_ = f32[22,6,8,128]{3,2,1,0:T(8,128)S(1)} collective-permute-done((f32[22,6,8,128]{3,2,1,0:T(8,128)S(1)}, f32[22,6,8,128]{3,2,1,0:T(8,128)S(1)}, u32[]{:S(2)}, u32[]{:S(2)}) %collective-permute-start.8) | collective-permute-done | bytes 540704 | tf_op jit(solution)/shard_map/ppermute | solution.py:629
  157.0 10.0 %correct.1.u_ref = f32[32,32,8,128]{3,2,1,0:T(8,128)S(1)} custom-call(s32[3]{0:T(128)S(1)} %pad_add_fusion.1.refs_0_, f32[8,128]{1,0:T(8,128)S(1)} %copy-done.7, f32[22,16,8,128]{3,2,1,0:T(8,128)S(1)} %get-tuple-element.28.refs_2_, f32[22,6,8,128]{3,2,1,0:T(8,128)S(1)} %collective-permute-done.7.refs_3_, ...), custom_call_target="tpu_custom_call" | custom-call | tf_op jit(solution)/shard_map/correct/pallas_call | solution.py:683
  167.0 0.0 copy-done.5
  167.0 0.0 copy-done.6
  167.0 6.0 %synthesis.1 = f32[16,8,64,128]{3,2,1,0:T(8,128)S(1)} custom-call(f32[32,32,8,128]{3,2,1,0:T(8,128)S(1)} %correct.1.u_ref, bf16[512,1024]{1,0:T(8,128)(2,1)S(1)} %copy-done.6, bf16[512,1024]{1,0:T(8,128)(2,1)S(1)} %copy-done.5), custom_call_target="tpu_custom_call" | custom-call | tf_op jit(solution)/shard_map/synthesis/pallas_call | solution.py:707
  173.0 0.0 copy-start.2
  173.0 2.0 copy-done.2
  175.0 4.7 %all-to-all-start.2 = ((f32[16,8,64,128]{3,2,1,0:T(8,128)}), f32[16,8,64,128]{3,2,1,0:T(8,128)}, u32[]{:S(2)}, u32[]{:S(2)}) async-start(f32[16,8,64,128]{3,2,1,0:T(8,128)} %copy-done.2), calls=%async_computation.2 | async-start | bytes 8388608 | tf_op jit(solution)/shard_map/all_to_all | solution.py:623
  179.7 0.1 pad_add_fusion.refs_0_
  179.8 92.4 %all-to-all-done.2.refs_1_ = f32[16,8,64,128]{3,2,1,0:T(8,128)} async-done(((f32[16,8,64,128]{3,2,1,0:T(8,128)}), f32[16,8,64,128]{3,2,1,0:T(8,128)}, u32[]{:S(2)}, u32[]{:S(2)}) %all-to-all-start.2) | async-done | bytes 4194336 | tf_op jit(solution)/shard_map/all_to_all | solution.py:623
  272.2 6.8 %unpack.1 = f32[64,32,512]{2,1,0:T(8,128)} custom-call(s32[2]{0:T(128)S(1)} %pad_add_fusion.refs_0_, f32[16,8,64,128]{3,2,1,0:T(8,128)} %all-to-all-done.2.refs_1_), custom_call_target="tpu_custom_call" | custom-call | tf_op jit(solution)/shard_map/unpack/pallas_call | solution.py:723
  (10 shorter events, 0.0 us)
Async XLA Ops:
  0.1 2.2 copy-start
  6.6 54.0 %all-to-all-start = ((f32[16,4,64,128]{3,2,1,0:T(8,128)}), f32[16,4,64,128]{3,2,1,0:T(8,128)S(1)}, u32[]{:S(2)}, u32[]{:S(2)}) async-start(f32[16,4,64,128]{3,2,1,0:T(8,128)} %pack.2), calls=%async_computation | async-start | bytes 4194304 | tf_op jit(solution)/shard_map/all_to_all | solution.py:623
  13.1 2.2 copy-start.1
  60.5 1.3 copy-start.3
  61.9 52.7 %all-to-all-start.1 = ((f32[16,4,64,128]{3,2,1,0:T(8,128)}), f32[16,4,64,128]{3,2,1,0:T(8,128)}, u32[]{:S(2)}, u32[]{:S(2)}) async-start(f32[16,4,64,128]{3,2,1,0:T(8,128)} %pack.3), calls=%async_computation.1 | async-start | bytes 4194304 | tf_op jit(solution)/shard_map/all_to_all | solution.py:623
  66.8 1.6 copy-start.4
  68.4 1.2 copy-start.8
  69.6 1.2 copy-start.10
  75.4 60.5 %collective-permute-start = (f32[14,32,8,128]{3,2,1,0:T(8,128)}, f32[14,32,8,128]{3,2,1,0:T(8,128)}, u32[]{:S(2)}, u32[]{:S(2)}) collective-permute-start(f32[14,32,8,128]{3,2,1,0:T(8,128)} %get-tuple-element.19), channel_id=1, source_target_pairs={{0,1},{1,0},{2,3},{3,2},{4,5},{5,4},{6,7},{7,6},{8,9},{9,8},{10,11... | collective-permute-start | bytes 5505032 | tf_op jit(solution)/shard_map/ppermute | solution.py:643
  76.7 49.1 %collective-permute-start.1 = (f32[14,3,8,128]{3,2,1,0:T(8,128)S(1)}, f32[14,3,8,128]{3,2,1,0:T(8,128)S(1)}, u32[]{:S(2)}, u32[]{:S(2)}) collective-permute-start(f32[14,3,8,128]{3,2,1,0:T(8,128)S(1)} %get-tuple-element.20), channel_id=1, source_target_pairs={{0,3},{1,2},{2,5},{3,4},{4,7},{5,6},{6,13},{7,12},{12,15},{13,14},... | collective-permute-start | bytes 516104 | tf_op jit(solution)/shard_map/ppermute | solution.py:645
  79.3 56.6 %copy-start.7 = (f32[8,128]{1,0:T(8,128)S(1)}, f32[8,128]{1,0:T(8,128)}, u32[]{:S(2)}) copy-start(f32[8,128]{1,0:T(8,128)} %constant.47.clone.refs_1_) | copy-start | bytes 12292
  79.4 49.6 %collective-permute-start.2 = (f32[14,3,8,128]{3,2,1,0:T(8,128)S(1)}, f32[14,3,8,128]{3,2,1,0:T(8,128)S(1)}, u32[]{:S(2)}, u32[]{:S(2)}) collective-permute-start(f32[14,3,8,128]{3,2,1,0:T(8,128)S(1)} %get-tuple-element.21), channel_id=1, source_target_pairs={{2,1},{3,0},{4,3},{5,2},{6,5},{7,4},{12,7},{13,6},{14,13},{15,12},... | collective-permute-start | bytes 516104 | tf_op jit(solution)/shard_map/ppermute | solution.py:646
  114.6 1.2 copy-start.9
  115.8 1.2 copy-start.11
  121.4 9.5 %collective-permute-start.5 = (f32[16,3,8,128]{3,2,1,0:T(8,128)S(1)}, f32[16,3,8,128]{3,2,1,0:T(8,128)S(1)}, u32[]{:S(2)}, u32[]{:S(2)}) collective-permute-start(f32[16,3,8,128]{3,2,1,0:T(8,128)S(1)} %get-tuple-element.26), channel_id=1, source_target_pairs={{0,2},{2,4},{4,6},{6,12},{12,14},{14,8},{8,10},{10,16},{16,18},{18... | collective-permute-start | bytes 589832 | tf_op jit(solution)/shard_map/ppermute | solution.py:629
  123.3 7.5 %collective-permute-start.6 = (f32[16,3,8,128]{3,2,1,0:T(8,128)S(1)}, f32[16,3,8,128]{3,2,1,0:T(8,128)S(1)}, u32[]{:S(2)}, u32[]{:S(2)}) collective-permute-start(f32[16,3,8,128]{3,2,1,0:T(8,128)S(1)} %get-tuple-element.27), channel_id=1, source_target_pairs={{2,0},{4,2},{6,4},{12,6},{14,12},{8,14},{10,8},{16,10},{18,16},{20... | collective-permute-start | bytes 589832 | tf_op jit(solution)/shard_map/ppermute | solution.py:629
  125.7 5.8 %collective-permute-start.3 = (f32[16,3,8,128]{3,2,1,0:T(8,128)S(1)}, f32[16,3,8,128]{3,2,1,0:T(8,128)S(1)}, u32[]{:S(2)}, u32[]{:S(2)}) collective-permute-start(f32[16,3,8,128]{3,2,1,0:T(8,128)S(1)} %get-tuple-element.23), channel_id=1, source_target_pairs={{0,2},{2,4},{4,6},{6,12},{12,14},{14,8},{8,10},{10,16},{16,18},{18... | collective-permute-start | bytes 589832 | tf_op jit(solution)/shard_map/ppermute | solution.py:629
  128.9 7.0 %collective-permute-start.4 = (f32[16,3,8,128]{3,2,1,0:T(8,128)S(1)}, f32[16,3,8,128]{3,2,1,0:T(8,128)S(1)}, u32[]{:S(2)}, u32[]{:S(2)}) collective-permute-start(f32[16,3,8,128]{3,2,1,0:T(8,128)S(1)} %get-tuple-element.24), channel_id=1, source_target_pairs={{2,0},{4,2},{6,4},{12,6},{14,12},{8,14},{10,8},{16,10},{18,16},{20... | collective-permute-start | bytes 589832 | tf_op jit(solution)/shard_map/ppermute | solution.py:629
  144.1 8.2 %collective-permute-start.7 = (f32[22,6,8,128]{3,2,1,0:T(8,128)S(1)}, f32[22,6,8,128]{3,2,1,0:T(8,128)S(1)}, u32[]{:S(2)}, u32[]{:S(2)}) collective-permute-start(f32[22,6,8,128]{3,2,1,0:T(8,128)S(1)} %get-tuple-element.29), channel_id=1, source_target_pairs={{0,2},{2,4},{4,6},{6,12},{12,14},{14,8},{8,10},{10,16},{16,18},{18... | collective-permute-start | bytes 1622024 | tf_op jit(solution)/shard_map/ppermute | solution.py:629
  146.1 11.0 %collective-permute-start.8 = (f32[22,6,8,128]{3,2,1,0:T(8,128)S(1)}, f32[22,6,8,128]{3,2,1,0:T(8,128)S(1)}, u32[]{:S(2)}, u32[]{:S(2)}) collective-permute-start(f32[22,6,8,128]{3,2,1,0:T(8,128)S(1)} %get-tuple-element.30), channel_id=1, source_target_pairs={{2,0},{4,2},{6,4},{12,6},{14,12},{8,14},{10,8},{16,10},{18,16},{20... | collective-permute-start | bytes 1622024 | tf_op jit(solution)/shard_map/ppermute | solution.py:629
  157.0 10.0 %copy-start.5 = (bf16[512,1024]{1,0:T(8,128)(2,1)S(1)}, bf16[512,1024]{1,0:T(8,128)(2,1)}, u32[]{:S(2)}) copy-start(bf16[512,1024]{1,0:T(8,128)(2,1)} %constant.51.clone.low_ref) | copy-start | bytes 3145732
  157.0 10.0 %copy-start.6 = (bf16[512,1024]{1,0:T(8,128)(2,1)S(1)}, bf16[512,1024]{1,0:T(8,128)(2,1)}, u32[]{:S(2)}) copy-start(bf16[512,1024]{1,0:T(8,128)(2,1)} %constant.50.clone.high_ref) | copy-start | bytes 3145732
  173.0 2.0 copy-start.2
  175.0 97.2 %all-to-all-start.2 = ((f32[16,8,64,128]{3,2,1,0:T(8,128)}), f32[16,8,64,128]{3,2,1,0:T(8,128)}, u32[]{:S(2)}, u32[]{:S(2)}) async-start(f32[16,8,64,128]{3,2,1,0:T(8,128)} %copy-done.2), calls=%async_computation.2 | async-start | bytes 8388608 | tf_op jit(solution)/shard_map/all_to_all | solution.py:623

commit v3 on v0

--- a/solution.py
+++ b/solution.py
@@ -2,14 +2,24 @@
 
 import jax
 import jax.numpy as jnp
+import numpy as np
 from jax import lax
+from jax.experimental import pallas as pl
+from jax.experimental.pallas import tpu as pltpu
 from jax.sharding import PartitionSpec as P
 
+PRE = 2
 POST = 2
 COARSE = 6
 
 
 OMEGA = 0.8
+
+LANES = 128
+TILE = 8
+DEEP = 2 * COARSE + 2
+NEAR = 3
+FAR = COARSE
 
 
 def with_halo(cells, sides, width):
@@ -70,12 +80,7 @@
     return jnp.repeat(jnp.repeat(correction, 2, axis=1), 2, axis=2)
 
 
-def pad_fine(field):
-    rows = with_halo(field, (("rad", 1),), 1)
-    return jnp.pad(rows, ((0, 0), (0, 0), (1, 1)))
-
-
-def pad_coarse(field):
+def pad_level(field):
     rows = with_halo(field, (("rad", 1),), 1)
     return jnp.pad(rows, ((0, 0), (0, 0), (1, 1)))
 
@@ -88,7 +93,8 @@
 
 def fine_cycle(source, fine_coef, pad_sweep, coarse_solve):
     iterate = OMEGA * source / fine_coef[0]
-    iterate = relax(iterate, source, fine_coef, pad_sweep)
+    for sweep_index in range(PRE - 1):
+        iterate = relax(iterate, source, fine_coef, pad_sweep)
     residual = source - apply_op(iterate, pad_sweep(iterate), fine_coef)
     iterate = iterate + prolong(coarse_solve(restrict(residual)))
     for sweep_index in range(POST):
@@ -96,7 +102,7 @@
     return iterate
 
 
-def body(density):
+def general_body(density):
     local_phi, local_rows, vertical_cells = density.shape
     az_count = lax.axis_size("az")
     azimuths = local_phi * az_count
@@ -137,16 +143,760 @@
     def coarse_halo(coarse_source):
         correction = OMEGA * coarse_source / coarse_coef[0]
         for sweep_index in range(COARSE - 1):
-            correction = relax(correction, coarse_source, coarse_coef, pad_coarse)
+            correction = relax(correction, coarse_source, coarse_coef, pad_level)
         return correction
 
-    iterate = fine_cycle(source, fine_coef, pad_fine, coarse_halo)
+    iterate = fine_cycle(source, fine_coef, pad_level, coarse_halo)
     mode_lines = iterate.reshape(local_phi, az_count, cell_count)
     physical = transform_with(
         synthesis_table, lax.all_to_all(mode_lines, "az", split_axis=1, concat_axis=0, tiled=True)
     )
     field = lax.all_to_all(physical, "az", split_axis=0, concat_axis=1, tiled=True)
     return field.reshape(local_phi, local_rows, vertical_cells)
+
+
+def mode_tables(azimuths):
+    half = azimuths // 2
+    even = np.concatenate([np.arange(0, half + 1, 2), np.arange(2, half, 2)])
+    odd = np.concatenate([np.arange(1, half, 2), np.arange(1, half, 2)])
+    even_cos = np.arange(half) <= half // 2
+    odd_cos = np.arange(half) < half // 2
+    modes = np.concatenate([even, odd])
+    is_cos = np.concatenate([even_cos, odd_cos])
+    angle = 2.0 * np.pi / azimuths * (np.arange(half)[:, None] * modes[None, :] % azimuths)
+    values = np.where(is_cos[None, :], np.cos(angle), np.sin(angle))
+    weight = np.where((modes == 0) | (modes == half), 1.0, 2.0) / azimuths
+    return -values, values * weight[None, :]
+
+
+def high_low(values):
+    values = values.astype(np.float32)
+    high = values.astype(jnp.bfloat16)
+    low = (values - high.astype(np.float32)).astype(jnp.bfloat16)
+    return jnp.asarray(high), jnp.asarray(low)
+
+
+def split_value(value):
+    high = value.astype(jnp.bfloat16)
+    return high, (value - high.astype(jnp.float32)).astype(jnp.bfloat16)
+
+
+def place():
+    az = lax.axis_index("az")
+    return lax.axis_index("rad"), az ^ (((az >> 2) & 1) << 1), lax.axis_size("az")
+
+
+def mode_squares(shape):
+    half = shape[0] * shape[1] // 2
+    index = lax.broadcasted_iota(jnp.int32, shape, 0) * shape[1] + lax.broadcasted_iota(jnp.int32, shape, 1)
+    even = 2 * jnp.where(index <= half // 2, index, index - half // 2)
+    odd = 2 * (index & (half // 2 - 1)) + 1
+    modes = jnp.where(index < half, even, odd)
+    return (modes * modes).astype(jnp.float32)
+
+
+def row_tile(position, local_rows, tile):
+    return jnp.where(position[0] == 0, local_rows // TILE - 1 - tile, tile)
+
+
+def chunk_masks(count, shape):
+    lane = lax.broadcasted_iota(jnp.int32, shape, len(shape) - 1) // (LANES // count)
+    return [lane == p for p in range(1, count)]
+
+
+def pick_chunks(parts, masks):
+    result = parts[0]
+    for part, mask in zip(parts[1:], masks):
+        result = jnp.where(mask, part, result)
+    return result
+
+
+def gather_rows(parts, masks):
+    count = len(parts)
+    chunk = LANES // count
+    turned = [pltpu.roll(part, i * chunk, 1) if i else part for i, part in enumerate(parts)]
+    return [pick_chunks([turned[(p - q) % count] for p in range(count)], masks) for q in range(count)]
+
+
+def scatter_rows(parts, masks):
+    count = len(parts)
+    chunk = LANES // count
+    rows = [pick_chunks([parts[(p - i) % count] for p in range(count)], masks) for i in range(count)]
+    return [pltpu.roll(row, LANES - i * chunk, 1) if i else row for i, row in enumerate(rows)]
+
+
+def turned_row(row, turn, rows):
+    low = row & (rows - 1)
+    return row - low + ((low + turn) & (rows - 1))
+
+
+def tile_row(position, row):
+    return jnp.where(position[0] == 0, TILE - 1 - row, row)
+
+
+def pack_kernel(block, order, first_tile, x_ref, o_ref, x, o, in_sems, out_sems):
+    position = place()
+    rows = LANES // block
+    local_phi, local_rows, cells = x_ref.shape
+    tiles, lane_tiles, groups = x.shape[0], x.shape[1], TILE // rows
+    pieces = [(j, k) for j in range(tiles) for k in range(lane_tiles)]
+    masks = chunk_masks(rows, (local_phi, LANES))
+    loads, stores = [], []
+    for n, (j, k) in enumerate(pieces):
+        start = pl.multiple_of(row_tile(position, local_rows, first_tile + j) * TILE, TILE)
+        source = x_ref.at[:, pl.ds(start, TILE), k * LANES : (k + 1) * LANES]
+        loads.append(pltpu.make_async_copy(source, x.at[j, k], in_sems.at[n]))
+        loads[-1].start()
+    for n, (j, k) in enumerate(pieces):
+        loads[n].wait()
+        flat = x.at[j, k].reshape(local_phi * TILE, LANES)
+        for group in range(groups):
+            parts = [
+                flat[pl.ds(tile_row(position, group * rows + i), local_phi, stride=TILE), :]
+                for i in range(rows)
+            ]
+            for q, part in enumerate(gather_rows(parts, masks)):
+                o[order[k * rows + q], j * groups + group] = part
+        if k == lane_tiles - 1:
+            span = slice(j * groups, (j + 1) * groups)
+            stores.append(pltpu.make_async_copy(o.at[:, span], o_ref.at[:, span], out_sems.at[j]))
+            stores[-1].start()
+    for store in stores:
+        store.wait()
+
+
+def unpack_kernel(block, order, x_ref, _, o_ref, x, o, in_sems, out_sems):
+    position = place()
+    rows = LANES // block
+    local_phi, local_rows, cells = o_ref.shape
+    tiles, lane_tiles, groups = o.shape[0], o.shape[1], TILE // rows
+    masks = chunk_masks(rows, (local_phi, LANES))
+    loads, stores = [], []
+    for j in range(tiles):
+        span = slice(j * groups, (j + 1) * groups)
+        loads.append(pltpu.make_async_copy(x_ref.at[:, span], x.at[:, span], in_sems.at[j]))
+        loads[-1].start()
+    for j in range(tiles):
+        loads[j].wait()
+        start = pl.multiple_of(row_tile(position, local_rows, j) * TILE, TILE)
+        for k in range(lane_tiles):
+            flat = o.at[j, k].reshape(local_phi * TILE, LANES)
+            for group in range(groups):
+                parts = [x[order[k * rows + q], j * groups + group] for q in range(rows)]
+                for i, part in enumerate(scatter_rows(parts, masks)):
+                    at = tile_row(position, group * rows + i)
+                    flat[pl.ds(at, local_phi, stride=TILE), :] = part
+            target = o_ref.at[:, pl.ds(start, TILE), k * LANES : (k + 1) * LANES]
+            stores.append(
+                pltpu.make_async_copy(o.at[j, k], target, out_sems.at[j * lane_tiles + k])
+            )
+            stores[-1].start()
+    for store in stores:
+        store.wait()
+
+
+def started(pairs, sems, first=0):
+    copies = []
+    for n, (src, dst) in enumerate(pairs):
+        copies.append(pltpu.make_async_copy(src, dst, sems.at[first + n]))
+        copies[-1].start()
+    return copies
+
+
+def finished(copies):
+    for copy in copies:
+        copy.wait()
+
+
+def sides_of(field, depth):
+    cells = field.shape[1]
+    return field, field.at[:, :depth], field.at[:, cells - depth : cells]
+
+
+def analysis_kernel(tile_groups, *refs):
+    position = place()
+    x_ref, high_ref, low_ref = refs[:3]
+    outs = refs[3:-8]
+    x, t_high, t_low, o, edge, in_sems, t_sems, out_sems = refs[-8:]
+    if len(outs) == 2:
+        held_refs = ()
+    else:
+        held_refs, outs = outs[:2], outs[2:]
+    sources, width, lanes = x.shape[0], x.shape[2], x.shape[3]
+    cells = o.shape[1]
+    half = sources // 2 * width
+    tiles = x.shape[1] // tile_groups
+    spans = [slice(n * tile_groups, (n + 1) * tile_groups) for n in range(tiles)]
+    pairs = [(x_ref.at[:, span], x.at[:, span]) for span in spans]
+    tables = started([(high_ref, t_high), (low_ref, t_low)], t_sems)
+    loads = started(pairs, in_sems)
+    group_rows = TILE // tile_groups
+    turn = position[1] & (group_rows - 1)
+    gathers, start = [], 0
+    for held in held_refs:
+        span = slice(start, start + held.shape[0])
+        sides = zip(sides_of(held, NEAR)[1:], (slice(0, NEAR), slice(NEAR, 2 * NEAR)))
+        pairs = [(side, edge.at[span, columns]) for side, columns in sides]
+        gathers += started(pairs, out_sems, out_sems.shape[0] - 4 + len(gathers))
+        start += held.shape[0]
+    stores = []
+    for n in range(tiles):
+        loads[n].wait()
+        parts = []
+        for parity in range(2):
+            turned = []
+            for group in range(n * tile_groups, (n + 1) * tile_groups):
+                near, far = x[: sources // 2, group], x[sources // 2 :, group]
+                folded = near + far if parity == 0 else near - far
+                turned.append(folded.reshape(half, lanes).T)
+            parts.append(split_value(jnp.concatenate(turned, axis=0)))
+        if n == 0:
+            finished(tables)
+        rows = slice(n * TILE, (n + 1) * TILE)
+        for parity, (high, low) in enumerate(parts):
+            columns = slice(parity * half, (parity + 1) * half)
+            result = (
+                jnp.dot(high, t_high[:, columns], preferred_element_type=jnp.float32)
+                + jnp.dot(high, t_low[:, columns], preferred_element_type=jnp.float32)
+                + jnp.dot(low, t_high[:, columns], preferred_element_type=jnp.float32)
+            )
+            for part in range(half // LANES):
+                piece = result[:, part * LANES : (part + 1) * LANES]
+                o[rows, :, parity * (half // LANES) + part, :] = piece.reshape(TILE, cells, LANES)
+        pairs = [
+            (o.at[turned_row(row, turn, group_rows)], outs[0].at[row])
+            for row in range(n * TILE, (n + 1) * TILE)
+        ]
+        stores += started(pairs, out_sems, len(stores))
+    if held_refs:
+        finished(gathers)
+        for row in range(o.shape[0]):
+            at = turned_row(row, turn, group_rows)
+            edge[start + row, :NEAR] = o[at, :NEAR]
+            edge[start + row, NEAR:] = o[at, cells - NEAR :]
+        pairs = [(edge.at[:, :NEAR], outs[1]), (edge.at[:, NEAR:], outs[2])]
+        stores += started(pairs, out_sems, len(stores))
+    else:
+        for row in range(DEEP):
+            edge[DEEP - 1 - row] = o[turned_row(row, turn, group_rows)]
+        stores += started([(edge, outs[1])], out_sems, len(stores))
+    finished(stores)
+
+
+def synthesis_tile(u, t_high, t_low, o):
+    rows, cells = u.shape[0], u.shape[1]
+    half = t_high.shape[0]
+    parts = half // LANES
+    sums = []
+    for parity in range(2):
+        field = jnp.concatenate(
+            [u[:, :, parity * parts + i, :].reshape(rows * cells, LANES) for i in range(parts)],
+            axis=1,
+        )
+        high, low = split_value(field)
+        columns = slice(parity * half, (parity + 1) * half)
+        contract = (((1,), (1,)), ((), ()))
+        sums.append(
+            lax.dot_general(t_high[:, columns], high, contract, preferred_element_type=jnp.float32)
+            + lax.dot_general(t_high[:, columns], low, contract, preferred_element_type=jnp.float32)
+            + lax.dot_general(t_low[:, columns], high, contract, preferred_element_type=jnp.float32)
+        )
+    near, far = sums[0] + sums[1], sums[0] - sums[1]
+    targets, groups, width, lanes = o.shape
+    for group in range(groups):
+        columns = slice(group * lanes, (group + 1) * lanes)
+        o[: targets // 2, group] = near[:, columns].reshape(targets // 2, width, lanes)
+        o[targets // 2 :, group] = far[:, columns].reshape(targets // 2, width, lanes)
+
+
+def row_weights(upper, boundary, first, count, squares, c_ref, ahead_ref, behind_ref):
+    def one(index, carry):
+        row = jnp.where(upper, index + (boundary + first), (boundary - 1 - first) - index)
+        number = jnp.full(squares.shape, row, jnp.int32).astype(jnp.float32)
+        radius = number + 0.5
+        outward = (number + 1.0) / radius
+        inward = number / radius
+        diagonal = outward + inward + 2.0 + squares / (radius * radius)
+        c_ref[index] = OMEGA / diagonal
+        ahead_ref[index] = jnp.where(upper, outward, inward)
+        behind_ref[index] = jnp.where(upper, inward, outward)
+        return carry
+
+    lax.fori_loop(0, count, one, 0)
+
+
+def cell_tiles(first, last, cells, size=16):
+    tiles = []
+    if first < 0:
+        tiles.append((first, -first, -1))
+    for start in range(max(first, 0), min(last, cells), size):
+        tiles.append((start, min(size, min(last, cells) - start), 0))
+    if last > cells:
+        tiles.append((cells, last - cells, 1))
+    return tiles
+
+
+def sweep(rows, cells, block, src, source, dst, weights, masks, turn=None):
+    (src_ref, src_t, src_z), (dst_ref, dst_t, dst_z) = src, dst
+    keep = 1.0 - OMEGA if source else 2.0 - OMEGA
+    c_ref, ahead_ref, behind_ref, w_t = weights
+    low = rows[0]
+
+    def one(step, carry):
+        at = step + (low - w_t)
+        target = step + (low - dst_t)
+        if turn:
+            target = turned_row(target, *turn)
+        c_row, ahead, behind = c_ref[at], ahead_ref[at], behind_ref[at]
+        for first, count, side in cell_tiles(cells[0], cells[1], block):
+            c = c_row if side == 0 else c_row * masks[0 if side < 0 else 1]
+            z = first - src_z
+            row = low - src_t
+            middle = src_ref[step + row, z - 1 : z + count + 1]
+            gathered = (
+                ahead * src_ref[step + (row + 1), z : z + count]
+                + behind * src_ref[step + (row - 1), z : z + count]
+                + (middle[:-2] + middle[2:])
+            )
+            if source:
+                g_ref, g_t, g_z = source
+                gathered += g_ref[step + (low - g_t), first - g_z : first - g_z + count]
+            dst_ref[target, first - dst_z : first - dst_z + count] = (
+                keep * middle[1:-1] + c * gathered
+            )
+        return carry
+
+    lax.fori_loop(0, rows[1] - low, one, 0)
+
+
+def first_sweep(rows, cells, block, source, dst, weights, masks):
+    (g_ref, g_t, g_z), (dst_ref, dst_t, dst_z) = source, dst
+    c_ref, w_t = weights[0], weights[3]
+    low = rows[0]
+
+    def one(step, carry):
+        c_row = c_ref[step + (low - w_t)]
+        for first, count, side in cell_tiles(cells[0], cells[1], block):
+            c = c_row if side == 0 else c_row * masks[0 if side < 0 else 1]
+            dst_ref[step + (low - dst_t), first - dst_z : first - dst_z + count] = (
+                c * g_ref[step + (low - g_t), first - g_z : first - g_z + count]
+            )
+        return carry
+
+    lax.fori_loop(0, rows[1] - low, one, 0)
+
+
+def side_masks(position, shape):
+    left = jnp.full(shape, position[1] > 0).astype(jnp.float32)
+    right = jnp.full(shape, position[1] < position[2] - 1).astype(jnp.float32)
+    return left, right
+
+
+def smooth_columns(local_rows, block, cells, g, u1, u2, s, weights, masks):
+    first = -DEEP
+    low, high = cells
+    c_ref, ahead_ref, behind_ref, _ = weights
+    g_at, u1_at, u2_at = (g, first, low), (u1, first, low), (u2, first + 1, low + 1)
+    total = g.shape[0]
+    u1[total] = jnp.zeros(u1.shape[1:], jnp.float32)
+    u2[total - 1] = jnp.zeros(u2.shape[1:], jnp.float32)
+    first_sweep((first, local_rows), cells, block, g_at, u1_at, weights, masks)
+    sweep(
+        (first + 1, local_rows), (low + 1, high - 1), block, u1_at, None, u2_at, weights, masks
+    )
+    start = max(low + 2, 0)
+    start += start % 2
+
+    def paired(values):
+        pairs = values.reshape(values.shape[0] // 2, 2, *values.shape[1:])
+        return pairs[:, 0], pairs[:, 1]
+
+    def pair_sums(values):
+        even, odd = paired(values)
+        return even + odd
+
+    def restrict_row(index, carry):
+        row = 2 * index + (DEEP - 2 * FAR)
+        center = behind_ref[row + 1] - OMEGA / c_ref[row] + 1.0
+        center_ahead = ahead_ref[row] - OMEGA / c_ref[row + 1] + 1.0
+        behind, ahead = behind_ref[row], ahead_ref[row + 1]
+        for at, count, _ in cell_tiles(start, start + 2 * s.shape[1], block):
+            z = at - u2_at[2]
+            here = u2[row - 1, z - 1 : z + count + 1]
+            there = u2[row, z - 1 : z + count + 1]
+            even, odd = paired(here + there)
+            cells = slice(at - low, at - low + count)
+            column = (at - start) // 2
+            s[index, column : column + count // 2] = (
+                pair_sums(g[row, cells] + g[row + 1, cells])
+                + (even[:-1] + odd[1:])
+                + behind * pair_sums(u2[row - 2, z : z + count])
+                + center * pair_sums(here[1:-1])
+                + center_ahead * pair_sums(there[1:-1])
+                + ahead * pair_sums(u2[row + 1, z : z + count])
+            )
+        return carry
+
+    lax.fori_loop(0, s.shape[0], restrict_row, 0)
+
+
+def inner_kernel(
+    local_rows, block, deep_ref, near_ref, far_ref, u_ref, s_ref,
+    g, u1, u2, s, c_ref, ahead_ref, behind_ref, in_sems, out_sems,
+):
+    pairs, start = [], 0
+    for ref in (deep_ref, near_ref, far_ref):
+        pairs.append((ref, g.at[start : start + ref.shape[0]]))
+        start += ref.shape[0]
+    loads = started(pairs, in_sems)
+    position, squares = place(), mode_squares(c_ref.shape[1:])
+    upper = position[0] == 1
+    row_weights(upper, local_rows, -DEEP, DEEP + local_rows, squares, c_ref, ahead_ref, behind_ref)
+    weights = (c_ref, ahead_ref, behind_ref, -DEEP)
+    finished(loads)
+    smooth_columns(local_rows, block, (0, block), g, u1, u2, s, weights, None)
+    pairs = [(u2.at[DEEP - 3 : DEEP - 1 + local_rows], u_ref), (s, s_ref)]
+    finished(started(pairs, out_sems))
+
+
+def outer_kernel(
+    local_rows, block,
+    deep_ref, near_ref, far_ref, left_ref, right_ref, inner_ref,
+    u_left_ref, u_right_ref, head_ref, tail_ref,
+    g_left, g_right, u1, u2_left, u2_right, s_left, s_right, head, tail,
+    c_ref, ahead_ref, behind_ref, in_sems, out_sems,
+):
+    wide = g_left.shape[1]
+    own = wide - NEAR
+    pairs, start = [], 0
+    for ref in (deep_ref, near_ref, far_ref):
+        span = slice(start, start + ref.shape[0])
+        pairs.append((ref.at[:, :own], g_left.at[span, NEAR:]))
+        pairs.append((ref.at[:, block - own :], g_right.at[span, :own]))
+        start = span.stop
+    pairs += [(left_ref, g_left.at[:, :NEAR]), (right_ref, g_right.at[:, own:])]
+    inner = inner_ref.shape[1]
+    pairs += [(inner_ref.at[:, : FAR - 1], head.at[:, 1:])]
+    pairs += [(inner_ref.at[:, inner - FAR + 1 :], tail.at[:, : FAR - 1])]
+    loads = started(pairs, in_sems)
+    position, squares = place(), mode_squares(c_ref.shape[1:])
+    upper = position[0] == 1
+    row_weights(upper, local_rows, -DEEP, DEEP + local_rows, squares, c_ref, ahead_ref, behind_ref)
+    masks = side_masks(position, squares.shape)
+    weights = (c_ref, ahead_ref, behind_ref, -DEEP)
+    finished(loads)
+    rows = slice(DEEP - 3, DEEP - 1 + local_rows)
+    smooth_columns(local_rows, block, (-NEAR, own), g_left, u1, u2_left, s_left, weights, masks)
+    head[:, 0] = s_left[:, 0]
+    pairs = [(u2_left.at[rows, :NEAR], u_left_ref), (head, head_ref)]
+    stores = started(pairs, out_sems)
+    smooth_columns(
+        local_rows, block, (block - own, block + NEAR), g_right, u1, u2_right, s_right, weights, masks
+    )
+    tail[:, FAR - 1] = s_right[:, 0]
+    pairs = [(u2_right.at[rows, wide - 2 - NEAR :], u_right_ref), (tail, tail_ref)]
+    finished(stores + started(pairs, out_sems, 2))
+
+
+def finish_kernel(local_rows, block, tile_groups, *refs):
+    (
+        high_ref, low_ref, o_ref,
+        s, e0, e1, u, v, g, w, o, t_high, t_low,
+        c_ref, ahead_ref, behind_ref, cc_ref, cahead_ref, cbehind_ref, in_sems, out_sems,
+    ) = refs[-21:]
+    s_inner, s_head, s_tail, s_left, s_right, u_inner, u_left, u_right = refs[:8]
+    g_refs = refs[8:13]
+    position, squares = place(), mode_squares(c_ref.shape[1:])
+    upper = position[0] == 1
+    half_rows, half = local_rows // 2, block // 2
+    pairs = [
+        (s_inner, s.at[:, FAR + 1 : FAR + half - 1]),
+        (s_head.at[:, 0:1], s.at[:, FAR : FAR + 1]),
+        (s_tail.at[:, FAR - 1 : FAR], s.at[:, FAR + half - 1 : FAR + half]),
+        (s_left, s.at[:, 0:FAR]),
+        (s_right, s.at[:, FAR + half : FAR + half + FAR]),
+    ]
+    s_loads = started(pairs, in_sems)
+    u_rows = slice(0, local_rows + 2)
+    pairs, start = [
+        (u_left, u.at[u_rows, :NEAR]),
+        (u_inner, u.at[u_rows, NEAR : NEAR + block - 2]),
+        (u_right, u.at[u_rows, NEAR + block - 2 :]),
+    ], 0
+    middle = slice(1, 1 + block)
+    for ref in g_refs[:3]:
+        rows = slice(DEEP - 1, DEEP) if start == 0 else slice(0, ref.shape[0])
+        count = rows.stop - rows.start
+        pairs.append((ref.at[rows], g.at[start : start + count, middle]))
+        start += count
+    rows = slice(DEEP - 1, DEEP + local_rows)
+    pairs.append((g_refs[3].at[rows, NEAR - 1 : NEAR], g.at[:, 0:1]))
+    pairs.append((g_refs[4].at[rows, 0:1], g.at[:, 1 + block : 2 + block]))
+    pairs += [(high_ref, t_high), (low_ref, t_low)]
+    loads = started(pairs, in_sems, len(s_loads))
+    masks = side_masks(position, squares.shape)
+    row_weights(upper, half_rows, -FAR, FAR + half_rows, squares, cc_ref, cahead_ref, cbehind_ref)
+    row_weights(upper, local_rows, -1, 1 + local_rows, squares, c_ref, ahead_ref, behind_ref)
+    coarse = (cc_ref, cahead_ref, cbehind_ref, -FAR)
+    fine = (c_ref, ahead_ref, behind_ref, -1)
+    for buffer in (e0, e1):
+        buffer[FAR + half_rows] = jnp.zeros(buffer.shape[1:], jnp.float32)
+    u[2 + local_rows] = jnp.zeros(u.shape[1:], jnp.float32)
+    v[1 + local_rows] = jnp.zeros(v.shape[1:], jnp.float32)
+    finished(s_loads)
+    s_at = (s, -FAR, -FAR)
+    here, there = (e0, -FAR, -FAR), (e1, -FAR, -FAR)
+    first_sweep((-FAR, half_rows), (-FAR, half + FAR), half, s_at, here, coarse, masks)
+    for step in range(1, COARSE):
+        sweep(
+            (step - FAR, half_rows), (step - FAR, half + FAR - step), half, here, s_at if step > 1 else None, there, coarse, masks
+        )
+        here, there = there, here
+    e = here[0]
+    finished(loads)
+
+    def add_correction(index, carry):
+        for first, count in ((-1, (half + 2) // 2), (-1 + (half + 2) // 2, half + 2 - (half + 2) // 2)):
+            part = e[index + FAR - 1, first + FAR : first + FAR + count]
+            twice = jnp.broadcast_to(part[:, None], (count, 2) + part.shape[1:])
+            twice = twice.reshape(2 * count, *part.shape[1:])
+            cells = slice(2 * first + 2, 2 * first + 2 + 2 * count)
+            for offset in range(2):
+                u[2 * index + offset, cells] = u[2 * index + offset, cells] + twice
+        return carry
+
+    lax.fori_loop(0, half_rows + 1, add_correction, 0)
+    u_at, v_at, g_at = (u, -2, -2), (v, -1, -1), (g, -1, -1)
+    sweep((-1, local_rows), (-1, block + 1), block, u_at, g_at, v_at, fine, masks)
+    group_rows = TILE // tile_groups
+    turn = (position[1] & (group_rows - 1), group_rows)
+    sweep((0, local_rows), (0, block), block, v_at, g_at, (w, 0, 0), fine, masks, turn)
+    stores = []
+    for n in range(local_rows // TILE):
+        span = slice(n * tile_groups, (n + 1) * tile_groups)
+        synthesis_tile(w.at[n * TILE : (n + 1) * TILE], t_high, t_low, o.at[:, span])
+        stores += started([(o.at[:, span], o_ref.at[:, span])], out_sems, n)
+    finished(stores)
+
+
+def params(mebibytes, *order):
+    return pltpu.CompilerParams(
+        dimension_semantics=order or None, vmem_limit_bytes=mebibytes * 1024 * 1024
+    )
+
+
+def cell_body(density):
+    local_phi, local_rows, vertical_cells = density.shape
+    az_count = lax.axis_size("az")
+    azimuths = local_phi * az_count
+    block = vertical_cells // az_count
+    rows = LANES // block
+    tiles = local_rows // TILE
+    groups = TILE // rows
+    chunks = 2
+    chunk_tiles = tiles // chunks
+    chunk_rows = local_rows // chunks
+    analysis, synthesis = mode_tables(azimuths)
+    point = (azimuths // LANES, LANES)
+    f32 = jnp.float32
+    a_high, a_low = high_low(analysis)
+    s_high, s_low = high_low(synthesis)
+    order = block_order(az_count)
+    product = 2 * 3 * azimuths * azimuths // 2
+    lane_tiles = vertical_cells // LANES
+    anywhere = pl.BlockSpec(memory_space=pl.ANY)
+    in_hbm = pl.BlockSpec(memory_space=pltpu.HBM)
+
+    def field(row_count, cell_count):
+        return jax.ShapeDtypeStruct((row_count, cell_count) + point, f32)
+
+    def scratch(row_count, *cell_count):
+        return pltpu.VMEM((row_count,) + cell_count + point, f32)
+
+    def semaphores(count):
+        return pltpu.SemaphoreType.DMA((count,))
+
+    def cost(mebibytes):
+        return pl.CostEstimate(flops=0, bytes_accessed=mebibytes * 1024 * 1024, transcendentals=0)
+
+    def pack(first_tile):
+        return pl.pallas_call(
+            lambda *refs: pack_kernel(block, order, first_tile, *refs),
+            in_specs=[in_hbm],
+            out_specs=in_hbm,
+            out_shape=jax.ShapeDtypeStruct(
+                (az_count, chunk_tiles * groups, local_phi, LANES), f32
+            ),
+            scratch_shapes=[
+                pltpu.VMEM((chunk_tiles, lane_tiles, local_phi, TILE, LANES), f32),
+                pltpu.VMEM((az_count, chunk_tiles * groups, local_phi, LANES), f32),
+                pltpu.SemaphoreType.DMA((chunk_tiles * lane_tiles,)),
+                pltpu.SemaphoreType.DMA((chunk_tiles,)),
+            ],
+            compiler_params=params(56),
+            name="pack",
+        )(density)
+
+    half_rows, half = local_rows // 2, block // 2
+    all_rows, coarse_rows = DEEP + local_rows, FAR + half_rows
+    tables = [pltpu.VMEM((azimuths // 2, azimuths), jnp.bfloat16)] * 2
+
+    def analyse(received, held):
+        out_shape = [field(chunk_rows, block)]
+        out_shape += [field(all_rows, NEAR)] * 2 if held else [field(DEEP, block)]
+        return pl.pallas_call(
+            lambda *refs: analysis_kernel(groups, *refs),
+            in_specs=[in_hbm] * 3 + [anywhere] * len(held),
+            out_specs=[anywhere] * len(out_shape),
+            out_shape=out_shape,
+            scratch_shapes=[
+                pltpu.VMEM((az_count, chunk_tiles * groups, local_phi, LANES), f32),
+                *tables,
+                scratch(chunk_rows, block),
+                scratch(all_rows, 2 * NEAR) if held else scratch(DEEP, block),
+                semaphores(chunk_tiles),
+                semaphores(2),
+                semaphores(chunk_rows + 6),
+            ],
+            compiler_params=params(56),
+            cost_estimate=cost(12),
+            name="analysis",
+        )(received, a_high, a_low, *held)
+
+    def exchange(value):
+        return lax.all_to_all(value, "az", split_axis=0, concat_axis=0, tiled=True)
+
+    to_right = [(order[i], order[i + 1]) for i in range(az_count - 1)]
+    to_left = [(b, a) for a, b in to_right]
+
+    def from_sides(head, tail):
+        return lax.ppermute(tail, "az", to_right), lax.ppermute(head, "az", to_left)
+
+    first_received = exchange(pack(0))
+    second_received = exchange(pack(chunk_tiles))
+    near, edge = analyse(first_received, ())
+    deep = lax.ppermute(edge, "rad", [(0, 1), (1, 0)])
+    far, head, tail = analyse(second_received, (deep, near))
+    fields = (deep, near, far, *from_sides(head, tail))
+
+    wide = 2 * NEAR + 1
+    weight_scratch = [scratch(all_rows)] * 3
+    u_inner, s_inner = pl.pallas_call(
+        lambda *refs: inner_kernel(local_rows, block, *refs),
+        in_specs=[anywhere] * 3,
+        out_specs=[anywhere] * 2,
+        out_shape=[field(local_rows + 2, block - 2), field(coarse_rows, half - 2)],
+        scratch_shapes=[
+            scratch(all_rows, block),
+            scratch(all_rows + 1, block),
+            scratch(all_rows, block - 2),
+            scratch(coarse_rows, half - 2),
+            *weight_scratch,
+            semaphores(3),
+            semaphores(2),
+        ],
+        compiler_params=params(28),
+        cost_estimate=cost(32),
+        name="inner",
+    )(*fields[:3])
+    u_left, u_right, s_head, s_tail = pl.pallas_call(
+        lambda *refs: outer_kernel(local_rows, block, *refs),
+        in_specs=[anywhere] * 6,
+        out_specs=[anywhere] * 4,
+        out_shape=[field(local_rows + 2, NEAR)] * 2 + [field(coarse_rows, FAR)] * 2,
+        scratch_shapes=[
+            scratch(all_rows, wide),
+            scratch(all_rows, wide),
+            scratch(all_rows + 1, wide),
+            scratch(all_rows, wide - 2),
+            scratch(all_rows, wide - 2),
+            scratch(coarse_rows, 1),
+            scratch(coarse_rows, 1),
+            scratch(coarse_rows, FAR),
+            scratch(coarse_rows, FAR),
+            *weight_scratch,
+            semaphores(10),
+            semaphores(4),
+        ],
+        compiler_params=params(20),
+        cost_estimate=cost(12),
+        name="outer",
+    )(*fields, s_inner)
+    s_parts = (s_inner, s_head, s_tail, *from_sides(s_head, s_tail))
+
+    received_shape = (az_count, tiles * groups, local_phi, LANES)
+    physical = pl.pallas_call(
+        lambda *refs: finish_kernel(local_rows, block, groups, *refs),
+        in_specs=[anywhere] * 13 + [in_hbm] * 2,
+        out_specs=in_hbm,
+        out_shape=jax.ShapeDtypeStruct(received_shape, f32),
+        scratch_shapes=[
+            scratch(coarse_rows, half + 2 * FAR),
+            scratch(coarse_rows + 1, half + 2 * FAR),
+            scratch(coarse_rows + 1, half + 2 * FAR),
+            scratch(local_rows + 3, block + 4),
+            scratch(local_rows + 2, block + 2),
+            scratch(local_rows + 1, block + 2),
+            scratch(local_rows, block),
+            pltpu.VMEM(received_shape, f32),
+            *tables,
+            scratch(local_rows + 1),
+            scratch(local_rows + 1),
+            scratch(local_rows + 1),
+            scratch(coarse_rows),
+            scratch(coarse_rows),
+            scratch(coarse_rows),
+            semaphores(15),
+            semaphores(tiles),
+        ],
+        compiler_params=params(46),
+        name="finish",
+    )(*s_parts, u_inner, u_left, u_right, *fields, s_high, s_low)
+
+    returned = exchange(physical)
+    side = jnp.stack([lax.axis_index("rad"), lax.axis_index("az")]).astype(jnp.int32)
+    return pl.pallas_call(
+        lambda *refs: unpack_kernel(block, order, *refs),
+        in_specs=[in_hbm, anywhere],
+        out_specs=in_hbm,
+        out_shape=jax.ShapeDtypeStruct(density.shape, f32),
+        scratch_shapes=[
+            pltpu.VMEM((az_count, tiles * groups, local_phi, LANES), f32),
+            pltpu.VMEM((tiles, lane_tiles, local_phi, TILE, LANES), f32),
+            pltpu.SemaphoreType.DMA((tiles,)),
+            pltpu.SemaphoreType.DMA((tiles * lane_tiles,)),
+        ],
+        compiler_params=params(56),
+        name="unpack",
+    )(returned, side)
+
+
+def block_order(az_count):
+    return [i ^ 2 if (i // 4) % 2 else i for i in range(az_count)]
+
+
+def fits_cells(density):
+    local_phi, local_rows, vertical_cells = density.shape
+    az_count, rad_count = lax.axis_size("az"), lax.axis_size("rad")
+    block = vertical_cells // az_count
+    return (
+        rad_count == 2
+        and vertical_cells % (az_count * 2) == 0
+        and vertical_cells % LANES == 0
+        and LANES // TILE <= block <= LANES
+        and LANES % block == 0
+        and block // 2 >= FAR
+        and local_rows % (4 * TILE) == 0
+        and local_rows // 2 >= DEEP
+        and az_count % 4 == 0
+        and local_phi % TILE == 0
+        and (az_count * local_phi) % (2 * LANES) == 0
+        and az_count * local_phi == TILE * LANES
+    )
+
+
+def body(density):
+    return cell_body(density) if fits_cells(density) else general_body(density)
 
 
 def solution(mesh):

time: 695 us -> 268 us (0.39)
  waiting for transfers between devices: 295 us -> 185 us
  blocking collectives: 96.9 us -> 0 us
  local copies, waits for them, and re-layouts: 81.2 us -> 4.38 us
  other arithmetic: 73.7 us -> 0.65 us
  matrix products: 67.7 us -> 0 us
  Pallas kernels: 0 us -> 47.8 us
  starting transfers between devices: 74.2 us -> 29.1 us
    all_to_all x3, waiting for transfers between devices: 277 us -> 176 us  [exchange(): return lax.all_to_all(value, 'az', split_axis=0, concat_axis=0, tiled=True)]
    all_to_all x1 -> x0, blocking collectives: 96.9 us -> none  [body(): lax.all_to_all(physical, 'az', split_axis=0, concat_axis=1, tiled=True)]
    dot_general x2 -> x0, matrix products: 67.7 us -> none  [transform_with(): jnp.dot(table, matrix, precision=lax.Precision.HIGHEST, preferred_element...]
    reshape x8 -> x0, local copies, waits for them, and re-layouts: 49.2 us -> none  [the longest x2 12.8 us: transform_with(): return result.reshape(azimuths, 1, width)]
    pallas_call x0 -> x8, Pallas kernels: none -> 47.8 us  [the longest x1 14.9 us: cell_body(): pl.pallas_call(lambda *refs: finish_kernel(local_rows, block, groups, *re...]
    ppermute x18 -> x5, starting transfers between devices: 47.7 us -> 11.8 us  [the longest x2 6.52 us: from_sides(): lax.ppermute(tail, 'az', to_right)]
    add x13 -> x0, other arithmetic: 29.6 us -> none  [the longest x8 24.9 us: relax(): iterate + OMEGA * (source - apply_op(iterate, pad_both(iterate), coeffici...]
    concatenate x9 -> x0, other arithmetic: 18.3 us -> none  [with_halo(): jnp.concatenate([lax.ppermute(tail, axis, [(i, (i + 1) % count) for i in...]
  transfers between devices with their start and end apart: 21 -> 8, of which waited for: 21 -> 7; matrix products, arithmetic and copies ran while one was open for 0% -> 0% of each run, Pallas kernels for 0% -> 6%
where the time goes in v3:
time: 268 us
  waiting for transfers between devices  185 us (69%)
  Pallas kernels  47.8 us (18%)
  starting transfers between devices  29.1 us (11%)
  local copies, waits for them, and re-layouts  4.38 us (2%)
    all_to_all x3, waiting for transfers between devices, exchange(): return lax.all_to_all(value, 'az', split_axis=0, concat_axis=0, tiled=True)  176 us
    all_to_all x3, starting transfers between devices, exchange(): return lax.all_to_all(value, 'az', split_axis=0, concat_axis=0, tiled=True)  17.3 us
    pallas_call x1, Pallas kernels, cell_body(): pl.pallas_call(lambda *refs: finish_kernel(local_rows, block, groups, *re...  14.9 us
    pallas_call x2, Pallas kernels, analyse(): pl.pallas_call(lambda *refs: analysis_kernel(groups, *refs), in_specs=[in...  13.7 us
    ppermute x2, starting transfers between devices, from_sides(): lax.ppermute(tail, 'az', to_right)  6.52 us
    pallas_call x2, Pallas kernels, pack(): pl.pallas_call(lambda *refs: pack_kernel(block, order, first_tile, *refs)...  6.04 us
    pallas_call x1, Pallas kernels, cell_body(): pl.pallas_call(lambda *refs: inner_kernel(local_rows, block, *refs), in_s...  5.66 us
  transfers between devices with their start and end apart: 8, of which 7 were waited for; matrix products, arithmetic and copies ran while one was open for 0% of the time, Pallas kernels for 6%

profile of v3, /device:TPU:11, one launch (start us, length us, event | category | flops | bytes accessed | tf_op | source)
XLA Modules:
  0.0 267.6 jit_solution(18066651211379198673)
XLA Ops:
  0.0 3.0 %pack.2 = f32[16,4,64,128]{3,2,1,0:T(8,128)} custom-call(f32[64,32,512]{2,1,0:T(8,128)} %refs_0_.3), custom_call_target="tpu_custom_call" | custom-call | tf_op jit(solution)/shard_map/pack/pallas_call | solution.py:723
  3.0 6.6 %all-to-all-start = ((f32[16,4,64,128]{3,2,1,0:T(8,128)}), f32[16,4,64,128]{3,2,1,0:T(8,128)S(1)}, u32[]{:S(2)}, u32[]{:S(2)}) async-start(f32[16,4,64,128]{3,2,1,0:T(8,128)} %pack.2), calls=%async_computation | async-start | bytes 4194304 | tf_op jit(solution)/shard_map/all_to_all | solution.py:767
  9.6 3.0 %pack.3 = f32[16,4,64,128]{3,2,1,0:T(8,128)} custom-call(f32[64,32,512]{2,1,0:T(8,128)} %refs_0_.3), custom_call_target="tpu_custom_call" | custom-call | tf_op jit(solution)/shard_map/pack/pallas_call | solution.py:723
  12.6 44.4 %all-to-all-done.refs_0_ = f32[16,4,64,128]{3,2,1,0:T(8,128)S(1)} async-done(((f32[16,4,64,128]{3,2,1,0:T(8,128)}), f32[16,4,64,128]{3,2,1,0:T(8,128)S(1)}, u32[]{:S(2)}, u32[]{:S(2)}) %all-to-all-start) | async-done | bytes 2097184 | tf_op jit(solution)/shard_map/all_to_all | solution.py:767
  57.0 0.0 copy-start.9
  57.0 4.9 %all-to-all-start.1 = ((f32[16,4,64,128]{3,2,1,0:T(8,128)}), f32[16,4,64,128]{3,2,1,0:T(8,128)}, u32[]{:S(2)}, u32[]{:S(2)}) async-start(f32[16,4,64,128]{3,2,1,0:T(8,128)} %pack.3), calls=%async_computation.1 | async-start | bytes 4194304 | tf_op jit(solution)/shard_map/all_to_all | solution.py:767
  61.9 0.0 copy-done.9
  61.9 6.9 %analysis.2 = (f32[16,32,8,128]{3,2,1,0:T(8,128)}, f32[14,32,8,128]{3,2,1,0:T(8,128)}) custom-call(f32[16,4,64,128]{3,2,1,0:T(8,128)} %copy-done.9, bf16[512,1024]{1,0:T(8,128)(2,1)} %constant.16.clone.refs_1_, bf16[512,1024]{1,0:T(8,128)(2,1)} %constant.17.clone.refs_2_), custom_call_target="tpu_custom_call" | custom-call | bytes 12582912 | tf_op jit(solution)/shard_map/analysis/pallas_call | solution.py:747
  68.9 1.3 collective-permute-start
  70.2 39.5 %all-to-all-done.1.refs_0_ = f32[16,4,64,128]{3,2,1,0:T(8,128)} async-done(((f32[16,4,64,128]{3,2,1,0:T(8,128)}), f32[16,4,64,128]{3,2,1,0:T(8,128)}, u32[]{:S(2)}, u32[]{:S(2)}) %all-to-all-start.1) | async-done | bytes 2097184 | tf_op jit(solution)/shard_map/all_to_all | solution.py:767
  109.6 0.7 collective-permute-done.refs_3_.refs_0_.refs_8_
  110.4 0.0 copy-start.1
  110.4 1.3 copy-done.1
  111.6 0.0 copy-start
  111.6 6.8 %analysis.3 = (f32[16,32,8,128]{3,2,1,0:T(8,128)}, f32[46,3,8,128]{3,2,1,0:T(8,128)}, f32[46,3,8,128]{3,2,1,0:T(8,128)}) custom-call(f32[16,4,64,128]{3,2,1,0:T(8,128)} %all-to-all-done.1.refs_0_, bf16[512,1024]{1,0:T(8,128)(2,1)} %constant.16.clone.refs_1_, bf16[512,1024]{1,0:T(8,128)(2,1)} %constant.17.clone.refs_2_, f32[14,32,8,128]{3,2,1,0:T(8,128)} %copy-done.1, ...), custom_call_target="tpu_custom_call" | custom-call | bytes 12582912 | tf_op jit(solution)/shard_map/analysis/pallas_call | solution.py:747
  118.4 3.3 %collective-permute-start.1 = (f32[46,3,8,128]{3,2,1,0:T(8,128)}, f32[46,3,8,128]{3,2,1,0:T(8,128)S(1)}, u32[]{:S(2)}, u32[]{:S(2)}) collective-permute-start(f32[46,3,8,128]{3,2,1,0:T(8,128)} %get-tuple-element.20), channel_id=1, source_target_pairs={{0,2},{2,4},{4,6},{6,12},{12,14},{14,8},{8,10},{10,16},{16,18},{18... | collective-permute-start | bytes 1695752 | tf_op jit(solution)/shard_map/ppermute | solution.py:773
  121.7 1.9 collective-permute-start.2
  123.6 0.0 copy-done
  123.6 0.0 copy-start.2
  123.7 1.5 copy-done.2
  125.2 0.0 copy-start.4
  125.2 1.6 copy-done.4
  126.7 0.0 copy-start.3
  126.7 0.0 copy-start.5
  126.7 5.7 %inner.1 = (f32[34,30,8,128]{3,2,1,0:T(8,128)S(1)}, f32[22,14,8,128]{3,2,1,0:T(8,128)S(1)}) custom-call(f32[14,32,8,128]{3,2,1,0:T(8,128)S(1)} %copy-done.2, f32[16,32,8,128]{3,2,1,0:T(8,128)S(1)} %copy-done, f32[16,32,8,128]{3,2,1,0:T(8,128)S(1)} %copy-done.4), custom_call_target="tpu_custom_call" | custom-call | bytes 33554432 | tf_op jit(solution)/shard_map/inner/pallas_call | solution.py:784
  132.4 0.0 copy-start.6
  132.4 0.0 collective-permute-done.1.refs_3_.refs_11_
  132.4 0.4 collective-permute-done.2.refs_4_.refs_12_
  132.9 0.0 copy-done.3
  132.9 0.0 copy-done.5
  132.9 0.0 copy-start.7
  132.9 0.0 copy-start.8
  132.9 3.9 %outer.1 = (f32[34,3,8,128]{3,2,1,0:T(8,128)S(1)}, f32[34,3,8,128]{3,2,1,0:T(8,128)S(1)}, f32[22,6,8,128]{3,2,1,0:T(8,128)S(1)}, f32[22,6,8,128]{3,2,1,0:T(8,128)S(1)}) custom-call(f32[14,32,8,128]{3,2,1,0:T(8,128)S(1)} %copy-done.3, f32[16,32,8,128]{3,2,1,0:T(8,128)S(1)} %copy-done, f32[16,32,8,128]{3,2,1,0:T(8,128)S(1)} %copy-done.5, ...), custom_call_target="tpu_custom_call" | custom-call | bytes 12582912 | tf_op jit(solution)/shard_map/outer/pallas_call | solution.py:802
  136.8 0.0 copy-done.6
  136.8 3.3 %collective-permute-start.3 = (f32[22,6,8,128]{3,2,1,0:T(8,128)S(1)}, f32[22,6,8,128]{3,2,1,0:T(8,128)S(1)}, u32[]{:S(2)}, u32[]{:S(2)}) collective-permute-start(f32[22,6,8,128]{3,2,1,0:T(8,128)S(1)} %get-tuple-element.23.refs_2_), channel_id=1, source_target_pairs={{0,2},{2,4},{4,6},{6,12},{12,14},{14,8},{8,10},{10,16},{16,18},{18... | collective-permute-start | bytes 1622024 | tf_op jit(solution)/shard_map/ppermute | solution.py:773
  140.1 2.1 collective-permute-start.4
  142.2 4.2 %collective-permute-done.3.refs_3_ = f32[22,6,8,128]{3,2,1,0:T(8,128)S(1)} collective-permute-done((f32[22,6,8,128]{3,2,1,0:T(8,128)S(1)}, f32[22,6,8,128]{3,2,1,0:T(8,128)S(1)}, u32[]{:S(2)}, u32[]{:S(2)}) %collective-permute-start.3) | collective-permute-done | bytes 540704 | tf_op jit(solution)/shard_map/ppermute | solution.py:773
  146.4 4.4 %collective-permute-done.4.refs_4_ = f32[22,6,8,128]{3,2,1,0:T(8,128)S(1)} collective-permute-done((f32[22,6,8,128]{3,2,1,0:T(8,128)S(1)}, f32[22,6,8,128]{3,2,1,0:T(8,128)S(1)}, u32[]{:S(2)}, u32[]{:S(2)}) %collective-permute-start.4) | collective-permute-done | bytes 540704 | tf_op jit(solution)/shard_map/ppermute | solution.py:773
  150.8 0.0 copy-done.7
  150.8 0.0 copy-done.8
  150.8 14.9 %finish.1 = f32[16,8,64,128]{3,2,1,0:T(8,128)} custom-call(f32[22,14,8,128]{3,2,1,0:T(8,128)S(1)} %get-tuple-element.19.refs_5_.refs_0_, f32[22,6,8,128]{3,2,1,0:T(8,128)S(1)} %get-tuple-element.22.refs_1_, f32[22,6,8,128]{3,2,1,0:T(8,128)S(1)} %get-tuple-element.23.refs_2_, f32[22,6,8,128]{3,2,1,0:T(8,128)S(1)} %collective-permute-done.3.refs_3_, ...), custom_call_target="tpu_custom_call" | custom-call | tf_op jit(solution)/shard_map/finish/pallas_call | solution.py:828
  165.7 5.8 %all-to-all-start.2 = ((f32[16,8,64,128]{3,2,1,0:T(8,128)}), f32[16,8,64,128]{3,2,1,0:T(8,128)}, u32[]{:S(2)}, u32[]{:S(2)}) async-start(f32[16,8,64,128]{3,2,1,0:T(8,128)} %finish.1), calls=%async_computation.2 | async-start | bytes 8388608 | tf_op jit(solution)/shard_map/all_to_all | solution.py:767
  171.5 0.6 pad_add_fusion.refs_1_
  172.1 91.8 %all-to-all-done.2.refs_0_ = f32[16,8,64,128]{3,2,1,0:T(8,128)} async-done(((f32[16,8,64,128]{3,2,1,0:T(8,128)}), f32[16,8,64,128]{3,2,1,0:T(8,128)}, u32[]{:S(2)}, u32[]{:S(2)}) %all-to-all-start.2) | async-done | bytes 4194336 | tf_op jit(solution)/shard_map/all_to_all | solution.py:767
  263.9 3.5 %unpack.1 = f32[64,32,512]{2,1,0:T(8,128)} custom-call(f32[16,8,64,128]{3,2,1,0:T(8,128)} %all-to-all-done.2.refs_0_, s32[2]{0:T(128)} %pad_add_fusion.refs_1_), custom_call_target="tpu_custom_call" | custom-call | tf_op jit(solution)/shard_map/unpack/pallas_call | solution.py:858
Async XLA Ops:
  3.0 54.0 %all-to-all-start = ((f32[16,4,64,128]{3,2,1,0:T(8,128)}), f32[16,4,64,128]{3,2,1,0:T(8,128)S(1)}, u32[]{:S(2)}, u32[]{:S(2)}) async-start(f32[16,4,64,128]{3,2,1,0:T(8,128)} %pack.2), calls=%async_computation | async-start | bytes 4194304 | tf_op jit(solution)/shard_map/all_to_all | solution.py:767
  57.0 4.9 %copy-start.9 = (f32[16,4,64,128]{3,2,1,0:T(8,128)}, f32[16,4,64,128]{3,2,1,0:T(8,128)S(1)}, u32[]{:S(2)}) copy-start(f32[16,4,64,128]{3,2,1,0:T(8,128)S(1)} %all-to-all-done.refs_0_) | copy-start | bytes 6291460
  57.0 52.6 %all-to-all-start.1 = ((f32[16,4,64,128]{3,2,1,0:T(8,128)}), f32[16,4,64,128]{3,2,1,0:T(8,128)}, u32[]{:S(2)}, u32[]{:S(2)}) async-start(f32[16,4,64,128]{3,2,1,0:T(8,128)} %pack.3), calls=%async_computation.1 | async-start | bytes 4194304 | tf_op jit(solution)/shard_map/all_to_all | solution.py:767
  68.9 41.5 %collective-permute-start = (f32[14,32,8,128]{3,2,1,0:T(8,128)}, f32[14,32,8,128]{3,2,1,0:T(8,128)S(1)}, u32[]{:S(2)}, u32[]{:S(2)}) collective-permute-start(f32[14,32,8,128]{3,2,1,0:T(8,128)} %get-tuple-element.16), channel_id=1, source_target_pairs={{0,1},{1,0},{2,3},{3,2},{4,5},{5,4},{6,7},{7,6},{8,9},{9,8},{10,11... | collective-permute-start | bytes 5505032 | tf_op jit(solution)/shard_map/ppermute | solution.py:778
  110.4 1.3 copy-start.1
  111.6 12.0 %copy-start = (f32[16,32,8,128]{3,2,1,0:T(8,128)S(1)}, f32[16,32,8,128]{3,2,1,0:T(8,128)}, u32[]{:S(2)}) copy-start(f32[16,32,8,128]{3,2,1,0:T(8,128)} %get-tuple-element.17.refs_4_.refs_1_.refs_9_) | copy-start | bytes 6291460
  118.4 14.0 %collective-permute-start.1 = (f32[46,3,8,128]{3,2,1,0:T(8,128)}, f32[46,3,8,128]{3,2,1,0:T(8,128)S(1)}, u32[]{:S(2)}, u32[]{:S(2)}) collective-permute-start(f32[46,3,8,128]{3,2,1,0:T(8,128)} %get-tuple-element.20), channel_id=1, source_target_pairs={{0,2},{2,4},{4,6},{6,12},{12,14},{14,8},{8,10},{10,16},{16,18},{18... | collective-permute-start | bytes 1695752 | tf_op jit(solution)/shard_map/ppermute | solution.py:773
  121.7 11.1 %collective-permute-start.2 = (f32[46,3,8,128]{3,2,1,0:T(8,128)}, f32[46,3,8,128]{3,2,1,0:T(8,128)S(1)}, u32[]{:S(2)}, u32[]{:S(2)}) collective-permute-start(f32[46,3,8,128]{3,2,1,0:T(8,128)} %get-tuple-element.21), channel_id=1, source_target_pairs={{2,0},{4,2},{6,4},{12,6},{14,12},{8,14},{10,8},{16,10},{18,16},{20... | collective-permute-start | bytes 1695752 | tf_op jit(solution)/shard_map/ppermute | solution.py:773
  123.6 1.5 copy-start.2
  125.2 1.6 copy-start.4
  126.7 6.1 %copy-start.3 = (f32[14,32,8,128]{3,2,1,0:T(8,128)S(1)}, f32[14,32,8,128]{3,2,1,0:T(8,128)}, u32[]{:S(2)}) copy-start(f32[14,32,8,128]{3,2,1,0:T(8,128)} %copy-done.1) | copy-start | bytes 5505028
  126.7 6.1 %copy-start.5 = (f32[16,32,8,128]{3,2,1,0:T(8,128)S(1)}, f32[16,32,8,128]{3,2,1,0:T(8,128)}, u32[]{:S(2)}) copy-start(f32[16,32,8,128]{3,2,1,0:T(8,128)} %get-tuple-element.18.refs_2_.refs_10_) | copy-start | bytes 6291460
  132.4 4.4 %copy-start.6 = (f32[34,30,8,128]{3,2,1,0:T(8,128)}, f32[34,30,8,128]{3,2,1,0:T(8,128)S(1)}, u32[]{:S(2)}) copy-start(f32[34,30,8,128]{3,2,1,0:T(8,128)S(1)} %get-tuple-element.24.refs_5_) | copy-start | bytes 12533764
  132.9 17.9 %copy-start.7 = (bf16[512,1024]{1,0:T(8,128)(2,1)S(1)}, bf16[512,1024]{1,0:T(8,128)(2,1)}, u32[]{:S(2)}) copy-start(bf16[512,1024]{1,0:T(8,128)(2,1)} %constant.18.clone.refs_13_) | copy-start | bytes 3145732
  132.9 17.9 %copy-start.8 = (bf16[512,1024]{1,0:T(8,128)(2,1)S(1)}, bf16[512,1024]{1,0:T(8,128)(2,1)}, u32[]{:S(2)}) copy-start(bf16[512,1024]{1,0:T(8,128)(2,1)} %constant.19.clone.refs_14_) | copy-start | bytes 3145732
  136.8 9.5 %collective-permute-start.3 = (f32[22,6,8,128]{3,2,1,0:T(8,128)S(1)}, f32[22,6,8,128]{3,2,1,0:T(8,128)S(1)}, u32[]{:S(2)}, u32[]{:S(2)}) collective-permute-start(f32[22,6,8,128]{3,2,1,0:T(8,128)S(1)} %get-tuple-element.23.refs_2_), channel_id=1, source_target_pairs={{0,2},{2,4},{4,6},{6,12},{12,14},{14,8},{8,10},{10,16},{16,18},{18... | collective-permute-start | bytes 1622024 | tf_op jit(solution)/shard_map/ppermute | solution.py:773
  140.1 10.7 %collective-permute-start.4 = (f32[22,6,8,128]{3,2,1,0:T(8,128)S(1)}, f32[22,6,8,128]{3,2,1,0:T(8,128)S(1)}, u32[]{:S(2)}, u32[]{:S(2)}) collective-permute-start(f32[22,6,8,128]{3,2,1,0:T(8,128)S(1)} %get-tuple-element.22.refs_1_), channel_id=1, source_target_pairs={{2,0},{4,2},{6,4},{12,6},{14,12},{8,14},{10,8},{16,10},{18,16},{20... | collective-permute-start | bytes 1622024 | tf_op jit(solution)/shard_map/ppermute | solution.py:773
  165.7 98.3 %all-to-all-start.2 = ((f32[16,8,64,128]{3,2,1,0:T(8,128)}), f32[16,8,64,128]{3,2,1,0:T(8,128)}, u32[]{:S(2)}, u32[]{:S(2)}) async-start(f32[16,8,64,128]{3,2,1,0:T(8,128)} %finish.1), calls=%async_computation.2 | async-start | bytes 8388608 | tf_op jit(solution)/shard_map/all_to_all | solution.py:767

commit v4 on v3

--- a/solution.py
+++ b/solution.py
@@ -313,15 +313,12 @@
     return field, field.at[:, :depth], field.at[:, cells - depth : cells]
 
 
-def analysis_kernel(tile_groups, *refs):
+def analysis_kernel(tile_groups, held_count, *refs):
     position = place()
     x_ref, high_ref, low_ref = refs[:3]
     outs = refs[3:-8]
     x, t_high, t_low, o, edge, in_sems, t_sems, out_sems = refs[-8:]
-    if len(outs) == 2:
-        held_refs = ()
-    else:
-        held_refs, outs = outs[:2], outs[2:]
+    held_refs, outs = outs[:held_count], outs[held_count:]
     sources, width, lanes = x.shape[0], x.shape[2], x.shape[3]
     cells = o.shape[1]
     half = sources // 2 * width
@@ -335,8 +332,11 @@
     gathers, start = [], 0
     for held in held_refs:
         span = slice(start, start + held.shape[0])
-        sides = zip(sides_of(held, NEAR)[1:], (slice(0, NEAR), slice(NEAR, 2 * NEAR)))
-        pairs = [(side, edge.at[span, columns]) for side, columns in sides]
+        if held.shape[1] == 2 * NEAR:
+            pairs = [(held, edge.at[span])]
+        else:
+            sides = zip(sides_of(held, NEAR)[1:], (slice(0, NEAR), slice(NEAR, 2 * NEAR)))
+            pairs = [(side, edge.at[span, columns]) for side, columns in sides]
         gathers += started(pairs, out_sems, out_sems.shape[0] - 4 + len(gathers))
         start += held.shape[0]
     stores = []
@@ -379,7 +379,9 @@
     else:
         for row in range(DEEP):
             edge[DEEP - 1 - row] = o[turned_row(row, turn, group_rows)]
-        stores += started([(edge, outs[1])], out_sems, len(stores))
+        _, head, tail = sides_of(edge, NEAR)
+        pairs = [(head, outs[1].at[:, :NEAR]), (tail, outs[1].at[:, NEAR:]), (edge, outs[2])]
+        stores += started(pairs, out_sems, len(stores))
     finished(stores)
 
 
@@ -743,9 +745,9 @@
 
     def analyse(received, held):
         out_shape = [field(chunk_rows, block)]
-        out_shape += [field(all_rows, NEAR)] * 2 if held else [field(DEEP, block)]
+        out_shape += [field(all_rows, NEAR)] * 2 if held else [field(DEEP, 2 * NEAR), field(DEEP, block)]
         return pl.pallas_call(
-            lambda *refs: analysis_kernel(groups, *refs),
+            lambda *refs: analysis_kernel(groups, len(held), *refs),
             in_specs=[in_hbm] * 3 + [anywhere] * len(held),
             out_specs=[anywhere] * len(out_shape),
             out_shape=out_shape,
@@ -774,9 +776,11 @@
 
     first_received = exchange(pack(0))
     second_received = exchange(pack(chunk_tiles))
-    near, edge = analyse(first_received, ())
+    near, edge_sides, edge = analyse(first_received, ())
+    deep_sides = lax.ppermute(edge_sides, "rad", [(0, 1), (1, 0)])
+    deep_sides, edge = lax.optimization_barrier((deep_sides, edge))
     deep = lax.ppermute(edge, "rad", [(0, 1), (1, 0)])
-    far, head, tail = analyse(second_received, (deep, near))
+    far, head, tail = analyse(second_received, (deep_sides, near))
     fields = (deep, near, far, *from_sides(head, tail))
 
     wide = 2 * NEAR + 1

time: 268 us -> 263 us (0.981)
    all_to_all x3, waiting for transfers between devices: 176 us -> 166 us  [exchange(): return lax.all_to_all(value, 'az', split_axis=0, concat_axis=0, tiled=True)]
    ppermute x0 -> x1, waiting for transfers between devices: none -> 8.26 us  [cell_body(): deep_sides = lax.ppermute(edge_sides, 'rad', [(0, 1), (1, 0)])]
  transfers between devices with their start and end apart: 8 -> 9, of which waited for: 7 -> 7; matrix products, arithmetic and copies ran while one was open for 0% -> 0% of each run, Pallas kernels for 6% -> 9%
where the time goes in v4:
time: 263 us
  waiting for transfers between devices  184 us (70%)
  Pallas kernels  47.9 us (18%)
  starting transfers between devices  28.2 us (11%)
    all_to_all x3, waiting for transfers between devices, exchange(): return lax.all_to_all(value, 'az', split_axis=0, concat_axis=0, tiled=True)  166 us
    all_to_all x3, starting transfers between devices, exchange(): return lax.all_to_all(value, 'az', split_axis=0, concat_axis=0, tiled=True)  16.8 us
    pallas_call x1, Pallas kernels, cell_body(): pl.pallas_call(lambda *refs: finish_kernel(local_rows, block, groups, *re...  14.9 us
    pallas_call x2, Pallas kernels, analyse(): pl.pallas_call(lambda *refs: analysis_kernel(groups, len(held), *refs), i...  13.8 us
    ppermute x1, waiting for transfers between devices, cell_body(): deep_sides = lax.ppermute(edge_sides, 'rad', [(0, 1), (1, 0)])  8.26 us
    pallas_call x2, Pallas kernels, pack(): pl.pallas_call(lambda *refs: pack_kernel(block, order, first_tile, *refs)...  6.04 us
    pallas_call x1, Pallas kernels, cell_body(): pl.pallas_call(lambda *refs: inner_kernel(local_rows, block, *refs), in_s...  5.66 us
  transfers between devices with their start and end apart: 9, of which 7 were waited for; matrix products, arithmetic and copies ran while one was open for 0% of the time, Pallas kernels for 9%

profile of v4, /device:TPU:11, one launch (start us, length us, event | category | flops | bytes accessed | tf_op | source)
XLA Modules:
  0.0 262.9 jit_solution(16617304792843599894)
XLA Ops:
  0.0 3.0 %pack.2 = f32[16,4,64,128]{3,2,1,0:T(8,128)} custom-call(f32[64,32,512]{2,1,0:T(8,128)} %refs_0_.3), custom_call_target="tpu_custom_call" | custom-call | tf_op jit(solution)/shard_map/pack/pallas_call | solution.py:725
  3.0 6.6 %all-to-all-start = ((f32[16,4,64,128]{3,2,1,0:T(8,128)}), f32[16,4,64,128]{3,2,1,0:T(8,128)S(1)}, u32[]{:S(2)}, u32[]{:S(2)}) async-start(f32[16,4,64,128]{3,2,1,0:T(8,128)} %pack.2), calls=%async_computation | async-start | bytes 4194304 | tf_op jit(solution)/shard_map/all_to_all | solution.py:769
  9.6 3.0 %pack.3 = f32[16,4,64,128]{3,2,1,0:T(8,128)} custom-call(f32[64,32,512]{2,1,0:T(8,128)} %refs_0_.3), custom_call_target="tpu_custom_call" | custom-call | tf_op jit(solution)/shard_map/pack/pallas_call | solution.py:725
  12.6 44.4 %all-to-all-done.refs_0_ = f32[16,4,64,128]{3,2,1,0:T(8,128)S(1)} async-done(((f32[16,4,64,128]{3,2,1,0:T(8,128)}), f32[16,4,64,128]{3,2,1,0:T(8,128)S(1)}, u32[]{:S(2)}, u32[]{:S(2)}) %all-to-all-start) | async-done | bytes 2097184 | tf_op jit(solution)/shard_map/all_to_all | solution.py:769
  57.0 0.0 copy-start.7
  57.0 4.9 %all-to-all-start.1 = ((f32[16,4,64,128]{3,2,1,0:T(8,128)}), f32[16,4,64,128]{3,2,1,0:T(8,128)}, u32[]{:S(2)}, u32[]{:S(2)}) async-start(f32[16,4,64,128]{3,2,1,0:T(8,128)} %pack.3), calls=%async_computation.1 | async-start | bytes 4194304 | tf_op jit(solution)/shard_map/all_to_all | solution.py:769
  61.9 0.0 copy-done.7
  61.9 7.1 %analysis.2 = (f32[16,32,8,128]{3,2,1,0:T(8,128)}, f32[14,6,8,128]{3,2,1,0:T(8,128)}, f32[14,32,8,128]{3,2,1,0:T(8,128)}) custom-call(f32[16,4,64,128]{3,2,1,0:T(8,128)} %copy-done.7, bf16[512,1024]{1,0:T(8,128)(2,1)} %constant.16.clone.refs_1_, bf16[512,1024]{1,0:T(8,128)(2,1)} %constant.17.clone.refs_2_), custom_call_target="tpu_custom_call" | custom-call | bytes 12582912 | tf_op jit(solution)/shard_map/analysis/pallas_call | solution.py:749
  69.0 1.3 collective-permute-start
  70.3 8.3 %collective-permute-done.refs_3_ = f32[14,6,8,128]{3,2,1,0:T(8,128)S(1)} collective-permute-done((f32[14,6,8,128]{3,2,1,0:T(8,128)}, f32[14,6,8,128]{3,2,1,0:T(8,128)S(1)}, u32[]{:S(2)}, u32[]{:S(2)}) %collective-permute-start) | collective-permute-done | bytes 344096 | tf_op jit(solution)/shard_map/ppermute | solution.py:780
  78.6 0.0 copy-start.8
  78.6 1.2 collective-permute-start.1
  79.8 29.8 %all-to-all-done.1.refs_0_ = f32[16,4,64,128]{3,2,1,0:T(8,128)} async-done(((f32[16,4,64,128]{3,2,1,0:T(8,128)}), f32[16,4,64,128]{3,2,1,0:T(8,128)}, u32[]{:S(2)}, u32[]{:S(2)}) %all-to-all-start.1) | async-done | bytes 2097184 | tf_op jit(solution)/shard_map/all_to_all | solution.py:769
  109.6 0.0 copy-done.8
  109.6 0.0 copy-start
  109.6 6.7 %analysis.3 = (f32[16,32,8,128]{3,2,1,0:T(8,128)}, f32[46,3,8,128]{3,2,1,0:T(8,128)}, f32[46,3,8,128]{3,2,1,0:T(8,128)}) custom-call(f32[16,4,64,128]{3,2,1,0:T(8,128)} %all-to-all-done.1.refs_0_, bf16[512,1024]{1,0:T(8,128)(2,1)} %constant.16.clone.refs_1_, bf16[512,1024]{1,0:T(8,128)(2,1)} %constant.17.clone.refs_2_, f32[14,6,8,128]{3,2,1,0:T(8,128)} %copy-done.8, ...), custom_call_target="tpu_custom_call" | custom-call | bytes 12582912 | tf_op jit(solution)/shard_map/analysis/pallas_call | solution.py:749
  116.4 1.9 collective-permute-start.2
  118.3 2.4 collective-permute-start.3
  120.7 0.0 collective-permute-done.1.refs_0_.refs_8_
  120.7 0.0 copy-start.3
  120.7 0.0 copy-done
  120.7 0.0 copy-start.1
  120.7 2.2 copy-done.1
  123.0 0.0 copy-start.2
  123.0 5.7 %inner.1 = (f32[34,30,8,128]{3,2,1,0:T(8,128)S(1)}, f32[22,14,8,128]{3,2,1,0:T(8,128)S(1)}) custom-call(f32[14,32,8,128]{3,2,1,0:T(8,128)S(1)} %collective-permute-done.1.refs_0_.refs_8_, f32[16,32,8,128]{3,2,1,0:T(8,128)S(1)} %copy-done, f32[16,32,8,128]{3,2,1,0:T(8,128)S(1)} %copy-done.1), custom_call_target="tpu_custom_call" | custom-call | bytes 33554432 | tf_op jit(solution)/shard_map/inner/pallas_call | solution.py:788
  128.7 0.0 copy-start.4
  128.7 0.0 collective-permute-done.2.refs_3_.refs_11_
  128.7 0.8 collective-permute-done.3.refs_4_.refs_12_
  129.4 0.0 copy-done.3
  129.4 0.0 copy-done.2
  129.4 0.0 copy-start.5
  129.4 0.0 copy-start.6
  129.5 3.9 %outer.1 = (f32[34,3,8,128]{3,2,1,0:T(8,128)S(1)}, f32[34,3,8,128]{3,2,1,0:T(8,128)S(1)}, f32[22,6,8,128]{3,2,1,0:T(8,128)S(1)}, f32[22,6,8,128]{3,2,1,0:T(8,128)S(1)}) custom-call(f32[14,32,8,128]{3,2,1,0:T(8,128)S(1)} %collective-permute-done.1.refs_0_.refs_8_, f32[16,32,8,128]{3,2,1,0:T(8,128)S(1)} %copy-done, f32[16,32,8,128]{3,2,1,0:T(8,128)S(1)} %copy-done.2, ...), custom_call_target="tpu_custom_call" | custom-call | bytes 12582912 | tf_op jit(solution)/shard_map/outer/pallas_call | solution.py:806
  133.4 0.0 copy-done.4
  133.4 2.4 collective-permute-start.4
  135.8 2.1 collective-permute-start.5
  138.0 4.2 %collective-permute-done.4.refs_3_ = f32[22,6,8,128]{3,2,1,0:T(8,128)S(1)} collective-permute-done((f32[22,6,8,128]{3,2,1,0:T(8,128)S(1)}, f32[22,6,8,128]{3,2,1,0:T(8,128)S(1)}, u32[]{:S(2)}, u32[]{:S(2)}) %collective-permute-start.4) | collective-permute-done | bytes 540704 | tf_op jit(solution)/shard_map/ppermute | solution.py:775
  142.1 4.4 %collective-permute-done.5.refs_4_ = f32[22,6,8,128]{3,2,1,0:T(8,128)S(1)} collective-permute-done((f32[22,6,8,128]{3,2,1,0:T(8,128)S(1)}, f32[22,6,8,128]{3,2,1,0:T(8,128)S(1)}, u32[]{:S(2)}, u32[]{:S(2)}) %collective-permute-start.5) | collective-permute-done | bytes 540704 | tf_op jit(solution)/shard_map/ppermute | solution.py:775
  146.5 0.0 copy-done.5
  146.5 0.0 copy-done.6
  146.5 14.9 %finish.1 = f32[16,8,64,128]{3,2,1,0:T(8,128)} custom-call(f32[22,14,8,128]{3,2,1,0:T(8,128)S(1)} %get-tuple-element.25.refs_5_.refs_0_, f32[22,6,8,128]{3,2,1,0:T(8,128)S(1)} %get-tuple-element.28.refs_1_, f32[22,6,8,128]{3,2,1,0:T(8,128)S(1)} %get-tuple-element.29.refs_2_, f32[22,6,8,128]{3,2,1,0:T(8,128)S(1)} %collective-permute-done.4.refs_3_, ...), custom_call_target="tpu_custom_call" | custom-call | tf_op jit(solution)/shard_map/finish/pallas_call | solution.py:832
  161.4 5.3 %all-to-all-start.2 = ((f32[16,8,64,128]{3,2,1,0:T(8,128)}), f32[16,8,64,128]{3,2,1,0:T(8,128)}, u32[]{:S(2)}, u32[]{:S(2)}) async-start(f32[16,8,64,128]{3,2,1,0:T(8,128)} %finish.1), calls=%async_computation.2 | async-start | bytes 8388608 | tf_op jit(solution)/shard_map/all_to_all | solution.py:769
  166.7 0.6 pad_add_fusion.refs_1_
  167.4 91.8 %all-to-all-done.2.refs_0_ = f32[16,8,64,128]{3,2,1,0:T(8,128)} async-done(((f32[16,8,64,128]{3,2,1,0:T(8,128)}), f32[16,8,64,128]{3,2,1,0:T(8,128)}, u32[]{:S(2)}, u32[]{:S(2)}) %all-to-all-start.2) | async-done | bytes 4194336 | tf_op jit(solution)/shard_map/all_to_all | solution.py:769
  259.2 3.5 %unpack.1 = f32[64,32,512]{2,1,0:T(8,128)} custom-call(f32[16,8,64,128]{3,2,1,0:T(8,128)} %all-to-all-done.2.refs_0_, s32[2]{0:T(128)} %pad_add_fusion.refs_1_), custom_call_target="tpu_custom_call" | custom-call | tf_op jit(solution)/shard_map/unpack/pallas_call | solution.py:862
Async XLA Ops:
  3.0 54.0 %all-to-all-start = ((f32[16,4,64,128]{3,2,1,0:T(8,128)}), f32[16,4,64,128]{3,2,1,0:T(8,128)S(1)}, u32[]{:S(2)}, u32[]{:S(2)}) async-start(f32[16,4,64,128]{3,2,1,0:T(8,128)} %pack.2), calls=%async_computation | async-start | bytes 4194304 | tf_op jit(solution)/shard_map/all_to_all | solution.py:769
  57.0 4.9 %copy-start.7 = (f32[16,4,64,128]{3,2,1,0:T(8,128)}, f32[16,4,64,128]{3,2,1,0:T(8,128)S(1)}, u32[]{:S(2)}) copy-start(f32[16,4,64,128]{3,2,1,0:T(8,128)S(1)} %all-to-all-done.refs_0_) | copy-start | bytes 6291460
  57.0 52.6 %all-to-all-start.1 = ((f32[16,4,64,128]{3,2,1,0:T(8,128)}), f32[16,4,64,128]{3,2,1,0:T(8,128)}, u32[]{:S(2)}, u32[]{:S(2)}) async-start(f32[16,4,64,128]{3,2,1,0:T(8,128)} %pack.3), calls=%async_computation.1 | async-start | bytes 4194304 | tf_op jit(solution)/shard_map/all_to_all | solution.py:769
  69.0 9.6 %collective-permute-start = (f32[14,6,8,128]{3,2,1,0:T(8,128)}, f32[14,6,8,128]{3,2,1,0:T(8,128)S(1)}, u32[]{:S(2)}, u32[]{:S(2)}) collective-permute-start(f32[14,6,8,128]{3,2,1,0:T(8,128)} %get-tuple-element.19), channel_id=1, source_target_pairs={{0,1},{1,0},{2,3},{3,2},{4,5},{5,4},{6,7},{7,6},{8,9},{9,8},{10,11... | collective-permute-start | bytes 1032200 | tf_op jit(solution)/shard_map/ppermute | solution.py:780
  78.6 31.0 %copy-start.8 = (f32[14,6,8,128]{3,2,1,0:T(8,128)}, f32[14,6,8,128]{3,2,1,0:T(8,128)S(1)}, u32[]{:S(2)}) copy-start(f32[14,6,8,128]{3,2,1,0:T(8,128)S(1)} %collective-permute-done.refs_3_) | copy-start | bytes 1032196
  78.6 42.1 %collective-permute-start.1 = (f32[14,32,8,128]{3,2,1,0:T(8,128)}, f32[14,32,8,128]{3,2,1,0:T(8,128)S(1)}, u32[]{:S(2)}, u32[]{:S(2)}) collective-permute-start(f32[14,32,8,128]{3,2,1,0:T(8,128)} %get-tuple-element.21), channel_id=1, source_target_pairs={{0,1},{1,0},{2,3},{3,2},{4,5},{5,4},{6,7},{7,6},{8,9},{9,8},{10,11... | collective-permute-start | bytes 5505032 | tf_op jit(solution)/shard_map/ppermute | solution.py:782
  109.6 11.1 %copy-start = (f32[16,32,8,128]{3,2,1,0:T(8,128)S(1)}, f32[16,32,8,128]{3,2,1,0:T(8,128)}, u32[]{:S(2)}) copy-start(f32[16,32,8,128]{3,2,1,0:T(8,128)} %get-tuple-element.22.refs_4_.refs_1_.refs_9_) | copy-start | bytes 6291460
  116.4 12.3 %collective-permute-start.2 = (f32[46,3,8,128]{3,2,1,0:T(8,128)}, f32[46,3,8,128]{3,2,1,0:T(8,128)S(1)}, u32[]{:S(2)}, u32[]{:S(2)}) collective-permute-start(f32[46,3,8,128]{3,2,1,0:T(8,128)} %get-tuple-element.26), channel_id=1, source_target_pairs={{0,2},{2,4},{4,6},{6,12},{12,14},{14,8},{8,10},{10,16},{16,18},{18... | collective-permute-start | bytes 1695752 | tf_op jit(solution)/shard_map/ppermute | solution.py:775
  118.3 11.1 %collective-permute-start.3 = (f32[46,3,8,128]{3,2,1,0:T(8,128)}, f32[46,3,8,128]{3,2,1,0:T(8,128)S(1)}, u32[]{:S(2)}, u32[]{:S(2)}) collective-permute-start(f32[46,3,8,128]{3,2,1,0:T(8,128)} %get-tuple-element.27), channel_id=1, source_target_pairs={{2,0},{4,2},{6,4},{12,6},{14,12},{8,14},{10,8},{16,10},{18,16},{20... | collective-permute-start | bytes 1695752 | tf_op jit(solution)/shard_map/ppermute | solution.py:775
  120.7 8.7 %copy-start.3 = (f32[14,32,8,128]{3,2,1,0:T(8,128)}, f32[14,32,8,128]{3,2,1,0:T(8,128)S(1)}, u32[]{:S(2)}) copy-start(f32[14,32,8,128]{3,2,1,0:T(8,128)S(1)} %collective-permute-done.1.refs_0_.refs_8_) | copy-start | bytes 5505028
  120.7 2.3 copy-start.1
  123.0 6.5 %copy-start.2 = (f32[16,32,8,128]{3,2,1,0:T(8,128)S(1)}, f32[16,32,8,128]{3,2,1,0:T(8,128)}, u32[]{:S(2)}) copy-start(f32[16,32,8,128]{3,2,1,0:T(8,128)} %get-tuple-element.24.refs_2_.refs_10_) | copy-start | bytes 6291460
  128.7 4.7 %copy-start.4 = (f32[34,30,8,128]{3,2,1,0:T(8,128)}, f32[34,30,8,128]{3,2,1,0:T(8,128)S(1)}, u32[]{:S(2)}) copy-start(f32[34,30,8,128]{3,2,1,0:T(8,128)S(1)} %get-tuple-element.30.refs_5_) | copy-start | bytes 12533764
  129.4 17.1 %copy-start.5 = (bf16[512,1024]{1,0:T(8,128)(2,1)S(1)}, bf16[512,1024]{1,0:T(8,128)(2,1)}, u32[]{:S(2)}) copy-start(bf16[512,1024]{1,0:T(8,128)(2,1)} %constant.18.clone.refs_13_) | copy-start | bytes 3145732
  129.4 17.1 %copy-start.6 = (bf16[512,1024]{1,0:T(8,128)(2,1)S(1)}, bf16[512,1024]{1,0:T(8,128)(2,1)}, u32[]{:S(2)}) copy-start(bf16[512,1024]{1,0:T(8,128)(2,1)} %constant.19.clone.refs_14_) | copy-start | bytes 3145732
  133.4 8.7 %collective-permute-start.4 = (f32[22,6,8,128]{3,2,1,0:T(8,128)S(1)}, f32[22,6,8,128]{3,2,1,0:T(8,128)S(1)}, u32[]{:S(2)}, u32[]{:S(2)}) collective-permute-start(f32[22,6,8,128]{3,2,1,0:T(8,128)S(1)} %get-tuple-element.29.refs_2_), channel_id=1, source_target_pairs={{0,2},{2,4},{4,6},{6,12},{12,14},{14,8},{8,10},{10,16},{16,18},{18... | collective-permute-start | bytes 1622024 | tf_op jit(solution)/shard_map/ppermute | solution.py:775
  135.8 10.7 %collective-permute-start.5 = (f32[22,6,8,128]{3,2,1,0:T(8,128)S(1)}, f32[22,6,8,128]{3,2,1,0:T(8,128)S(1)}, u32[]{:S(2)}, u32[]{:S(2)}) collective-permute-start(f32[22,6,8,128]{3,2,1,0:T(8,128)S(1)} %get-tuple-element.28.refs_1_), channel_id=1, source_target_pairs={{2,0},{4,2},{6,4},{12,6},{14,12},{8,14},{10,8},{16,10},{18,16},{20... | collective-permute-start | bytes 1622024 | tf_op jit(solution)/shard_map/ppermute | solution.py:775
  161.4 97.8 %all-to-all-start.2 = ((f32[16,8,64,128]{3,2,1,0:T(8,128)}), f32[16,8,64,128]{3,2,1,0:T(8,128)}, u32[]{:S(2)}, u32[]{:S(2)}) async-start(f32[16,8,64,128]{3,2,1,0:T(8,128)} %finish.1), calls=%async_computation.2 | async-start | bytes 8388608 | tf_op jit(solution)/shard_map/all_to_all | solution.py:769

commit v5 on v4

--- a/solution.py
+++ b/solution.py
@@ -156,17 +156,28 @@
 
 
 def mode_tables(azimuths):
-    half = azimuths // 2
-    even = np.concatenate([np.arange(0, half + 1, 2), np.arange(2, half, 2)])
-    odd = np.concatenate([np.arange(1, half, 2), np.arange(1, half, 2)])
-    even_cos = np.arange(half) <= half // 2
-    odd_cos = np.arange(half) < half // 2
-    modes = np.concatenate([even, odd])
-    is_cos = np.concatenate([even_cos, odd_cos])
+    half, quarter = azimuths // 2, azimuths // 4
+    fours = np.concatenate([np.arange(0, half + 1, 4), np.arange(4, half, 4)])
+    twos = np.concatenate([np.arange(2, half, 4)] * 2)
+    odd = np.concatenate([np.arange(1, half, 2)] * 2)
+    modes = np.concatenate([fours, twos, odd])
+    index = np.arange(quarter)
+    is_cos = np.concatenate(
+        [index <= quarter // 2, index < quarter // 2, np.arange(half) < quarter]
+    )
     angle = 2.0 * np.pi / azimuths * (np.arange(half)[:, None] * modes[None, :] % azimuths)
     values = np.where(is_cos[None, :], np.cos(angle), np.sin(angle))
-    weight = np.where((modes == 0) | (modes == half), 1.0, 2.0) / azimuths
-    return -values, values * weight[None, :]
+    weighted = values * (np.where((modes == 0) | (modes == half), 1.0, 2.0) / azimuths)[None, :]
+    return -values, weighted
+
+
+def table_parts(table, azimuths):
+    quarter = azimuths // 4
+    return [
+        (table.at[0:quarter, 0:quarter], 0),
+        (table.at[0:quarter, quarter : 2 * quarter], quarter),
+        (table.at[:, 2 * quarter :], 2 * quarter),
+    ]
 
 
 def high_low(values):
@@ -188,10 +199,12 @@
 
 def mode_squares(shape):
     half = shape[0] * shape[1] // 2
+    quarter, eighth = half // 2, half // 4
     index = lax.broadcasted_iota(jnp.int32, shape, 0) * shape[1] + lax.broadcasted_iota(jnp.int32, shape, 1)
-    even = 2 * jnp.where(index <= half // 2, index, index - half // 2)
-    odd = 2 * (index & (half // 2 - 1)) + 1
-    modes = jnp.where(index < half, even, odd)
+    fours = 4 * jnp.where(index <= eighth, index, index - eighth)
+    twos = 4 * (index & (eighth - 1)) + 2
+    odd = 2 * (index & (quarter - 1)) + 1
+    modes = jnp.where(index < quarter, fours, jnp.where(index < half, twos, odd))
     return (modes * modes).astype(jnp.float32)
 
 
@@ -342,27 +355,28 @@
     stores = []
     for n in range(tiles):
         loads[n].wait()
-        parts = []
-        for parity in range(2):
-            turned = []
-            for group in range(n * tile_groups, (n + 1) * tile_groups):
-                near, far = x[: sources // 2, group], x[sources // 2 :, group]
-                folded = near + far if parity == 0 else near - far
-                turned.append(folded.reshape(half, lanes).T)
-            parts.append(split_value(jnp.concatenate(turned, axis=0)))
+        turned = [[], [], []]
+        for group in range(n * tile_groups, (n + 1) * tile_groups):
+            near = x[: sources // 2, group].reshape(half, lanes)
+            far = x[sources // 2 :, group].reshape(half, lanes)
+            even = near + far
+            low_half, high_half = even[: half // 2], even[half // 2 :]
+            for part, folded in zip(turned, (low_half + high_half, low_half - high_half, near - far)):
+                part.append(folded.T)
+        parts = [split_value(jnp.concatenate(part, axis=0)) for part in turned]
         if n == 0:
             finished(tables)
         rows = slice(n * TILE, (n + 1) * TILE)
-        for parity, (high, low) in enumerate(parts):
-            columns = slice(parity * half, (parity + 1) * half)
+        columns = zip(parts, table_parts(t_high, 2 * half), table_parts(t_low, 2 * half))
+        for (high, low), (part_high, first), (part_low, _) in columns:
             result = (
-                jnp.dot(high, t_high[:, columns], preferred_element_type=jnp.float32)
-                + jnp.dot(high, t_low[:, columns], preferred_element_type=jnp.float32)
-                + jnp.dot(low, t_high[:, columns], preferred_element_type=jnp.float32)
+                jnp.dot(high, part_high[...], preferred_element_type=jnp.float32)
+                + jnp.dot(high, part_low[...], preferred_element_type=jnp.float32)
+                + jnp.dot(low, part_high[...], preferred_element_type=jnp.float32)
             )
-            for part in range(half // LANES):
+            for part in range(result.shape[1] // LANES):
                 piece = result[:, part * LANES : (part + 1) * LANES]
-                o[rows, :, parity * (half // LANES) + part, :] = piece.reshape(TILE, cells, LANES)
+                o[rows, :, first // LANES + part, :] = piece.reshape(TILE, cells, LANES)
         pairs = [
             (o.at[turned_row(row, turn, group_rows)], outs[0].at[row])
             for row in range(n * TILE, (n + 1) * TILE)
@@ -388,22 +402,20 @@
 def synthesis_tile(u, t_high, t_low, o):
     rows, cells = u.shape[0], u.shape[1]
     half = t_high.shape[0]
-    parts = half // LANES
+    contract = (((1,), (1,)), ((), ()))
     sums = []
-    for parity in range(2):
-        field = jnp.concatenate(
-            [u[:, :, parity * parts + i, :].reshape(rows * cells, LANES) for i in range(parts)],
-            axis=1,
+    for (part_high, first), (part_low, _) in zip(table_parts(t_high, 2 * half), table_parts(t_low, 2 * half)):
+        parts = range(first // LANES, (first + part_high.shape[1]) // LANES)
+        field = jnp.concatenate([u[:, :, i, :].reshape(rows * cells, LANES) for i in parts], axis=1)
+        high, low = split_value(field)
+        sums.append(
+            lax.dot_general(part_high[...], high, contract, preferred_element_type=jnp.float32)
+            + lax.dot_general(part_high[...], low, contract, preferred_element_type=jnp.float32)
+            + lax.dot_general(part_low[...], high, contract, preferred_element_type=jnp.float32)
         )
-        high, low = split_value(field)
-        columns = slice(parity * half, (parity + 1) * half)
-        contract = (((1,), (1,)), ((), ()))
-        sums.append(
-            lax.dot_general(t_high[:, columns], high, contract, preferred_element_type=jnp.float32)
-            + lax.dot_general(t_high[:, columns], low, contract, preferred_element_type=jnp.float32)
-            + lax.dot_general(t_low[:, columns], high, contract, preferred_element_type=jnp.float32)
-        )
-    near, far = sums[0] + sums[1], sums[0] - sums[1]
+    fours, twos, odd = sums
+    even = jnp.concatenate([fours + twos, fours - twos], axis=0)
+    near, far = even + odd, even - odd
     targets, groups, width, lanes = o.shape
     for group in range(groups):
         columns = slice(group * lanes, (group + 1) * lanes)
@@ -600,14 +612,73 @@
     finished(stores + started(pairs, out_sems, 2))
 
 
+def field_pairs(g_refs, g):
+    pairs, start = [], 0
+    local_rows, middle = g.shape[0] - 1, slice(1, g.shape[1] - 1)
+    for ref in g_refs[:3]:
+        rows = slice(DEEP - 1, DEEP) if start == 0 else slice(0, ref.shape[0])
+        count = rows.stop - rows.start
+        pairs.append((ref.at[rows], g.at[start : start + count, middle]))
+        start += count
+    rows = slice(DEEP - 1, DEEP + local_rows)
+    pairs.append((g_refs[3].at[rows, NEAR - 1 : NEAR], g.at[:, 0:1]))
+    pairs.append((g_refs[4].at[rows, 0:1], g.at[:, middle.stop : middle.stop + 1]))
+    return pairs
+
+
+def settle_kernel(
+    local_rows, block, inner_ref, left_ref, right_ref, *refs
+):
+    g_refs = refs[:5]
+    v_ref, u, g, v, c_ref, ahead_ref, behind_ref, in_sems, out_sems = refs[5:]
+    rows = slice(0, local_rows + 2)
+    pairs = [
+        (left_ref, u.at[rows, :NEAR]),
+        (inner_ref, u.at[rows, NEAR : NEAR + block - 2]),
+        (right_ref, u.at[rows, NEAR + block - 2 :]),
+    ]
+    loads = started(pairs + field_pairs(g_refs, g), in_sems)
+    position, squares = place(), mode_squares(c_ref.shape[1:])
+    masks = side_masks(position, squares.shape)
+    upper = position[0] == 1
+    row_weights(upper, local_rows, -1, 1 + local_rows, squares, c_ref, ahead_ref, behind_ref)
+    u[2 + local_rows] = jnp.zeros(u.shape[1:], jnp.float32)
+    finished(loads)
+    u_at, v_at, g_at = (u, -2, -2), (v, -1, -1), (g, -1, -1)
+    weights = (c_ref, ahead_ref, behind_ref, -1)
+    sweep((-1, local_rows), (-1, block + 1), block, u_at, g_at, v_at, weights, masks)
+    finished(started([(v, v_ref)], out_sems))
+
+
+def add_share(v, row, e, here, other, weights, masks, half):
+    c, stay, cross = weights
+    keep = 1.0 - OMEGA
+    count = half // 2
+    for first in (0, count):
+        line = e[here, FAR + first - 1 : FAR + first + count + 1]
+        common = (keep + c * stay + c) * line[1:-1] + (c * cross) * e[other, FAR + first : FAR + first + count]
+        beside = c * line
+        pairs = jnp.stack([common + beside[:-2], common + beside[2:]], axis=1)
+        cells = slice(1 + 2 * first, 1 + 2 * (first + count))
+        v[row, cells] = v[row, cells] + pairs.reshape(2 * count, *pairs.shape[2:])
+    for near, beside, cell, mask in (
+        (FAR - 1, FAR, 0, masks[0]), (FAR + half, FAR + half - 1, 2 * half + 1, masks[1]),
+    ):
+        c_side = c * mask
+        v[row, cell] = v[row, cell] + (
+            (keep + c_side * stay + c_side) * e[here, near]
+            + (c_side * cross) * e[other, near]
+            + c_side * e[here, beside]
+        )
+
+
 def finish_kernel(local_rows, block, tile_groups, *refs):
     (
         high_ref, low_ref, o_ref,
-        s, e0, e1, u, v, g, w, o, t_high, t_low,
+        s, e0, e1, v, g, w, o, t_high, t_low,
         c_ref, ahead_ref, behind_ref, cc_ref, cahead_ref, cbehind_ref, in_sems, out_sems,
-    ) = refs[-21:]
-    s_inner, s_head, s_tail, s_left, s_right, u_inner, u_left, u_right = refs[:8]
-    g_refs = refs[8:13]
+    ) = refs[-20:]
+    s_inner, s_head, s_tail, s_left, s_right, v_ref = refs[:6]
     position, squares = place(), mode_squares(c_ref.shape[1:])
     upper = position[0] == 1
     half_rows, half = local_rows // 2, block // 2
@@ -619,21 +690,7 @@
         (s_right, s.at[:, FAR + half : FAR + half + FAR]),
     ]
     s_loads = started(pairs, in_sems)
-    u_rows = slice(0, local_rows + 2)
-    pairs, start = [
-        (u_left, u.at[u_rows, :NEAR]),
-        (u_inner, u.at[u_rows, NEAR : NEAR + block - 2]),
-        (u_right, u.at[u_rows, NEAR + block - 2 :]),
-    ], 0
-    middle = slice(1, 1 + block)
-    for ref in g_refs[:3]:
-        rows = slice(DEEP - 1, DEEP) if start == 0 else slice(0, ref.shape[0])
-        count = rows.stop - rows.start
-        pairs.append((ref.at[rows], g.at[start : start + count, middle]))
-        start += count
-    rows = slice(DEEP - 1, DEEP + local_rows)
-    pairs.append((g_refs[3].at[rows, NEAR - 1 : NEAR], g.at[:, 0:1]))
-    pairs.append((g_refs[4].at[rows, 0:1], g.at[:, 1 + block : 2 + block]))
+    pairs = [(v_ref, v.at[: local_rows + 1])] + field_pairs(refs[6:11], g)
     pairs += [(high_ref, t_high), (low_ref, t_low)]
     loads = started(pairs, in_sems, len(s_loads))
     masks = side_masks(position, squares.shape)
@@ -643,7 +700,6 @@
     fine = (c_ref, ahead_ref, behind_ref, -1)
     for buffer in (e0, e1):
         buffer[FAR + half_rows] = jnp.zeros(buffer.shape[1:], jnp.float32)
-    u[2 + local_rows] = jnp.zeros(u.shape[1:], jnp.float32)
     v[1 + local_rows] = jnp.zeros(v.shape[1:], jnp.float32)
     finished(s_loads)
     s_at = (s, -FAR, -FAR)
@@ -651,25 +707,24 @@
     first_sweep((-FAR, half_rows), (-FAR, half + FAR), half, s_at, here, coarse, masks)
     for step in range(1, COARSE):
         sweep(
-            (step - FAR, half_rows), (step - FAR, half + FAR - step), half, here, s_at if step > 1 else None, there, coarse, masks
+            (step - FAR, half_rows), (step - FAR, half + FAR - step), half,
+            here, s_at if step > 1 else None, there, coarse, masks,
         )
         here, there = there, here
     e = here[0]
     finished(loads)
 
-    def add_correction(index, carry):
-        for first, count in ((-1, (half + 2) // 2), (-1 + (half + 2) // 2, half + 2 - (half + 2) // 2)):
-            part = e[index + FAR - 1, first + FAR : first + FAR + count]
-            twice = jnp.broadcast_to(part[:, None], (count, 2) + part.shape[1:])
-            twice = twice.reshape(2 * count, *part.shape[1:])
-            cells = slice(2 * first + 2, 2 * first + 2 + 2 * count)
-            for offset in range(2):
-                u[2 * index + offset, cells] = u[2 * index + offset, cells] + twice
+    def add_rows(index, carry):
+        row, at = 2 * index + 1, index + FAR
+        even = (c_ref[row], ahead_ref[row], behind_ref[row])
+        add_share(v, row, e, at, at - 1, even, masks, half)
+        odd = (c_ref[row + 1], behind_ref[row + 1], ahead_ref[row + 1])
+        add_share(v, row + 1, e, at, at + 1, odd, masks, half)
         return carry
 
-    lax.fori_loop(0, half_rows + 1, add_correction, 0)
-    u_at, v_at, g_at = (u, -2, -2), (v, -1, -1), (g, -1, -1)
-    sweep((-1, local_rows), (-1, block + 1), block, u_at, g_at, v_at, fine, masks)
+    add_share(v, 0, e, FAR - 1, FAR, (c_ref[0], behind_ref[0], ahead_ref[0]), masks, half)
+    lax.fori_loop(0, half_rows, add_rows, 0)
+    v_at, g_at = (v, -1, -1), (g, -1, -1)
     group_rows = TILE // tile_groups
     turn = (position[1] & (group_rows - 1), group_rows)
     sweep((0, local_rows), (0, block), block, v_at, g_at, (w, 0, 0), fine, masks, turn)
@@ -828,17 +883,34 @@
     )(*fields, s_inner)
     s_parts = (s_inner, s_head, s_tail, *from_sides(s_head, s_tail))
 
+    settled = pl.pallas_call(
+        lambda *refs: settle_kernel(local_rows, block, *refs),
+        in_specs=[anywhere] * 8,
+        out_specs=anywhere,
+        out_shape=field(local_rows + 1, block + 2),
+        scratch_shapes=[
+            scratch(local_rows + 3, block + 4),
+            scratch(local_rows + 1, block + 2),
+            scratch(local_rows + 1, block + 2),
+            *[scratch(local_rows + 1)] * 3,
+            semaphores(8),
+            semaphores(1),
+        ],
+        compiler_params=params(24),
+        cost_estimate=cost(16),
+        name="settle",
+    )(u_inner, u_left, u_right, *fields)
+
     received_shape = (az_count, tiles * groups, local_phi, LANES)
     physical = pl.pallas_call(
         lambda *refs: finish_kernel(local_rows, block, groups, *refs),
-        in_specs=[anywhere] * 13 + [in_hbm] * 2,
+        in_specs=[anywhere] * 11 + [in_hbm] * 2,
         out_specs=in_hbm,
         out_shape=jax.ShapeDtypeStruct(received_shape, f32),
         scratch_shapes=[
             scratch(coarse_rows, half + 2 * FAR),
             scratch(coarse_rows + 1, half + 2 * FAR),
             scratch(coarse_rows + 1, half + 2 * FAR),
-            scratch(local_rows + 3, block + 4),
             scratch(local_rows + 2, block + 2),
             scratch(local_rows + 1, block + 2),
             scratch(local_rows, block),
@@ -850,12 +922,12 @@
             scratch(coarse_rows),
             scratch(coarse_rows),
             scratch(coarse_rows),
-            semaphores(15),
+            semaphores(13),
             semaphores(tiles),
         ],
         compiler_params=params(46),
         name="finish",
-    )(*s_parts, u_inner, u_left, u_right, *fields, s_high, s_low)
+    )(*s_parts, settled, *fields, s_high, s_low)
 
     returned = exchange(physical)
     side = jnp.stack([lax.axis_index("rad"), lax.axis_index("az")]).astype(jnp.int32)

time: 263 us -> 261 us (level)
  waiting for transfers between devices: 184 us -> 178 us
    ppermute x2, waiting for transfers between devices: 4.16 us -> 0.01 us  [from_sides(): lax.ppermute(tail, 'az', to_right)]
    pallas_call x0 -> x1, Pallas kernels: none -> 3.74 us  [cell_body(): pl.pallas_call(lambda *refs: settle_kernel(local_rows, block, *refs), in_...]
  transfers between devices with their start and end apart: 9 -> 9, of which waited for: 7 -> 6; matrix products, arithmetic and copies ran while one was open for 0% -> 0% of each run, Pallas kernels for 9% -> 10%
where the time goes in v5:
time: 261 us; the launch traced here: 260 us
  waiting for transfers between devices  178 us (68%)
  Pallas kernels  48.9 us (19%)
  starting transfers between devices  28.2 us (11%)
  local copies, waits for them, and re-layouts  4.36 us (2%)
    all_to_all x3, waiting for transfers between devices, exchange(): return lax.all_to_all(value, 'az', split_axis=0, concat_axis=0, tiled=True)  166 us
    all_to_all x3, starting transfers between devices, exchange(): return lax.all_to_all(value, 'az', split_axis=0, concat_axis=0, tiled=True)  16.8 us
    pallas_call x2, Pallas kernels, analyse(): pl.pallas_call(lambda *refs: analysis_kernel(groups, len(held), *refs), i...  13.2 us
    pallas_call x1, Pallas kernels, cell_body(): pl.pallas_call(lambda *refs: finish_kernel(local_rows, block, groups, *re...  12.9 us
    ppermute x1, waiting for transfers between devices, cell_body(): deep_sides = lax.ppermute(edge_sides, 'rad', [(0, 1), (1, 0)])  8.25 us
    pallas_call x2, Pallas kernels, pack(): pl.pallas_call(lambda *refs: pack_kernel(block, order, first_tile, *refs)...  6.05 us
    pallas_call x1, Pallas kernels, cell_body(): pl.pallas_call(lambda *refs: inner_kernel(local_rows, block, *refs), in_s...  5.66 us
  transfers between devices with their start and end apart: 9, of which 6 were waited for; matrix products, arithmetic and copies ran while one was open for 0% of the time, Pallas kernels for 10%

profile of v5, /device:TPU:11, one launch (start us, length us, event | category | flops | bytes accessed | tf_op | source)
XLA Modules:
  0.0 260.5 jit_solution(3412262073217081642)
XLA Ops:
  0.0 3.0 %pack.2 = f32[16,4,64,128]{3,2,1,0:T(8,128)} custom-call(f32[64,32,512]{2,1,0:T(8,128)} %refs_0_.3), custom_call_target="tpu_custom_call" | custom-call | tf_op jit(solution)/shard_map/pack/pallas_call | solution.py:780
  3.0 6.6 %all-to-all-start = ((f32[16,4,64,128]{3,2,1,0:T(8,128)}), f32[16,4,64,128]{3,2,1,0:T(8,128)S(1)}, u32[]{:S(2)}, u32[]{:S(2)}) async-start(f32[16,4,64,128]{3,2,1,0:T(8,128)} %pack.2), calls=%async_computation | async-start | bytes 4194304 | tf_op jit(solution)/shard_map/all_to_all | solution.py:824
  9.6 3.0 %pack.3 = f32[16,4,64,128]{3,2,1,0:T(8,128)} custom-call(f32[64,32,512]{2,1,0:T(8,128)} %refs_0_.3), custom_call_target="tpu_custom_call" | custom-call | tf_op jit(solution)/shard_map/pack/pallas_call | solution.py:780
  12.6 44.4 %all-to-all-done.refs_0_ = f32[16,4,64,128]{3,2,1,0:T(8,128)S(1)} async-done(((f32[16,4,64,128]{3,2,1,0:T(8,128)}), f32[16,4,64,128]{3,2,1,0:T(8,128)S(1)}, u32[]{:S(2)}, u32[]{:S(2)}) %all-to-all-start) | async-done | bytes 2097184 | tf_op jit(solution)/shard_map/all_to_all | solution.py:824
  57.0 0.0 copy-start.7
  57.0 4.9 %all-to-all-start.1 = ((f32[16,4,64,128]{3,2,1,0:T(8,128)}), f32[16,4,64,128]{3,2,1,0:T(8,128)}, u32[]{:S(2)}, u32[]{:S(2)}) async-start(f32[16,4,64,128]{3,2,1,0:T(8,128)} %pack.3), calls=%async_computation.1 | async-start | bytes 4194304 | tf_op jit(solution)/shard_map/all_to_all | solution.py:824
  61.9 0.0 copy-done.7
  61.9 6.8 %analysis.2 = (f32[16,32,8,128]{3,2,1,0:T(8,128)}, f32[14,6,8,128]{3,2,1,0:T(8,128)}, f32[14,32,8,128]{3,2,1,0:T(8,128)}) custom-call(f32[16,4,64,128]{3,2,1,0:T(8,128)} %copy-done.7, bf16[512,1024]{1,0:T(8,128)(2,1)} %constant.16.clone.refs_1_, bf16[512,1024]{1,0:T(8,128)(2,1)} %constant.17.clone.refs_2_), custom_call_target="tpu_custom_call" | custom-call | bytes 12582912 | tf_op jit(solution)/shard_map/analysis/pallas_call | solution.py:804
  68.7 1.3 collective-permute-start
  70.0 8.3 %collective-permute-done.refs_3_ = f32[14,6,8,128]{3,2,1,0:T(8,128)S(1)} collective-permute-done((f32[14,6,8,128]{3,2,1,0:T(8,128)}, f32[14,6,8,128]{3,2,1,0:T(8,128)S(1)}, u32[]{:S(2)}, u32[]{:S(2)}) %collective-permute-start) | collective-permute-done | bytes 344096 | tf_op jit(solution)/shard_map/ppermute | solution.py:835
  78.3 0.0 copy-start.8
  78.3 1.2 collective-permute-start.1
  79.5 30.1 %all-to-all-done.1.refs_0_ = f32[16,4,64,128]{3,2,1,0:T(8,128)} async-done(((f32[16,4,64,128]{3,2,1,0:T(8,128)}), f32[16,4,64,128]{3,2,1,0:T(8,128)}, u32[]{:S(2)}, u32[]{:S(2)}) %all-to-all-start.1) | async-done | bytes 2097184 | tf_op jit(solution)/shard_map/all_to_all | solution.py:824
  109.6 0.0 copy-done.8
  109.6 0.0 copy-start
  109.6 6.4 %analysis.3 = (f32[16,32,8,128]{3,2,1,0:T(8,128)}, f32[46,3,8,128]{3,2,1,0:T(8,128)}, f32[46,3,8,128]{3,2,1,0:T(8,128)}) custom-call(f32[16,4,64,128]{3,2,1,0:T(8,128)} %all-to-all-done.1.refs_0_, bf16[512,1024]{1,0:T(8,128)(2,1)} %constant.16.clone.refs_1_, bf16[512,1024]{1,0:T(8,128)(2,1)} %constant.17.clone.refs_2_, f32[14,6,8,128]{3,2,1,0:T(8,128)} %copy-done.8, ...), custom_call_target="tpu_custom_call" | custom-call | bytes 12582912 | tf_op jit(solution)/shard_map/analysis/pallas_call | solution.py:804
  116.0 1.9 collective-permute-start.2
  118.0 2.4 collective-permute-start.3
  120.4 0.0 collective-permute-done.1.refs_0_.refs_3_.refs_6_
  120.4 0.0 copy-start.3
  120.4 0.0 copy-done
  120.4 0.0 copy-start.1
  120.4 2.2 copy-done.1
  122.7 0.0 copy-start.2
  122.7 5.7 %inner.1 = (f32[34,30,8,128]{3,2,1,0:T(8,128)S(1)}, f32[22,14,8,128]{3,2,1,0:T(8,128)S(1)}) custom-call(f32[14,32,8,128]{3,2,1,0:T(8,128)S(1)} %collective-permute-done.1.refs_0_.refs_3_.refs_6_, f32[16,32,8,128]{3,2,1,0:T(8,128)S(1)} %copy-done, f32[16,32,8,128]{3,2,1,0:T(8,128)S(1)} %copy-done.1), custom_call_target="tpu_custom_call" | custom-call | bytes 33554432 | tf_op jit(solution)/shard_map/inner/pallas_call | solution.py:843
  128.3 0.0 collective-permute-done.2.refs_3_.refs_6_.refs_9_
  128.3 0.8 collective-permute-done.3.refs_4_.refs_7_.refs_10_
  129.1 0.0 copy-done.2
  129.1 3.9 %outer.1 = (f32[34,3,8,128]{3,2,1,0:T(8,128)S(1)}, f32[34,3,8,128]{3,2,1,0:T(8,128)S(1)}, f32[22,6,8,128]{3,2,1,0:T(8,128)S(1)}, f32[22,6,8,128]{3,2,1,0:T(8,128)S(1)}) custom-call(f32[14,32,8,128]{3,2,1,0:T(8,128)S(1)} %collective-permute-done.1.refs_0_.refs_3_.refs_6_, f32[16,32,8,128]{3,2,1,0:T(8,128)S(1)} %copy-done, f32[16,32,8,128]{3,2,1,0:T(8,128)S(1)} %copy-done.2, ...), custom_call_target="tpu_custom_call" | custom-call | bytes 12582912 | tf_op jit(solution)/shard_map/outer/pallas_call | solution.py:861
  133.0 2.4 collective-permute-start.4
  135.5 2.1 collective-permute-start.5
  137.6 0.0 copy-done.3
  137.6 0.0 copy-start.5
  137.6 0.0 copy-start.6
  137.6 3.7 %settle.1.refs_5_ = f32[33,34,8,128]{3,2,1,0:T(8,128)S(1)} custom-call(f32[34,30,8,128]{3,2,1,0:T(8,128)S(1)} %get-tuple-element.30.refs_0_, f32[34,3,8,128]{3,2,1,0:T(8,128)S(1)} %get-tuple-element.31.refs_1_, f32[34,3,8,128]{3,2,1,0:T(8,128)S(1)} %get-tuple-element.32.refs_2_, f32[14,32,8,128]{3,2,1,0:T(8,128)S(1)} %collective-permute-done.1.refs_0_.refs_3_.refs_6_, ...), custom_call_target="tpu_custom_call" | custom-call | bytes 16777216 | tf_op jit(solution)/shard_map/settle/pallas_call | solution.py:886
  141.4 0.0 copy-start.4
  141.4 2.1 copy-done.4
  143.5 0.0 collective-permute-done.4.refs_3_
  143.5 2.7 %collective-permute-done.5.refs_4_ = f32[22,6,8,128]{3,2,1,0:T(8,128)S(1)} collective-permute-done((f32[22,6,8,128]{3,2,1,0:T(8,128)S(1)}, f32[22,6,8,128]{3,2,1,0:T(8,128)S(1)}, u32[]{:S(2)}, u32[]{:S(2)}) %collective-permute-start.5) | collective-permute-done | bytes 540704 | tf_op jit(solution)/shard_map/ppermute | solution.py:830
  146.1 0.0 copy-done.5
  146.1 0.0 copy-done.6
  146.1 12.9 %finish.1 = f32[16,8,64,128]{3,2,1,0:T(8,128)} custom-call(f32[22,14,8,128]{3,2,1,0:T(8,128)S(1)} %get-tuple-element.25.refs_5_.refs_0_, f32[22,6,8,128]{3,2,1,0:T(8,128)S(1)} %get-tuple-element.28.refs_1_, f32[22,6,8,128]{3,2,1,0:T(8,128)S(1)} %get-tuple-element.29.refs_2_, f32[22,6,8,128]{3,2,1,0:T(8,128)S(1)} %collective-permute-done.4.refs_3_, ...), custom_call_target="tpu_custom_call" | custom-call | tf_op jit(solution)/shard_map/finish/pallas_call | solution.py:905
  159.0 5.3 %all-to-all-start.2 = ((f32[16,8,64,128]{3,2,1,0:T(8,128)}), f32[16,8,64,128]{3,2,1,0:T(8,128)}, u32[]{:S(2)}, u32[]{:S(2)}) async-start(f32[16,8,64,128]{3,2,1,0:T(8,128)} %finish.1), calls=%async_computation.2 | async-start | bytes 8388608 | tf_op jit(solution)/shard_map/all_to_all | solution.py:824
  164.3 0.6 pad_add_fusion.refs_1_
  165.0 91.8 %all-to-all-done.2.refs_0_ = f32[16,8,64,128]{3,2,1,0:T(8,128)} async-done(((f32[16,8,64,128]{3,2,1,0:T(8,128)}), f32[16,8,64,128]{3,2,1,0:T(8,128)}, u32[]{:S(2)}, u32[]{:S(2)}) %all-to-all-start.2) | async-done | bytes 4194336 | tf_op jit(solution)/shard_map/all_to_all | solution.py:824
  256.8 3.5 %unpack.1 = f32[64,32,512]{2,1,0:T(8,128)} custom-call(f32[16,8,64,128]{3,2,1,0:T(8,128)} %all-to-all-done.2.refs_0_, s32[2]{0:T(128)} %pad_add_fusion.refs_1_), custom_call_target="tpu_custom_call" | custom-call | tf_op jit(solution)/shard_map/unpack/pallas_call | solution.py:934
Async XLA Ops:
  3.0 54.0 %all-to-all-start = ((f32[16,4,64,128]{3,2,1,0:T(8,128)}), f32[16,4,64,128]{3,2,1,0:T(8,128)S(1)}, u32[]{:S(2)}, u32[]{:S(2)}) async-start(f32[16,4,64,128]{3,2,1,0:T(8,128)} %pack.2), calls=%async_computation | async-start | bytes 4194304 | tf_op jit(solution)/shard_map/all_to_all | solution.py:824
  57.0 4.9 %copy-start.7 = (f32[16,4,64,128]{3,2,1,0:T(8,128)}, f32[16,4,64,128]{3,2,1,0:T(8,128)S(1)}, u32[]{:S(2)}) copy-start(f32[16,4,64,128]{3,2,1,0:T(8,128)S(1)} %all-to-all-done.refs_0_) | copy-start | bytes 6291460
  57.0 52.6 %all-to-all-start.1 = ((f32[16,4,64,128]{3,2,1,0:T(8,128)}), f32[16,4,64,128]{3,2,1,0:T(8,128)}, u32[]{:S(2)}, u32[]{:S(2)}) async-start(f32[16,4,64,128]{3,2,1,0:T(8,128)} %pack.3), calls=%async_computation.1 | async-start | bytes 4194304 | tf_op jit(solution)/shard_map/all_to_all | solution.py:824
  68.7 9.6 %collective-permute-start = (f32[14,6,8,128]{3,2,1,0:T(8,128)}, f32[14,6,8,128]{3,2,1,0:T(8,128)S(1)}, u32[]{:S(2)}, u32[]{:S(2)}) collective-permute-start(f32[14,6,8,128]{3,2,1,0:T(8,128)} %get-tuple-element.19), channel_id=1, source_target_pairs={{0,1},{1,0},{2,3},{3,2},{4,5},{5,4},{6,7},{7,6},{8,9},{9,8},{10,11... | collective-permute-start | bytes 1032200 | tf_op jit(solution)/shard_map/ppermute | solution.py:835
  78.3 31.4 %copy-start.8 = (f32[14,6,8,128]{3,2,1,0:T(8,128)}, f32[14,6,8,128]{3,2,1,0:T(8,128)S(1)}, u32[]{:S(2)}) copy-start(f32[14,6,8,128]{3,2,1,0:T(8,128)S(1)} %collective-permute-done.refs_3_) | copy-start | bytes 1032196
  78.3 42.1 %collective-permute-start.1 = (f32[14,32,8,128]{3,2,1,0:T(8,128)}, f32[14,32,8,128]{3,2,1,0:T(8,128)S(1)}, u32[]{:S(2)}, u32[]{:S(2)}) collective-permute-start(f32[14,32,8,128]{3,2,1,0:T(8,128)} %get-tuple-element.21), channel_id=1, source_target_pairs={{0,1},{1,0},{2,3},{3,2},{4,5},{5,4},{6,7},{7,6},{8,9},{9,8},{10,11... | collective-permute-start | bytes 5505032 | tf_op jit(solution)/shard_map/ppermute | solution.py:837
  109.6 10.8 %copy-start = (f32[16,32,8,128]{3,2,1,0:T(8,128)S(1)}, f32[16,32,8,128]{3,2,1,0:T(8,128)}, u32[]{:S(2)}) copy-start(f32[16,32,8,128]{3,2,1,0:T(8,128)} %get-tuple-element.22.refs_4_.refs_1_.refs_7_) | copy-start | bytes 6291460
  116.0 12.3 %collective-permute-start.2 = (f32[46,3,8,128]{3,2,1,0:T(8,128)}, f32[46,3,8,128]{3,2,1,0:T(8,128)S(1)}, u32[]{:S(2)}, u32[]{:S(2)}) collective-permute-start(f32[46,3,8,128]{3,2,1,0:T(8,128)} %get-tuple-element.26), channel_id=1, source_target_pairs={{0,2},{2,4},{4,6},{6,12},{12,14},{14,8},{8,10},{10,16},{16,18},{18... | collective-permute-start | bytes 1695752 | tf_op jit(solution)/shard_map/ppermute | solution.py:830
  118.0 11.1 %collective-permute-start.3 = (f32[46,3,8,128]{3,2,1,0:T(8,128)}, f32[46,3,8,128]{3,2,1,0:T(8,128)S(1)}, u32[]{:S(2)}, u32[]{:S(2)}) collective-permute-start(f32[46,3,8,128]{3,2,1,0:T(8,128)} %get-tuple-element.27), channel_id=1, source_target_pairs={{2,0},{4,2},{6,4},{12,6},{14,12},{8,14},{10,8},{16,10},{18,16},{20... | collective-permute-start | bytes 1695752 | tf_op jit(solution)/shard_map/ppermute | solution.py:830
  120.4 17.2 %copy-start.3 = (f32[14,32,8,128]{3,2,1,0:T(8,128)}, f32[14,32,8,128]{3,2,1,0:T(8,128)S(1)}, u32[]{:S(2)}) copy-start(f32[14,32,8,128]{3,2,1,0:T(8,128)S(1)} %collective-permute-done.1.refs_0_.refs_3_.refs_6_) | copy-start | bytes 5505028
  120.4 2.3 copy-start.1
  122.7 6.5 %copy-start.2 = (f32[16,32,8,128]{3,2,1,0:T(8,128)S(1)}, f32[16,32,8,128]{3,2,1,0:T(8,128)}, u32[]{:S(2)}) copy-start(f32[16,32,8,128]{3,2,1,0:T(8,128)} %get-tuple-element.24.refs_2_.refs_5_.refs_8_) | copy-start | bytes 6291460
  133.0 10.4 %collective-permute-start.4 = (f32[22,6,8,128]{3,2,1,0:T(8,128)S(1)}, f32[22,6,8,128]{3,2,1,0:T(8,128)S(1)}, u32[]{:S(2)}, u32[]{:S(2)}) collective-permute-start(f32[22,6,8,128]{3,2,1,0:T(8,128)S(1)} %get-tuple-element.29.refs_2_), channel_id=1, source_target_pairs={{0,2},{2,4},{4,6},{6,12},{12,14},{14,8},{8,10},{10,16},{16,18},{18... | collective-permute-start | bytes 1622024 | tf_op jit(solution)/shard_map/ppermute | solution.py:830
  135.5 10.7 %collective-permute-start.5 = (f32[22,6,8,128]{3,2,1,0:T(8,128)S(1)}, f32[22,6,8,128]{3,2,1,0:T(8,128)S(1)}, u32[]{:S(2)}, u32[]{:S(2)}) collective-permute-start(f32[22,6,8,128]{3,2,1,0:T(8,128)S(1)} %get-tuple-element.28.refs_1_), channel_id=1, source_target_pairs={{2,0},{4,2},{6,4},{12,6},{14,12},{8,14},{10,8},{16,10},{18,16},{20... | collective-permute-start | bytes 1622024 | tf_op jit(solution)/shard_map/ppermute | solution.py:830
  137.6 8.5 %copy-start.5 = (bf16[512,1024]{1,0:T(8,128)(2,1)S(1)}, bf16[512,1024]{1,0:T(8,128)(2,1)}, u32[]{:S(2)}) copy-start(bf16[512,1024]{1,0:T(8,128)(2,1)} %constant.18.clone.refs_11_) | copy-start | bytes 3145732
  137.6 8.5 %copy-start.6 = (bf16[512,1024]{1,0:T(8,128)(2,1)S(1)}, bf16[512,1024]{1,0:T(8,128)(2,1)}, u32[]{:S(2)}) copy-start(bf16[512,1024]{1,0:T(8,128)(2,1)} %constant.19.clone.refs_12_) | copy-start | bytes 3145732
  141.4 2.1 copy-start.4
  159.0 97.8 %all-to-all-start.2 = ((f32[16,8,64,128]{3,2,1,0:T(8,128)}), f32[16,8,64,128]{3,2,1,0:T(8,128)}, u32[]{:S(2)}, u32[]{:S(2)}) async-start(f32[16,8,64,128]{3,2,1,0:T(8,128)} %finish.1), calls=%async_computation.2 | async-start | bytes 8388608 | tf_op jit(solution)/shard_map/all_to_all | solution.py:824

commit v6 on v5

--- a/solution.py
+++ b/solution.py
@@ -450,7 +450,29 @@
     return tiles
 
 
-def sweep(rows, cells, block, src, source, dst, weights, masks, turn=None):
+def run_rows(count, *bodies):
+    def both(pair, carry):
+        for body in bodies:
+            body(2 * pair + count % 2, None)
+        for body in bodies:
+            body(2 * pair + (1 + count % 2), None)
+        return carry
+
+    if count % 2:
+        for body in bodies:
+            body(0, None)
+    lax.fori_loop(0, count // 2, both, 0)
+
+
+def sweep(*args):
+    run_rows(*sweep_rows(*args))
+
+
+def first_sweep(*args):
+    run_rows(*first_sweep_rows(*args))
+
+
+def sweep_rows(rows, cells, block, src, source, dst, weights, masks, turn=None):
     (src_ref, src_t, src_z), (dst_ref, dst_t, dst_z) = src, dst
     keep = 1.0 - OMEGA if source else 2.0 - OMEGA
     c_ref, ahead_ref, behind_ref, w_t = weights
@@ -480,10 +502,10 @@
             )
         return carry
 
-    lax.fori_loop(0, rows[1] - low, one, 0)
-
-
-def first_sweep(rows, cells, block, source, dst, weights, masks):
+    return rows[1] - low, one
+
+
+def first_sweep_rows(rows, cells, block, source, dst, weights, masks):
     (g_ref, g_t, g_z), (dst_ref, dst_t, dst_z) = source, dst
     c_ref, w_t = weights[0], weights[3]
     low = rows[0]
@@ -497,7 +519,7 @@
             )
         return carry
 
-    lax.fori_loop(0, rows[1] - low, one, 0)
+    return rows[1] - low, one
 
 
 def side_masks(position, shape):
@@ -506,18 +528,26 @@
     return left, right
 
 
-def smooth_columns(local_rows, block, cells, g, u1, u2, s, weights, masks):
+def smooth_columns(local_rows, block, strips, weights, masks):
     first = -DEEP
-    low, high = cells
+    firsts, seconds, restricts = [], [], []
+    for cells, g, u1, u2, s in strips:
+        low, high = cells
+        g_at, u1_at, u2_at = (g, first, low), (u1, first, low), (u2, first + 1, low + 1)
+        total = g.shape[0]
+        u1[total] = jnp.zeros(u1.shape[1:], jnp.float32)
+        u2[total - 1] = jnp.zeros(u2.shape[1:], jnp.float32)
+        firsts.append(first_sweep_rows((first, local_rows), cells, block, g_at, u1_at, weights, masks))
+        rows, inside = (first + 1, local_rows), (low + 1, high - 1)
+        seconds.append(sweep_rows(rows, inside, block, u1_at, None, u2_at, weights, masks))
+        restricts.append(restrict_rows(cells, block, g, u2, s, weights))
+    for stage in (firsts, seconds, restricts):
+        run_rows(stage[0][0], *[body for _, body in stage])
+
+
+def restrict_rows(cells, block, g, u2, s, weights):
+    low = cells[0]
     c_ref, ahead_ref, behind_ref, _ = weights
-    g_at, u1_at, u2_at = (g, first, low), (u1, first, low), (u2, first + 1, low + 1)
-    total = g.shape[0]
-    u1[total] = jnp.zeros(u1.shape[1:], jnp.float32)
-    u2[total - 1] = jnp.zeros(u2.shape[1:], jnp.float32)
-    first_sweep((first, local_rows), cells, block, g_at, u1_at, weights, masks)
-    sweep(
-        (first + 1, local_rows), (low + 1, high - 1), block, u1_at, None, u2_at, weights, masks
-    )
     start = max(low + 2, 0)
     start += start % 2
 
@@ -535,7 +565,7 @@
         center_ahead = ahead_ref[row] - OMEGA / c_ref[row + 1] + 1.0
         behind, ahead = behind_ref[row], ahead_ref[row + 1]
         for at, count, _ in cell_tiles(start, start + 2 * s.shape[1], block):
-            z = at - u2_at[2]
+            z = at - (low + 1)
             here = u2[row - 1, z - 1 : z + count + 1]
             there = u2[row, z - 1 : z + count + 1]
             even, odd = paired(here + there)
@@ -551,7 +581,7 @@
             )
         return carry
 
-    lax.fori_loop(0, s.shape[0], restrict_row, 0)
+    return s.shape[0], restrict_row
 
 
 def inner_kernel(
@@ -568,7 +598,7 @@
     row_weights(upper, local_rows, -DEEP, DEEP + local_rows, squares, c_ref, ahead_ref, behind_ref)
     weights = (c_ref, ahead_ref, behind_ref, -DEEP)
     finished(loads)
-    smooth_columns(local_rows, block, (0, block), g, u1, u2, s, weights, None)
+    smooth_columns(local_rows, block, [((0, block), g, u1, u2, s)], weights, None)
     pairs = [(u2.at[DEEP - 3 : DEEP - 1 + local_rows], u_ref), (s, s_ref)]
     finished(started(pairs, out_sems))
 
@@ -577,7 +607,7 @@
     local_rows, block,
     deep_ref, near_ref, far_ref, left_ref, right_ref, inner_ref,
     u_left_ref, u_right_ref, head_ref, tail_ref,
-    g_left, g_right, u1, u2_left, u2_right, s_left, s_right, head, tail,
+    g_left, g_right, u1_left, u1_right, u2_left, u2_right, s_left, s_right, head, tail,
     c_ref, ahead_ref, behind_ref, in_sems, out_sems,
 ):
     wide = g_left.shape[1]
@@ -600,16 +630,16 @@
     weights = (c_ref, ahead_ref, behind_ref, -DEEP)
     finished(loads)
     rows = slice(DEEP - 3, DEEP - 1 + local_rows)
-    smooth_columns(local_rows, block, (-NEAR, own), g_left, u1, u2_left, s_left, weights, masks)
+    strips = [
+        ((-NEAR, own), g_left, u1_left, u2_left, s_left),
+        ((block - own, block + NEAR), g_right, u1_right, u2_right, s_right),
+    ]
+    smooth_columns(local_rows, block, strips, weights, masks)
     head[:, 0] = s_left[:, 0]
-    pairs = [(u2_left.at[rows, :NEAR], u_left_ref), (head, head_ref)]
-    stores = started(pairs, out_sems)
-    smooth_columns(
-        local_rows, block, (block - own, block + NEAR), g_right, u1, u2_right, s_right, weights, masks
-    )
     tail[:, FAR - 1] = s_right[:, 0]
-    pairs = [(u2_right.at[rows, wide - 2 - NEAR :], u_right_ref), (tail, tail_ref)]
-    finished(stores + started(pairs, out_sems, 2))
+    pairs = [(head, head_ref), (tail, tail_ref), (u2_left.at[rows, :NEAR], u_left_ref)]
+    pairs.append((u2_right.at[rows, wide - 2 - NEAR :], u_right_ref))
+    finished(started(pairs, out_sems))
 
 
 def field_pairs(g_refs, g):
@@ -867,6 +897,7 @@
             scratch(all_rows, wide),
             scratch(all_rows, wide),
             scratch(all_rows + 1, wide),
+            scratch(all_rows + 1, wide),
             scratch(all_rows, wide - 2),
             scratch(all_rows, wide - 2),
             scratch(coarse_rows, 1),

time: 261 us -> 259 us (level)
  no operation moved by 1% of the time
where the time goes in v6:
time: 259 us; the launch traced here: 258 us
  waiting for transfers between devices  178 us (69%)
  Pallas kernels  46.6 us (18%)
  starting transfers between devices  27.8 us (11%)
  local copies, waits for them, and re-layouts  4.36 us (2%)
    all_to_all x3, waiting for transfers between devices, exchange(): return lax.all_to_all(value, 'az', split_axis=0, concat_axis=0, tiled=True)  166 us
    all_to_all x3, starting transfers between devices, exchange(): return lax.all_to_all(value, 'az', split_axis=0, concat_axis=0, tiled=True)  16.5 us
    pallas_call x2, Pallas kernels, analyse(): pl.pallas_call(lambda *refs: analysis_kernel(groups, len(held), *refs), i...  13.2 us
    pallas_call x1, Pallas kernels, cell_body(): pl.pallas_call(lambda *refs: finish_kernel(local_rows, block, groups, *re...  12.3 us
    ppermute x1, waiting for transfers between devices, cell_body(): deep_sides = lax.ppermute(edge_sides, 'rad', [(0, 1), (1, 0)])  8.25 us
    pallas_call x2, Pallas kernels, pack(): pl.pallas_call(lambda *refs: pack_kernel(block, order, first_tile, *refs)...  6.05 us
    pallas_call x1, Pallas kernels, cell_body(): pl.pallas_call(lambda *refs: inner_kernel(local_rows, block, *refs), in_s...  5.24 us
  transfers between devices with their start and end apart: 9, of which 6 were waited for; matrix products, arithmetic and copies ran while one was open for 0% of the time, Pallas kernels for 10%

profile of v6, /device:TPU:11, one launch (start us, length us, event | category | flops | bytes accessed | tf_op | source)
XLA Modules:
  0.0 258.3 jit_solution(14559875690924019858)
XLA Ops:
  0.0 3.0 %pack.2 = f32[16,4,64,128]{3,2,1,0:T(8,128)} custom-call(f32[64,32,512]{2,1,0:T(8,128)} %refs_0_.3), custom_call_target="tpu_custom_call" | custom-call | tf_op jit(solution)/shard_map/pack/pallas_call | solution.py:810
  3.0 6.6 %all-to-all-start = ((f32[16,4,64,128]{3,2,1,0:T(8,128)}), f32[16,4,64,128]{3,2,1,0:T(8,128)S(1)}, u32[]{:S(2)}, u32[]{:S(2)}) async-start(f32[16,4,64,128]{3,2,1,0:T(8,128)} %pack.2), calls=%async_computation | async-start | bytes 4194304 | tf_op jit(solution)/shard_map/all_to_all | solution.py:854
  9.6 3.0 %pack.3 = f32[16,4,64,128]{3,2,1,0:T(8,128)} custom-call(f32[64,32,512]{2,1,0:T(8,128)} %refs_0_.3), custom_call_target="tpu_custom_call" | custom-call | tf_op jit(solution)/shard_map/pack/pallas_call | solution.py:810
  12.6 44.4 %all-to-all-done.refs_0_ = f32[16,4,64,128]{3,2,1,0:T(8,128)S(1)} async-done(((f32[16,4,64,128]{3,2,1,0:T(8,128)}), f32[16,4,64,128]{3,2,1,0:T(8,128)S(1)}, u32[]{:S(2)}, u32[]{:S(2)}) %all-to-all-start) | async-done | bytes 2097184 | tf_op jit(solution)/shard_map/all_to_all | solution.py:854
  57.0 0.0 copy-start.7
  57.0 4.9 %all-to-all-start.1 = ((f32[16,4,64,128]{3,2,1,0:T(8,128)}), f32[16,4,64,128]{3,2,1,0:T(8,128)}, u32[]{:S(2)}, u32[]{:S(2)}) async-start(f32[16,4,64,128]{3,2,1,0:T(8,128)} %pack.3), calls=%async_computation.1 | async-start | bytes 4194304 | tf_op jit(solution)/shard_map/all_to_all | solution.py:854
  61.9 0.0 copy-done.7
  61.9 6.8 %analysis.2 = (f32[16,32,8,128]{3,2,1,0:T(8,128)}, f32[14,6,8,128]{3,2,1,0:T(8,128)}, f32[14,32,8,128]{3,2,1,0:T(8,128)}) custom-call(f32[16,4,64,128]{3,2,1,0:T(8,128)} %copy-done.7, bf16[512,1024]{1,0:T(8,128)(2,1)} %constant.16.clone.refs_1_, bf16[512,1024]{1,0:T(8,128)(2,1)} %constant.17.clone.refs_2_), custom_call_target="tpu_custom_call" | custom-call | bytes 12582912 | tf_op jit(solution)/shard_map/analysis/pallas_call | solution.py:834
  68.7 1.3 collective-permute-start
  70.0 8.3 %collective-permute-done.refs_3_ = f32[14,6,8,128]{3,2,1,0:T(8,128)S(1)} collective-permute-done((f32[14,6,8,128]{3,2,1,0:T(8,128)}, f32[14,6,8,128]{3,2,1,0:T(8,128)S(1)}, u32[]{:S(2)}, u32[]{:S(2)}) %collective-permute-start) | collective-permute-done | bytes 344096 | tf_op jit(solution)/shard_map/ppermute | solution.py:865
  78.3 0.0 copy-start.8
  78.3 1.2 collective-permute-start.1
  79.5 30.1 %all-to-all-done.1.refs_0_ = f32[16,4,64,128]{3,2,1,0:T(8,128)} async-done(((f32[16,4,64,128]{3,2,1,0:T(8,128)}), f32[16,4,64,128]{3,2,1,0:T(8,128)}, u32[]{:S(2)}, u32[]{:S(2)}) %all-to-all-start.1) | async-done | bytes 2097184 | tf_op jit(solution)/shard_map/all_to_all | solution.py:854
  109.6 0.0 copy-done.8
  109.6 0.0 copy-start
  109.6 6.4 %analysis.3 = (f32[16,32,8,128]{3,2,1,0:T(8,128)}, f32[46,3,8,128]{3,2,1,0:T(8,128)}, f32[46,3,8,128]{3,2,1,0:T(8,128)}) custom-call(f32[16,4,64,128]{3,2,1,0:T(8,128)} %all-to-all-done.1.refs_0_, bf16[512,1024]{1,0:T(8,128)(2,1)} %constant.16.clone.refs_1_, bf16[512,1024]{1,0:T(8,128)(2,1)} %constant.17.clone.refs_2_, f32[14,6,8,128]{3,2,1,0:T(8,128)} %copy-done.8, ...), custom_call_target="tpu_custom_call" | custom-call | bytes 12582912 | tf_op jit(solution)/shard_map/analysis/pallas_call | solution.py:834
  116.0 1.9 collective-permute-start.2
  118.0 2.4 collective-permute-start.3
  120.4 0.0 collective-permute-done.1.refs_0_.refs_3_.refs_6_
  120.4 0.0 copy-start.3
  120.4 0.0 copy-done
  120.4 0.0 copy-start.1
  120.4 2.2 copy-done.1
  122.7 0.0 copy-start.2
  122.7 5.2 %inner.1 = (f32[34,30,8,128]{3,2,1,0:T(8,128)S(1)}, f32[22,14,8,128]{3,2,1,0:T(8,128)S(1)}) custom-call(f32[14,32,8,128]{3,2,1,0:T(8,128)S(1)} %collective-permute-done.1.refs_0_.refs_3_.refs_6_, f32[16,32,8,128]{3,2,1,0:T(8,128)S(1)} %copy-done, f32[16,32,8,128]{3,2,1,0:T(8,128)S(1)} %copy-done.1), custom_call_target="tpu_custom_call" | custom-call | bytes 33554432 | tf_op jit(solution)/shard_map/inner/pallas_call | solution.py:873
  127.9 0.0 collective-permute-done.2.refs_3_.refs_6_.refs_9_
  127.9 1.2 collective-permute-done.3.refs_4_.refs_7_.refs_10_
  129.1 0.0 copy-done.2
  129.1 2.7 %outer.1 = (f32[34,3,8,128]{3,2,1,0:T(8,128)S(1)}, f32[34,3,8,128]{3,2,1,0:T(8,128)S(1)}, f32[22,6,8,128]{3,2,1,0:T(8,128)S(1)}, f32[22,6,8,128]{3,2,1,0:T(8,128)S(1)}) custom-call(f32[14,32,8,128]{3,2,1,0:T(8,128)S(1)} %collective-permute-done.1.refs_0_.refs_3_.refs_6_, f32[16,32,8,128]{3,2,1,0:T(8,128)S(1)} %copy-done, f32[16,32,8,128]{3,2,1,0:T(8,128)S(1)} %copy-done.2, ...), custom_call_target="tpu_custom_call" | custom-call | bytes 12582912 | tf_op jit(solution)/shard_map/outer/pallas_call | solution.py:891
  131.9 2.0 collective-permute-start.4
  133.9 2.5 collective-permute-start.5
  136.4 0.0 copy-done.3
  136.4 0.0 copy-start.5
  136.4 0.0 copy-start.6
  136.4 3.6 %settle.1.refs_5_ = f32[33,34,8,128]{3,2,1,0:T(8,128)S(1)} custom-call(f32[34,30,8,128]{3,2,1,0:T(8,128)S(1)} %get-tuple-element.30.refs_0_, f32[34,3,8,128]{3,2,1,0:T(8,128)S(1)} %get-tuple-element.31.refs_1_, f32[34,3,8,128]{3,2,1,0:T(8,128)S(1)} %get-tuple-element.32.refs_2_, f32[14,32,8,128]{3,2,1,0:T(8,128)S(1)} %collective-permute-done.1.refs_0_.refs_3_.refs_6_, ...), custom_call_target="tpu_custom_call" | custom-call | bytes 16777216 | tf_op jit(solution)/shard_map/settle/pallas_call | solution.py:917
  140.0 0.0 copy-start.4
  140.0 2.1 copy-done.4
  142.1 0.0 collective-permute-done.4.refs_3_
  142.1 2.7 %collective-permute-done.5.refs_4_ = f32[22,6,8,128]{3,2,1,0:T(8,128)S(1)} collective-permute-done((f32[22,6,8,128]{3,2,1,0:T(8,128)S(1)}, f32[22,6,8,128]{3,2,1,0:T(8,128)S(1)}, u32[]{:S(2)}, u32[]{:S(2)}) %collective-permute-start.5) | collective-permute-done | bytes 540704 | tf_op jit(solution)/shard_map/ppermute | solution.py:860
  144.9 0.0 copy-done.5
  144.9 0.0 copy-done.6
  144.9 12.3 %finish.1 = f32[16,8,64,128]{3,2,1,0:T(8,128)} custom-call(f32[22,14,8,128]{3,2,1,0:T(8,128)S(1)} %get-tuple-element.25.refs_5_.refs_0_, f32[22,6,8,128]{3,2,1,0:T(8,128)S(1)} %get-tuple-element.28.refs_1_, f32[22,6,8,128]{3,2,1,0:T(8,128)S(1)} %get-tuple-element.29.refs_2_, f32[22,6,8,128]{3,2,1,0:T(8,128)S(1)} %collective-permute-done.4.refs_3_, ...), custom_call_target="tpu_custom_call" | custom-call | tf_op jit(solution)/shard_map/finish/pallas_call | solution.py:936
  157.1 5.0 %all-to-all-start.2 = ((f32[16,8,64,128]{3,2,1,0:T(8,128)}), f32[16,8,64,128]{3,2,1,0:T(8,128)}, u32[]{:S(2)}, u32[]{:S(2)}) async-start(f32[16,8,64,128]{3,2,1,0:T(8,128)} %finish.1), calls=%async_computation.2 | async-start | bytes 8388608 | tf_op jit(solution)/shard_map/all_to_all | solution.py:854
  162.1 0.6 pad_add_fusion.refs_1_
  162.8 91.8 %all-to-all-done.2.refs_0_ = f32[16,8,64,128]{3,2,1,0:T(8,128)} async-done(((f32[16,8,64,128]{3,2,1,0:T(8,128)}), f32[16,8,64,128]{3,2,1,0:T(8,128)}, u32[]{:S(2)}, u32[]{:S(2)}) %all-to-all-start.2) | async-done | bytes 4194336 | tf_op jit(solution)/shard_map/all_to_all | solution.py:854
  254.6 3.5 %unpack.1 = f32[64,32,512]{2,1,0:T(8,128)} custom-call(f32[16,8,64,128]{3,2,1,0:T(8,128)} %all-to-all-done.2.refs_0_, s32[2]{0:T(128)} %pad_add_fusion.refs_1_), custom_call_target="tpu_custom_call" | custom-call | tf_op jit(solution)/shard_map/unpack/pallas_call | solution.py:965
Async XLA Ops:
  3.0 54.0 %all-to-all-start = ((f32[16,4,64,128]{3,2,1,0:T(8,128)}), f32[16,4,64,128]{3,2,1,0:T(8,128)S(1)}, u32[]{:S(2)}, u32[]{:S(2)}) async-start(f32[16,4,64,128]{3,2,1,0:T(8,128)} %pack.2), calls=%async_computation | async-start | bytes 4194304 | tf_op jit(solution)/shard_map/all_to_all | solution.py:854
  57.0 4.9 %copy-start.7 = (f32[16,4,64,128]{3,2,1,0:T(8,128)}, f32[16,4,64,128]{3,2,1,0:T(8,128)S(1)}, u32[]{:S(2)}) copy-start(f32[16,4,64,128]{3,2,1,0:T(8,128)S(1)} %all-to-all-done.refs_0_) | copy-start | bytes 6291460
  57.0 52.6 %all-to-all-start.1 = ((f32[16,4,64,128]{3,2,1,0:T(8,128)}), f32[16,4,64,128]{3,2,1,0:T(8,128)}, u32[]{:S(2)}, u32[]{:S(2)}) async-start(f32[16,4,64,128]{3,2,1,0:T(8,128)} %pack.3), calls=%async_computation.1 | async-start | bytes 4194304 | tf_op jit(solution)/shard_map/all_to_all | solution.py:854
  68.7 9.6 %collective-permute-start = (f32[14,6,8,128]{3,2,1,0:T(8,128)}, f32[14,6,8,128]{3,2,1,0:T(8,128)S(1)}, u32[]{:S(2)}, u32[]{:S(2)}) collective-permute-start(f32[14,6,8,128]{3,2,1,0:T(8,128)} %get-tuple-element.19), channel_id=1, source_target_pairs={{0,1},{1,0},{2,3},{3,2},{4,5},{5,4},{6,7},{7,6},{8,9},{9,8},{10,11... | collective-permute-start | bytes 1032200 | tf_op jit(solution)/shard_map/ppermute | solution.py:865
  78.3 31.4 %copy-start.8 = (f32[14,6,8,128]{3,2,1,0:T(8,128)}, f32[14,6,8,128]{3,2,1,0:T(8,128)S(1)}, u32[]{:S(2)}) copy-start(f32[14,6,8,128]{3,2,1,0:T(8,128)S(1)} %collective-permute-done.refs_3_) | copy-start | bytes 1032196
  78.3 42.1 %collective-permute-start.1 = (f32[14,32,8,128]{3,2,1,0:T(8,128)}, f32[14,32,8,128]{3,2,1,0:T(8,128)S(1)}, u32[]{:S(2)}, u32[]{:S(2)}) collective-permute-start(f32[14,32,8,128]{3,2,1,0:T(8,128)} %get-tuple-element.21), channel_id=1, source_target_pairs={{0,1},{1,0},{2,3},{3,2},{4,5},{5,4},{6,7},{7,6},{8,9},{9,8},{10,11... | collective-permute-start | bytes 5505032 | tf_op jit(solution)/shard_map/ppermute | solution.py:867
  109.6 10.8 %copy-start = (f32[16,32,8,128]{3,2,1,0:T(8,128)S(1)}, f32[16,32,8,128]{3,2,1,0:T(8,128)}, u32[]{:S(2)}) copy-start(f32[16,32,8,128]{3,2,1,0:T(8,128)} %get-tuple-element.22.refs_4_.refs_1_.refs_7_) | copy-start | bytes 6291460
  116.0 11.9 %collective-permute-start.2 = (f32[46,3,8,128]{3,2,1,0:T(8,128)}, f32[46,3,8,128]{3,2,1,0:T(8,128)S(1)}, u32[]{:S(2)}, u32[]{:S(2)}) collective-permute-start(f32[46,3,8,128]{3,2,1,0:T(8,128)} %get-tuple-element.26), channel_id=1, source_target_pairs={{0,2},{2,4},{4,6},{6,12},{12,14},{14,8},{8,10},{10,16},{16,18},{18... | collective-permute-start | bytes 1695752 | tf_op jit(solution)/shard_map/ppermute | solution.py:860
  118.0 11.1 %collective-permute-start.3 = (f32[46,3,8,128]{3,2,1,0:T(8,128)}, f32[46,3,8,128]{3,2,1,0:T(8,128)S(1)}, u32[]{:S(2)}, u32[]{:S(2)}) collective-permute-start(f32[46,3,8,128]{3,2,1,0:T(8,128)} %get-tuple-element.27), channel_id=1, source_target_pairs={{2,0},{4,2},{6,4},{12,6},{14,12},{8,14},{10,8},{16,10},{18,16},{20... | collective-permute-start | bytes 1695752 | tf_op jit(solution)/shard_map/ppermute | solution.py:860
  120.4 16.0 %copy-start.3 = (f32[14,32,8,128]{3,2,1,0:T(8,128)}, f32[14,32,8,128]{3,2,1,0:T(8,128)S(1)}, u32[]{:S(2)}) copy-start(f32[14,32,8,128]{3,2,1,0:T(8,128)S(1)} %collective-permute-done.1.refs_0_.refs_3_.refs_6_) | copy-start | bytes 5505028
  120.4 2.3 copy-start.1
  122.7 6.5 %copy-start.2 = (f32[16,32,8,128]{3,2,1,0:T(8,128)S(1)}, f32[16,32,8,128]{3,2,1,0:T(8,128)}, u32[]{:S(2)}) copy-start(f32[16,32,8,128]{3,2,1,0:T(8,128)} %get-tuple-element.24.refs_2_.refs_5_.refs_8_) | copy-start | bytes 6291460
  131.9 10.3 %collective-permute-start.4 = (f32[22,6,8,128]{3,2,1,0:T(8,128)S(1)}, f32[22,6,8,128]{3,2,1,0:T(8,128)S(1)}, u32[]{:S(2)}, u32[]{:S(2)}) collective-permute-start(f32[22,6,8,128]{3,2,1,0:T(8,128)S(1)} %get-tuple-element.29.refs_2_), channel_id=1, source_target_pairs={{0,2},{2,4},{4,6},{6,12},{12,14},{14,8},{8,10},{10,16},{16,18},{18... | collective-permute-start | bytes 1622024 | tf_op jit(solution)/shard_map/ppermute | solution.py:860
  133.9 11.0 %collective-permute-start.5 = (f32[22,6,8,128]{3,2,1,0:T(8,128)S(1)}, f32[22,6,8,128]{3,2,1,0:T(8,128)S(1)}, u32[]{:S(2)}, u32[]{:S(2)}) collective-permute-start(f32[22,6,8,128]{3,2,1,0:T(8,128)S(1)} %get-tuple-element.28.refs_1_), channel_id=1, source_target_pairs={{2,0},{4,2},{6,4},{12,6},{14,12},{8,14},{10,8},{16,10},{18,16},{20... | collective-permute-start | bytes 1622024 | tf_op jit(solution)/shard_map/ppermute | solution.py:860
  136.4 8.5 %copy-start.5 = (bf16[512,1024]{1,0:T(8,128)(2,1)S(1)}, bf16[512,1024]{1,0:T(8,128)(2,1)}, u32[]{:S(2)}) copy-start(bf16[512,1024]{1,0:T(8,128)(2,1)} %constant.18.clone.refs_11_) | copy-start | bytes 3145732
  136.4 8.5 %copy-start.6 = (bf16[512,1024]{1,0:T(8,128)(2,1)S(1)}, bf16[512,1024]{1,0:T(8,128)(2,1)}, u32[]{:S(2)}) copy-start(bf16[512,1024]{1,0:T(8,128)(2,1)} %constant.19.clone.refs_12_) | copy-start | bytes 3145732
  140.0 2.1 copy-start.4
  157.1 97.5 %all-to-all-start.2 = ((f32[16,8,64,128]{3,2,1,0:T(8,128)}), f32[16,8,64,128]{3,2,1,0:T(8,128)}, u32[]{:S(2)}, u32[]{:S(2)}) async-start(f32[16,8,64,128]{3,2,1,0:T(8,128)} %finish.1), calls=%async_computation.2 | async-start | bytes 8388608 | tf_op jit(solution)/shard_map/all_to_all | solution.py:854

commit v7 on v6

--- a/solution.py
+++ b/solution.py
@@ -450,18 +450,19 @@
     return tiles
 
 
-def run_rows(count, *bodies):
-    def both(pair, carry):
+def run_rows(count, *bodies, together=4):
+    rest = count % together
+
+    def several(index, carry):
+        for row in range(together):
+            for body in bodies:
+                body(together * index + (rest + row), None)
+        return carry
+
+    for row in range(rest):
         for body in bodies:
-            body(2 * pair + count % 2, None)
-        for body in bodies:
-            body(2 * pair + (1 + count % 2), None)
-        return carry
-
-    if count % 2:
-        for body in bodies:
-            body(0, None)
-    lax.fori_loop(0, count // 2, both, 0)
+            body(row, None)
+    lax.fori_loop(0, count // together, several, 0)
 
 
 def sweep(*args):

time: 259 us -> 258 us (level)
  no operation moved by 1% of the time
where the time goes in v7:
time: 258 us
  waiting for transfers between devices  179 us (69%)
  Pallas kernels  46 us (18%)
  starting transfers between devices  27.7 us (11%)
  local copies, waits for them, and re-layouts  4.36 us (2%)
    all_to_all x3, waiting for transfers between devices, exchange(): return lax.all_to_all(value, 'az', split_axis=0, concat_axis=0, tiled=True)  166 us
    all_to_all x3, starting transfers between devices, exchange(): return lax.all_to_all(value, 'az', split_axis=0, concat_axis=0, tiled=True)  16.3 us
    pallas_call x2, Pallas kernels, analyse(): pl.pallas_call(lambda *refs: analysis_kernel(groups, len(held), *refs), i...  13.2 us
    pallas_call x1, Pallas kernels, cell_body(): pl.pallas_call(lambda *refs: finish_kernel(local_rows, block, groups, *re...  12 us
    ppermute x1, waiting for transfers between devices, cell_body(): deep_sides = lax.ppermute(edge_sides, 'rad', [(0, 1), (1, 0)])  8.25 us
    pallas_call x2, Pallas kernels, pack(): pl.pallas_call(lambda *refs: pack_kernel(block, order, first_tile, *refs)...  6.05 us
  transfers between devices with their start and end apart: 9, of which 6 were waited for; matrix products, arithmetic and copies ran while one was open for 0% of the time, Pallas kernels for 10%

profile of v7, /device:TPU:11, one launch (start us, length us, event | category | flops | bytes accessed | tf_op | source)
XLA Modules:
  0.0 257.7 jit_solution(7828218198737065119)
XLA Ops:
  0.0 3.0 %pack.2 = f32[16,4,64,128]{3,2,1,0:T(8,128)} custom-call(f32[64,32,512]{2,1,0:T(8,128)} %refs_0_.3), custom_call_target="tpu_custom_call" | custom-call | tf_op jit(solution)/shard_map/pack/pallas_call | solution.py:811
  3.0 6.6 %all-to-all-start = ((f32[16,4,64,128]{3,2,1,0:T(8,128)}), f32[16,4,64,128]{3,2,1,0:T(8,128)S(1)}, u32[]{:S(2)}, u32[]{:S(2)}) async-start(f32[16,4,64,128]{3,2,1,0:T(8,128)} %pack.2), calls=%async_computation | async-start | bytes 4194304 | tf_op jit(solution)/shard_map/all_to_all | solution.py:855
  9.6 3.0 %pack.3 = f32[16,4,64,128]{3,2,1,0:T(8,128)} custom-call(f32[64,32,512]{2,1,0:T(8,128)} %refs_0_.3), custom_call_target="tpu_custom_call" | custom-call | tf_op jit(solution)/shard_map/pack/pallas_call | solution.py:811
  12.6 44.4 %all-to-all-done.refs_0_ = f32[16,4,64,128]{3,2,1,0:T(8,128)S(1)} async-done(((f32[16,4,64,128]{3,2,1,0:T(8,128)}), f32[16,4,64,128]{3,2,1,0:T(8,128)S(1)}, u32[]{:S(2)}, u32[]{:S(2)}) %all-to-all-start) | async-done | bytes 2097184 | tf_op jit(solution)/shard_map/all_to_all | solution.py:855
  57.0 0.0 copy-start.7
  57.0 4.9 %all-to-all-start.1 = ((f32[16,4,64,128]{3,2,1,0:T(8,128)}), f32[16,4,64,128]{3,2,1,0:T(8,128)}, u32[]{:S(2)}, u32[]{:S(2)}) async-start(f32[16,4,64,128]{3,2,1,0:T(8,128)} %pack.3), calls=%async_computation.1 | async-start | bytes 4194304 | tf_op jit(solution)/shard_map/all_to_all | solution.py:855
  61.9 0.0 copy-done.7
  61.9 6.8 %analysis.2 = (f32[16,32,8,128]{3,2,1,0:T(8,128)}, f32[14,6,8,128]{3,2,1,0:T(8,128)}, f32[14,32,8,128]{3,2,1,0:T(8,128)}) custom-call(f32[16,4,64,128]{3,2,1,0:T(8,128)} %copy-done.7, bf16[512,1024]{1,0:T(8,128)(2,1)} %constant.16.clone.refs_1_, bf16[512,1024]{1,0:T(8,128)(2,1)} %constant.17.clone.refs_2_), custom_call_target="tpu_custom_call" | custom-call | bytes 12582912 | tf_op jit(solution)/shard_map/analysis/pallas_call | solution.py:835
  68.7 1.3 collective-permute-start
  70.0 8.3 %collective-permute-done.refs_3_ = f32[14,6,8,128]{3,2,1,0:T(8,128)S(1)} collective-permute-done((f32[14,6,8,128]{3,2,1,0:T(8,128)}, f32[14,6,8,128]{3,2,1,0:T(8,128)S(1)}, u32[]{:S(2)}, u32[]{:S(2)}) %collective-permute-start) | collective-permute-done | bytes 344096 | tf_op jit(solution)/shard_map/ppermute | solution.py:866
  78.3 0.0 copy-start.8
  78.3 1.2 collective-permute-start.1
  79.5 30.1 %all-to-all-done.1.refs_0_ = f32[16,4,64,128]{3,2,1,0:T(8,128)} async-done(((f32[16,4,64,128]{3,2,1,0:T(8,128)}), f32[16,4,64,128]{3,2,1,0:T(8,128)}, u32[]{:S(2)}, u32[]{:S(2)}) %all-to-all-start.1) | async-done | bytes 2097184 | tf_op jit(solution)/shard_map/all_to_all | solution.py:855
  109.6 0.0 copy-done.8
  109.6 0.0 copy-start
  109.6 6.4 %analysis.3 = (f32[16,32,8,128]{3,2,1,0:T(8,128)}, f32[46,3,8,128]{3,2,1,0:T(8,128)}, f32[46,3,8,128]{3,2,1,0:T(8,128)}) custom-call(f32[16,4,64,128]{3,2,1,0:T(8,128)} %all-to-all-done.1.refs_0_, bf16[512,1024]{1,0:T(8,128)(2,1)} %constant.16.clone.refs_1_, bf16[512,1024]{1,0:T(8,128)(2,1)} %constant.17.clone.refs_2_, f32[14,6,8,128]{3,2,1,0:T(8,128)} %copy-done.8, ...), custom_call_target="tpu_custom_call" | custom-call | bytes 12582912 | tf_op jit(solution)/shard_map/analysis/pallas_call | solution.py:835
  116.0 1.9 collective-permute-start.2
  118.0 2.4 collective-permute-start.3
  120.4 0.0 collective-permute-done.1.refs_0_.refs_3_.refs_6_
  120.4 0.0 copy-start.3
  120.4 0.0 copy-done
  120.4 0.0 copy-start.1
  120.4 2.2 copy-done.1
  122.7 0.0 copy-start.2
  122.7 5.1 %inner.1 = (f32[34,30,8,128]{3,2,1,0:T(8,128)S(1)}, f32[22,14,8,128]{3,2,1,0:T(8,128)S(1)}) custom-call(f32[14,32,8,128]{3,2,1,0:T(8,128)S(1)} %collective-permute-done.1.refs_0_.refs_3_.refs_6_, f32[16,32,8,128]{3,2,1,0:T(8,128)S(1)} %copy-done, f32[16,32,8,128]{3,2,1,0:T(8,128)S(1)} %copy-done.1), custom_call_target="tpu_custom_call" | custom-call | bytes 33554432 | tf_op jit(solution)/shard_map/inner/pallas_call | solution.py:874
  127.8 0.0 collective-permute-done.2.refs_3_.refs_6_.refs_9_
  127.8 1.3 collective-permute-done.3.refs_4_.refs_7_.refs_10_
  129.1 0.0 copy-done.2
  129.1 2.6 outer.1
  131.7 1.9 collective-permute-start.4
  133.6 2.6 %collective-permute-start.5 = (f32[22,6,8,128]{3,2,1,0:T(8,128)S(1)}, f32[22,6,8,128]{3,2,1,0:T(8,128)S(1)}, u32[]{:S(2)}, u32[]{:S(2)}) collective-permute-start(f32[22,6,8,128]{3,2,1,0:T(8,128)S(1)} %get-tuple-element.28.refs_1_), channel_id=1, source_target_pairs={{2,0},{4,2},{6,4},{12,6},{14,12},{8,14},{10,8},{16,10},{18,16},{20... | collective-permute-start | bytes 1622024 | tf_op jit(solution)/shard_map/ppermute | solution.py:861
  136.2 0.0 copy-done.3
  136.2 0.0 copy-start.5
  136.2 0.0 copy-start.6
  136.3 3.6 %settle.1.refs_5_ = f32[33,34,8,128]{3,2,1,0:T(8,128)S(1)} custom-call(f32[34,30,8,128]{3,2,1,0:T(8,128)S(1)} %get-tuple-element.30.refs_0_, f32[34,3,8,128]{3,2,1,0:T(8,128)S(1)} %get-tuple-element.31.refs_1_, f32[34,3,8,128]{3,2,1,0:T(8,128)S(1)} %get-tuple-element.32.refs_2_, f32[14,32,8,128]{3,2,1,0:T(8,128)S(1)} %collective-permute-done.1.refs_0_.refs_3_.refs_6_, ...), custom_call_target="tpu_custom_call" | custom-call | bytes 16777216 | tf_op jit(solution)/shard_map/settle/pallas_call | solution.py:918
  139.8 0.0 copy-start.4
  139.8 2.1 copy-done.4
  141.9 0.0 collective-permute-done.4.refs_3_
  141.9 2.8 %collective-permute-done.5.refs_4_ = f32[22,6,8,128]{3,2,1,0:T(8,128)S(1)} collective-permute-done((f32[22,6,8,128]{3,2,1,0:T(8,128)S(1)}, f32[22,6,8,128]{3,2,1,0:T(8,128)S(1)}, u32[]{:S(2)}, u32[]{:S(2)}) %collective-permute-start.5) | collective-permute-done | bytes 540704 | tf_op jit(solution)/shard_map/ppermute | solution.py:861
  144.7 0.0 copy-done.5
  144.7 0.0 copy-done.6
  144.7 12.0 %finish.1 = f32[16,8,64,128]{3,2,1,0:T(8,128)} custom-call(f32[22,14,8,128]{3,2,1,0:T(8,128)S(1)} %get-tuple-element.25.refs_5_.refs_0_, f32[22,6,8,128]{3,2,1,0:T(8,128)S(1)} %get-tuple-element.28.refs_1_, f32[22,6,8,128]{3,2,1,0:T(8,128)S(1)} %get-tuple-element.29.refs_2_, f32[22,6,8,128]{3,2,1,0:T(8,128)S(1)} %collective-permute-done.4.refs_3_, ...), custom_call_target="tpu_custom_call" | custom-call | tf_op jit(solution)/shard_map/finish/pallas_call | solution.py:937
  156.8 4.8 %all-to-all-start.2 = ((f32[16,8,64,128]{3,2,1,0:T(8,128)}), f32[16,8,64,128]{3,2,1,0:T(8,128)}, u32[]{:S(2)}, u32[]{:S(2)}) async-start(f32[16,8,64,128]{3,2,1,0:T(8,128)} %finish.1), calls=%async_computation.2 | async-start | bytes 8388608 | tf_op jit(solution)/shard_map/all_to_all | solution.py:855
  161.6 0.6 pad_add_fusion.refs_1_
  162.2 91.8 %all-to-all-done.2.refs_0_ = f32[16,8,64,128]{3,2,1,0:T(8,128)} async-done(((f32[16,8,64,128]{3,2,1,0:T(8,128)}), f32[16,8,64,128]{3,2,1,0:T(8,128)}, u32[]{:S(2)}, u32[]{:S(2)}) %all-to-all-start.2) | async-done | bytes 4194336 | tf_op jit(solution)/shard_map/all_to_all | solution.py:855
  254.1 3.5 %unpack.1 = f32[64,32,512]{2,1,0:T(8,128)} custom-call(f32[16,8,64,128]{3,2,1,0:T(8,128)} %all-to-all-done.2.refs_0_, s32[2]{0:T(128)} %pad_add_fusion.refs_1_), custom_call_target="tpu_custom_call" | custom-call | tf_op jit(solution)/shard_map/unpack/pallas_call | solution.py:966
Async XLA Ops:
  3.0 54.0 %all-to-all-start = ((f32[16,4,64,128]{3,2,1,0:T(8,128)}), f32[16,4,64,128]{3,2,1,0:T(8,128)S(1)}, u32[]{:S(2)}, u32[]{:S(2)}) async-start(f32[16,4,64,128]{3,2,1,0:T(8,128)} %pack.2), calls=%async_computation | async-start | bytes 4194304 | tf_op jit(solution)/shard_map/all_to_all | solution.py:855
  57.0 4.9 %copy-start.7 = (f32[16,4,64,128]{3,2,1,0:T(8,128)}, f32[16,4,64,128]{3,2,1,0:T(8,128)S(1)}, u32[]{:S(2)}) copy-start(f32[16,4,64,128]{3,2,1,0:T(8,128)S(1)} %all-to-all-done.refs_0_) | copy-start | bytes 6291460
  57.0 52.6 %all-to-all-start.1 = ((f32[16,4,64,128]{3,2,1,0:T(8,128)}), f32[16,4,64,128]{3,2,1,0:T(8,128)}, u32[]{:S(2)}, u32[]{:S(2)}) async-start(f32[16,4,64,128]{3,2,1,0:T(8,128)} %pack.3), calls=%async_computation.1 | async-start | bytes 4194304 | tf_op jit(solution)/shard_map/all_to_all | solution.py:855
  68.7 9.6 %collective-permute-start = (f32[14,6,8,128]{3,2,1,0:T(8,128)}, f32[14,6,8,128]{3,2,1,0:T(8,128)S(1)}, u32[]{:S(2)}, u32[]{:S(2)}) collective-permute-start(f32[14,6,8,128]{3,2,1,0:T(8,128)} %get-tuple-element.19), channel_id=1, source_target_pairs={{0,1},{1,0},{2,3},{3,2},{4,5},{5,4},{6,7},{7,6},{8,9},{9,8},{10,11... | collective-permute-start | bytes 1032200 | tf_op jit(solution)/shard_map/ppermute | solution.py:866
  78.3 31.4 %copy-start.8 = (f32[14,6,8,128]{3,2,1,0:T(8,128)}, f32[14,6,8,128]{3,2,1,0:T(8,128)S(1)}, u32[]{:S(2)}) copy-start(f32[14,6,8,128]{3,2,1,0:T(8,128)S(1)} %collective-permute-done.refs_3_) | copy-start | bytes 1032196
  78.3 42.1 %collective-permute-start.1 = (f32[14,32,8,128]{3,2,1,0:T(8,128)}, f32[14,32,8,128]{3,2,1,0:T(8,128)S(1)}, u32[]{:S(2)}, u32[]{:S(2)}) collective-permute-start(f32[14,32,8,128]{3,2,1,0:T(8,128)} %get-tuple-element.21), channel_id=1, source_target_pairs={{0,1},{1,0},{2,3},{3,2},{4,5},{5,4},{6,7},{7,6},{8,9},{9,8},{10,11... | collective-permute-start | bytes 5505032 | tf_op jit(solution)/shard_map/ppermute | solution.py:868
  109.6 10.8 %copy-start = (f32[16,32,8,128]{3,2,1,0:T(8,128)S(1)}, f32[16,32,8,128]{3,2,1,0:T(8,128)}, u32[]{:S(2)}) copy-start(f32[16,32,8,128]{3,2,1,0:T(8,128)} %get-tuple-element.22.refs_4_.refs_1_.refs_7_) | copy-start | bytes 6291460
  116.0 11.7 %collective-permute-start.2 = (f32[46,3,8,128]{3,2,1,0:T(8,128)}, f32[46,3,8,128]{3,2,1,0:T(8,128)S(1)}, u32[]{:S(2)}, u32[]{:S(2)}) collective-permute-start(f32[46,3,8,128]{3,2,1,0:T(8,128)} %get-tuple-element.26), channel_id=1, source_target_pairs={{0,2},{2,4},{4,6},{6,12},{12,14},{14,8},{8,10},{10,16},{16,18},{18... | collective-permute-start | bytes 1695752 | tf_op jit(solution)/shard_map/ppermute | solution.py:861
  118.0 11.1 %collective-permute-start.3 = (f32[46,3,8,128]{3,2,1,0:T(8,128)}, f32[46,3,8,128]{3,2,1,0:T(8,128)S(1)}, u32[]{:S(2)}, u32[]{:S(2)}) collective-permute-start(f32[46,3,8,128]{3,2,1,0:T(8,128)} %get-tuple-element.27), channel_id=1, source_target_pairs={{2,0},{4,2},{6,4},{12,6},{14,12},{8,14},{10,8},{16,10},{18,16},{20... | collective-permute-start | bytes 1695752 | tf_op jit(solution)/shard_map/ppermute | solution.py:861
  120.4 15.8 %copy-start.3 = (f32[14,32,8,128]{3,2,1,0:T(8,128)}, f32[14,32,8,128]{3,2,1,0:T(8,128)S(1)}, u32[]{:S(2)}) copy-start(f32[14,32,8,128]{3,2,1,0:T(8,128)S(1)} %collective-permute-done.1.refs_0_.refs_3_.refs_6_) | copy-start | bytes 5505028
  120.4 2.3 copy-start.1
  122.7 6.5 %copy-start.2 = (f32[16,32,8,128]{3,2,1,0:T(8,128)S(1)}, f32[16,32,8,128]{3,2,1,0:T(8,128)}, u32[]{:S(2)}) copy-start(f32[16,32,8,128]{3,2,1,0:T(8,128)} %get-tuple-element.24.refs_2_.refs_5_.refs_8_) | copy-start | bytes 6291460
  131.7 10.2 %collective-permute-start.4 = (f32[22,6,8,128]{3,2,1,0:T(8,128)S(1)}, f32[22,6,8,128]{3,2,1,0:T(8,128)S(1)}, u32[]{:S(2)}, u32[]{:S(2)}) collective-permute-start(f32[22,6,8,128]{3,2,1,0:T(8,128)S(1)} %get-tuple-element.29.refs_2_), channel_id=1, source_target_pairs={{0,2},{2,4},{4,6},{6,12},{12,14},{14,8},{8,10},{10,16},{16,18},{18... | collective-permute-start | bytes 1622024 | tf_op jit(solution)/shard_map/ppermute | solution.py:861
  133.6 11.1 %collective-permute-start.5 = (f32[22,6,8,128]{3,2,1,0:T(8,128)S(1)}, f32[22,6,8,128]{3,2,1,0:T(8,128)S(1)}, u32[]{:S(2)}, u32[]{:S(2)}) collective-permute-start(f32[22,6,8,128]{3,2,1,0:T(8,128)S(1)} %get-tuple-element.28.refs_1_), channel_id=1, source_target_pairs={{2,0},{4,2},{6,4},{12,6},{14,12},{8,14},{10,8},{16,10},{18,16},{20... | collective-permute-start | bytes 1622024 | tf_op jit(solution)/shard_map/ppermute | solution.py:861
  136.2 8.5 %copy-start.5 = (bf16[512,1024]{1,0:T(8,128)(2,1)S(1)}, bf16[512,1024]{1,0:T(8,128)(2,1)}, u32[]{:S(2)}) copy-start(bf16[512,1024]{1,0:T(8,128)(2,1)} %constant.18.clone.refs_11_) | copy-start | bytes 3145732
  136.2 8.5 %copy-start.6 = (bf16[512,1024]{1,0:T(8,128)(2,1)S(1)}, bf16[512,1024]{1,0:T(8,128)(2,1)}, u32[]{:S(2)}) copy-start(bf16[512,1024]{1,0:T(8,128)(2,1)} %constant.19.clone.refs_12_) | copy-start | bytes 3145732
  139.8 2.1 copy-start.4
  156.8 97.3 %all-to-all-start.2 = ((f32[16,8,64,128]{3,2,1,0:T(8,128)}), f32[16,8,64,128]{3,2,1,0:T(8,128)}, u32[]{:S(2)}, u32[]{:S(2)}) async-start(f32[16,8,64,128]{3,2,1,0:T(8,128)} %finish.1), calls=%async_computation.2 | async-start | bytes 8388608 | tf_op jit(solution)/shard_map/all_to_all | solution.py:855
